TPU v7x, 32 devices: a whole 2x2x4 slice. The times are simulated.
32 devices in a mesh: ctxa: 4 (over y, x), ctxb: 8 (over z, core).
Axes of the slice: x: 2, y: 2, z: 4, core: 2. Of those that a mesh axis runs over, the one named last changes fastest.
Arguments:
- queries: bfloat16 [8192, 384], P(('ctxa', 'ctxb')), may hold values from -6 to 6
- key_matrix: bfloat16 [8192, 384], P(('ctxa', 'ctxb')), may hold values from -6 to 6
- value_matrix: bfloat16 [8192, 384], P(('ctxa', 'ctxb')), may hold values from -6 to 6
- grad_out: bfloat16 [8192, 384], P(('ctxa', 'ctxb')), may hold values from -6 to 6
- offsets: int32 [6], replicated, may hold values from 0 to 127
Outputs:
- grad_queries: bfloat16 [8192, 384], P(('ctxa', 'ctxb'))
- grad_keys: bfloat16 [8192, 384], P(('ctxa', 'ctxb'))
- grad_values: bfloat16 [8192, 384], P(('ctxa', 'ctxb'))
All inputs are finite; a program needn't handle non-finite values.
Results may differ from a plain program's by a relative error of at most 0.0086.
Values may be sent and summed in bfloat16 or wider, within the bound.
No kernel may reach another device: no remote copies, remote signals or barrier semaphores. Data moves between devices by JAX's collectives and lax.ppermute only.
A program may use at most 128 MiB of HBM per device.

v0:
```python
from functools import partial

import jax
import jax.numpy as jnp
from jax import lax
from jax.sharding import PartitionSpec as P

HD = 64
GROUP_BITS = 2
MIDDLE_DILATION = 8
UPPER_DILATION = 128


FILL_LOW = -1e30


def partner(value, axis, bit):
    mask = 2**bit
    pairs = [(source, source ^ mask) for source in range(lax.axis_size(axis))]
    return lax.ppermute(value, axis, pairs)


def selection_mask(offsets, spacing_factor):
    return (
        jnp.arange(spacing_factor, dtype=jnp.int32)[None, :] == (offsets % spacing_factor)[:, None]
    )


def select_rows(source, level_mask):
    head_count, spacing_factor = level_mask.shape
    pieces = source.reshape(
        source.shape[0] // spacing_factor, spacing_factor, head_count, source.shape[1] // head_count
    )
    kept = jnp.where(level_mask.T[None, :, :, None], pieces, jnp.zeros((), source.dtype))
    return jnp.transpose(jnp.sum(kept, axis=1), (1, 0, 2))


def place_rows(rows, level_mask):
    head_count, spacing_factor = level_mask.shape
    spread = jnp.where(
        level_mask.T[None, :, :, None], jnp.transpose(rows, (1, 0, 2))[:, None, :, :], 0.0
    )
    return spread.reshape(rows.shape[1] * spacing_factor, head_count * rows.shape[2])


def spread_scalar(values, level_mask, filler):
    return jnp.where(level_mask[:, None, :], values[:, :, None], filler).reshape(
        values.shape[0], -1
    )


def collect_scalar(values, level_mask):
    head_count, spacing_factor = level_mask.shape
    shaped = values.reshape(head_count, -1, spacing_factor)
    return jnp.sum(jnp.where(level_mask[:, None, :], shaped, 0.0), axis=2)


def level_forward(query_matrix, key_matrix, value_matrix):
    logit_scale = HD ** (-0.5)
    attention_logits = (
        jnp.einsum("sle,sie->sli", query_matrix, key_matrix, preferred_element_type=jnp.float32)
        * logit_scale
    )
    row_max = jnp.max(attention_logits, axis=-1)
    weight_tensors = jnp.exp(attention_logits - row_max[..., None])
    row_sum = jnp.sum(weight_tensors, axis=-1)
    row_accumulator = jnp.einsum(
        "fco,fox->fcx",
        weight_tensors.astype(jnp.bfloat16),
        value_matrix,
        preferred_element_type=jnp.float32,
    )
    return (row_max, row_sum, row_accumulator)


def level_backward(query_matrix, key_matrix, value_matrix, gradient_rows, log_sum, row_dot, wanted):
    logit_scale = HD ** (-0.5)
    attention_logits = (
        jnp.einsum("sle,sie->sli", query_matrix, key_matrix, preferred_element_type=jnp.float32)
        * logit_scale
    )
    probs = jnp.exp(attention_logits - log_sum[..., None])
    probability_gradient = jnp.einsum(
        "sle,sie->sli", gradient_rows, value_matrix, preferred_element_type=jnp.float32
    )
    score_gradient = (probs * (probability_gradient - row_dot[..., None]) * logit_scale).astype(
        jnp.bfloat16
    )
    results = ()
    if wanted != "keys":
        results = results + (
            jnp.einsum(
                "fco,fox->fcx", score_gradient, key_matrix, preferred_element_type=jnp.float32
            ),
        )
    if wanted != "queries":
        key_gradient = jnp.einsum(
            "axm,axh->amh", score_gradient, query_matrix, preferred_element_type=jnp.float32
        )
        value_gradient = jnp.einsum(
            "axm,axh->amh",
            probs.astype(jnp.bfloat16),
            gradient_rows,
            preferred_element_type=jnp.float32,
        )
        results = results + (key_gradient, value_gradient)
    return results


def by_heads(kernel, arrays):
    stacked = tuple((member[:, None] for member in arrays))
    results = lax.map(lambda grouped: kernel(*grouped), stacked)
    return tuple((member[:, 0] for member in results))


def join_halves(mine_part, their_part, low_side, axis_pos):
    return jnp.where(
        low_side,
        jnp.concatenate((mine_part, their_part), axis=axis_pos),
        jnp.concatenate((their_part, mine_part), axis=axis_pos),
    )


def near_key_gather(stacked):
    position = lax.axis_index("ctxb")
    for bit_pos in range(GROUP_BITS):
        low_side = position >> bit_pos & 1 == 0
        stacked = join_halves(stacked, partner(stacked, "ctxb", bit_pos), low_side, 1)
    return stacked


def near_reduce(stacked):
    position = lax.axis_index("ctxb")
    for bit_pos in reversed(range(GROUP_BITS)):
        half_rows = stacked.shape[1] // 2
        upper_side = position >> bit_pos & 1 == 1
        lower_part = stacked[:, :half_rows]
        upper_part = stacked[:, half_rows:]
        kept_part = jnp.where(upper_side, upper_part, lower_part)
        sent_part = jnp.where(upper_side, lower_part, upper_part)
        stacked = kept_part + partner(sent_part, "ctxb", bit_pos)
    return stacked


def from_segment(first_part, second_part):
    return (
        lax.all_gather(first_part, "ctxb", axis=1, tiled=True),
        lax.all_gather(second_part, "ctxb", axis=1, tiled=True),
    )


def from_everyone(first_part, second_part):
    return (
        lax.all_gather(first_part, ("ctxa", "ctxb"), axis=1, tiled=True),
        lax.all_gather(second_part, ("ctxa", "ctxb"), axis=1, tiled=True),
    )


def local(queries, key_matrix, value_matrix, grad_out, offsets):
    tok_rows = queries.shape[0]
    head_count = offsets.shape[0]
    mask_per_level = [
        selection_mask(offsets, spacing_factor)
        for spacing_factor in (1, MIDDLE_DILATION, UPPER_DILATION)
    ]
    query_sets = [select_rows(queries, level_mask) for level_mask in mask_per_level]
    own_keys = [select_rows(key_matrix, level_mask) for level_mask in mask_per_level]
    own_values = [select_rows(value_matrix, level_mask) for level_mask in mask_per_level]
    grad_sets = [select_rows(grad_out, level_mask) for level_mask in mask_per_level]
    near_stack = near_key_gather(jnp.stack((key_matrix, value_matrix)))
    near_keys = select_rows(near_stack[0], mask_per_level[0])
    near_values = select_rows(near_stack[1], mask_per_level[0])
    mid_keys, mid_values = from_segment(own_keys[1], own_values[1])
    far_keys, far_values = from_everyone(own_keys[2], own_values[2])
    key_sets = [near_keys, mid_keys, far_keys]
    value_sets = [near_values, mid_values, far_values]
    stats = [
        by_heads(level_forward, (query_sets[level_idx], key_sets[level_idx], value_sets[level_idx]))
        for level_idx in range(3)
    ]
    spread_levels = jnp.stack(
        [
            spread_scalar(
                stats[level_idx][0] + jnp.log(stats[level_idx][1]),
                mask_per_level[level_idx],
                FILL_LOW,
            )
            for level_idx in range(3)
        ]
    )
    lse_max = jnp.max(spread_levels, axis=0)
    log_sum = lse_max + jnp.log(jnp.sum(jnp.exp(spread_levels - lse_max), axis=0))
    level_sums = [collect_scalar(log_sum, level_mask) for level_mask in mask_per_level]
    attended = jnp.zeros((tok_rows, queries.shape[1]), jnp.float32)
    for level_idx in range(3):
        row_max, row_sum, row_accumulator = stats[level_idx]
        attended = attended + place_rows(
            row_accumulator * jnp.exp(row_max - level_sums[level_idx])[..., None],
            mask_per_level[level_idx],
        )
    row_dots = jnp.sum(
        grad_out.astype(jnp.float32).reshape(tok_rows, head_count, -1)
        * attended.reshape(tok_rows, head_count, -1),
        axis=-1,
    ).T
    dot_sets = [collect_scalar(row_dots, level_mask) for level_mask in mask_per_level]
    near_dq, group_dk, group_dv = by_heads(
        partial(level_backward, wanted="all"),
        (query_sets[0], near_keys, near_values, grad_sets[0], level_sums[0], dot_sets[0]),
    )
    near_sums = near_reduce(
        jnp.stack(
            (place_rows(group_dk, mask_per_level[0]), place_rows(group_dv, mask_per_level[0]))
        )
    )
    near_key_grad = near_sums[0]
    near_value_grad = near_sums[1]
    (mid_dq,) = by_heads(
        partial(level_backward, wanted="queries"),
        (query_sets[1], mid_keys, mid_values, grad_sets[1], level_sums[1], dot_sets[1]),
    )
    group_queries, group_grads = from_segment(query_sets[1], grad_sets[1])
    group_sums, group_dots = (
        lax.all_gather(level_sums[1], "ctxb", axis=1, tiled=True),
        lax.all_gather(dot_sets[1], "ctxb", axis=1, tiled=True),
    )
    mid_dk, mid_dv = by_heads(
        partial(level_backward, wanted="keys"),
        (group_queries, own_keys[1], own_values[1], group_grads, group_sums, group_dots),
    )
    (far_dq,) = by_heads(
        partial(level_backward, wanted="queries"),
        (query_sets[2], far_keys, far_values, grad_sets[2], level_sums[2], dot_sets[2]),
    )
    all_queries, all_grads = from_everyone(query_sets[2], grad_sets[2])
    all_sums, all_dots = (
        lax.all_gather(level_sums[2], ("ctxa", "ctxb"), axis=1, tiled=True),
        lax.all_gather(dot_sets[2], ("ctxa", "ctxb"), axis=1, tiled=True),
    )
    far_dk, far_dv = by_heads(
        partial(level_backward, wanted="keys"),
        (all_queries, own_keys[2], own_values[2], all_grads, all_sums, all_dots),
    )
    grad_q = (
        place_rows(near_dq, mask_per_level[0])
        + place_rows(mid_dq, mask_per_level[1])
        + place_rows(far_dq, mask_per_level[2])
    )
    grad_k = (
        near_key_grad
        + place_rows(mid_dk, mask_per_level[1])
        + place_rows(far_dk, mask_per_level[2])
    )
    grad_v = (
        near_value_grad
        + place_rows(mid_dv, mask_per_level[1])
        + place_rows(far_dv, mask_per_level[2])
    )
    return (grad_q.astype(jnp.bfloat16), grad_k.astype(jnp.bfloat16), grad_v.astype(jnp.bfloat16))


def solution(mesh):
    placed = (
        P(("ctxa", "ctxb"), None),
        P(("ctxa", "ctxb"), None),
        P(("ctxa", "ctxb"), None),
        P(("ctxa", "ctxb"), None),
        P(),
    )
    return jax.shard_map(
        local,
        mesh=mesh,
        in_specs=placed,
        out_specs=(P(("ctxa", "ctxb"), None), P(("ctxa", "ctxb"), None), P(("ctxa", "ctxb"), None)),
        check_vma=False,
    )
```

profile of v0, /device:TPU:0, one launch (start us, length us, event | category | flops | bytes accessed | tf_op | source)
XLA Modules:
  0.0 629.5 jit_solution(15358927248383743621)
XLA Ops:
  9.5 2.9 fusion.201
  12.8 43.3 %all_gather.38 = bf16[6,64,64]{2,0,1:T(8,128)(2,1)S(1)} all-gather(bf16[6,2,64]{2,0,1:T(8,128)(2,1)S(1)} %copy.337), channel_id=1, replica_groups=mesh['ctxa'=4,'ctxb'=8] {'ctxa','ctxb'}, dimensions={1}, use_global_device_ids=true | all-gather | bytes 50688 | tf_op jit(solution)/shard_map/all_gather | solution.py:154
  56.1 37.2 %all_gather.39 = bf16[6,64,64]{2,0,1:T(8,128)(2,1)S(1)} all-gather(bf16[6,2,64]{2,0,1:T(8,128)(2,1)S(1)} %copy.339), channel_id=1, replica_groups=mesh['ctxa'=4,'ctxb'=8] {'ctxa','ctxb'}, dimensions={1}, use_global_device_ids=true | all-gather | bytes 50688 | tf_op jit(solution)/shard_map/all_gather | solution.py:155
  93.3 7.1 %while.102 = (s32[]{:T(128)}, f32[6,1,2]{2,1,0:T(1,128)S(1)}, f32[6,1,2]{2,1,0:T(1,128)}, f32[6,1,2,64]{3,2,1,0:T(2,128)S(1)}, bf16[6,1,2,64]{3,2,1,0:T(2,128)(2...) while((s32[]{:T(128)}, f32[6,1,2]{2,1,0:T(1,128)S(1)}, ...), condition=%wide.region_17.18_spmd, body=%wide.region_14.17_spmd.sunk | while | flops 33534 | bytes 41081 | solution.py:112
  104.8 14.4 %all_gather.36 = bf16[6,256,64]{2,1,0:T(8,128)(2,1)S(1)} all-gather(bf16[6,32,64]{2,1,0:T(8,128)(2,1)S(1)} %copy.329), channel_id=1, replica_groups=mesh['ctxa'=4,'ctxb'=8] {'ctxb'}, dimensions={1}, use_global_device_ids=true | all-gather | bytes 221184 | tf_op jit(solution)/shard_map/all_gather | solution.py:147
  119.2 14.5 %all_gather.37 = bf16[6,256,64]{2,1,0:T(8,128)(2,1)S(1)} all-gather(bf16[6,32,64]{2,1,0:T(8,128)(2,1)S(1)} %copy.330), channel_id=1, replica_groups=mesh['ctxa'=4,'ctxb'=8] {'ctxb'}, dimensions={1}, use_global_device_ids=true | all-gather | bytes 221184 | tf_op jit(solution)/shard_map/all_gather | solution.py:148
  133.8 4.4 while.101
  148.4 45.9 %all_gather.46 = bf16[6,64,64]{2,0,1:T(8,128)(2,1)S(1)} all-gather(bf16[6,2,64]{2,0,1:T(8,128)(2,1)S(1)} %copy.390), channel_id=1, replica_groups=mesh['ctxa'=4,'ctxb'=8] {'ctxa','ctxb'}, dimensions={1}, use_global_device_ids=true | all-gather | bytes 50688 | tf_op jit(solution)/shard_map/all_gather | solution.py:155
  196.4 37.1 %all_gather.44 = bf16[6,64,64]{2,0,1:T(8,128)(2,1)S(1)} all-gather(bf16[6,2,64]{2,0,1:T(8,128)(2,1)S(1)} %copy.387), channel_id=1, replica_groups=mesh['ctxa'=4,'ctxb'=8] {'ctxa','ctxb'}, dimensions={1}, use_global_device_ids=true | all-gather | bytes 50688 | tf_op jit(solution)/shard_map/all_gather | solution.py:154
  237.1 15.5 %all_gather.42 = bf16[6,256,64]{2,1,0:T(8,128)(2,1)} all-gather(bf16[6,32,64]{2,1,0:T(8,128)(2,1)S(1)} %copy.377), channel_id=1, replica_groups=mesh['ctxa'=4,'ctxb'=8] {'ctxb'}, dimensions={1}, use_global_device_ids=true | all-gather | bytes 221184 | tf_op jit(solution)/shard_map/all_gather | solution.py:148
  252.6 15.7 %all_gather.40 = bf16[6,256,64]{2,1,0:T(8,128)(2,1)} all-gather(bf16[6,32,64]{2,1,0:T(8,128)(2,1)S(1)} %copy.375), channel_id=1, replica_groups=mesh['ctxa'=4,'ctxb'=8] {'ctxb'}, dimensions={1}, use_global_device_ids=true | all-gather | bytes 221184 | tf_op jit(solution)/shard_map/all_gather | solution.py:147
  273.8 23.2 %while.100 = (s32[]{:T(128)}, f32[6,1,256]{2,0,1:T(8,128)S(1)}, f32[6,1,256]{2,0,1:T(8,128)}, f32[6,1,256,64]{2,3,1,0:T(8,128)}, bf16[6,1,256,64]{3,2,1,0:T(8,12...) while((s32[]{:T(128)}, f32[6,1,256]{2,0,1:T(8,128)S(1)}, ...), condition=%wide.region_3.4_spmd, body=%wide.region_0.3_spmd.sunk | while | flops 68681216 | bytes 3811437 | solution.py:112
  312.7 2.2 broadcast_in_dim.551
  314.8 2.1 broadcast_in_dim.552
  318.8 2.2 copy.349
  321.0 2.1 fusion.197
  327.7 40.8 %all-gather.2 = f32[32,2,6]{2,1,0:T(2,128)} all-gather(f32[1,2,6]{2,1,0:T(2,128)} %bitcast.662), channel_id=1, replica_groups=mesh['ctxa'=4,'ctxb'=8] {'ctxa','ctxb'}, dimensions={0}, use_global_device_ids=true | all-gather | bytes 1584 | tf_op jit(solution)/shard_map/all_gather | solution.py:237
  369.9 14.0 %all-gather = f32[8,32,6]{1,2,0:T(8,128)S(1)} all-gather(f32[1,32,6]{1,2,0:T(8,128)S(1)} %bitcast.645), channel_id=1, replica_groups=mesh['ctxa'=4,'ctxb'=8] {'ctxb'}, dimensions={0}, use_global_device_ids=true | all-gather | bytes 6912 | tf_op jit(solution)/shard_map/all_gather | solution.py:224
  387.4 39.4 %all-gather.3 = f32[32,2,6]{2,1,0:T(2,128)} all-gather(f32[1,2,6]{2,1,0:T(2,128)} %bitcast.663), channel_id=1, replica_groups=mesh['ctxa'=4,'ctxb'=8] {'ctxa','ctxb'}, dimensions={0}, use_global_device_ids=true | all-gather | bytes 1584 | tf_op jit(solution)/shard_map/all_gather | solution.py:238
  430.7 29.9 %while.107 = (s32[]{:T(128)}, f32[6,1,2,64]{3,2,1,0:T(2,128)}, f32[6,1,2,64]{3,2,1,0:T(2,128)}, bf16[6,1,64,64]{3,2,1,0:T(8,128)(2,1)}, bf16[6,1,2,64]{3,2,1,0:T...) while((s32[]{:T(128)}, f32[6,1,2,64]{3,2,1,0:T(2,128)}, ...), condition=%wide.region_35.36_spmd, body=%wide.region_34.35_spmd.sunk | while | flops 66434 | bytes 76145 | solution.py:112
  462.8 23.3 %while.104 = (s32[]{:T(128)}, f32[6,1,32,64]{3,2,1,0:T(8,128)}, bf16[6,1,32,64]{3,2,1,0:T(8,128)(2,1)}, bf16[6,1,256,64]{3,2,1,0:T(8,128)(2,1)S(1)}, f32[6,1,32]...) while((s32[]{:T(128)}, f32[6,1,32,64]{3,2,1,0:T(8,128)}, ...), condition=%wide.region_27.28_spmd, body=%wide.region_26.27_spmd.sunk | while | flops 3194882 | bytes 299625 | solution.py:112
  486.1 14.5 %all-gather.1 = f32[8,32,6]{1,2,0:T(8,128)S(1)} all-gather(f32[1,32,6]{1,2,0:T(8,128)} %bitcast.651), channel_id=1, replica_groups=mesh['ctxa'=4,'ctxb'=8] {'ctxb'}, dimensions={0}, use_global_device_ids=true | all-gather | bytes 6912 | tf_op jit(solution)/shard_map/all_gather | solution.py:225
  500.7 23.1 %while.106 = (s32[]{:T(128)}, f32[6,1,32,64]{3,2,1,0:T(8,128)S(1)}, f32[6,1,32,64]{3,2,1,0:T(8,128)S(1)}, bf16[6,1,256,64]{3,2,1,0:T(8,128)(2,1)}, bf16[6,1,32,6...) while((s32[]{:T(128)}, f32[6,1,32,64]{3,2,1,0:T(8,128)S(1)}, ...), condition=%wide.region_33.34_spmd, body=%wide.region_32.33_spmd.sunk | while | flops 4251650 | bytes 419953 | solution.py:112
  524.6 44.3 %while.103 = (s32[]{:T(128)}, f32[6,1,256,64]{2,3,1,0:T(8,128)S(1)}, f32[6,1,1024,64]{2,3,1,0:T(8,128)}, f32[6,1,1024,64]{2,3,1,0:T(8,128)}, bf16[6,1,256,64]{3,...) while((s32[]{:T(128)}, f32[6,1,256,64]{2,3,1,0:T(8,128)S(1)}, ...), condition=%wide.region_23.24_spmd, body=%wide.region_22.23_spmd.sunk | while | flops 169607168 | bytes 6302845 | solution.py:112
  552.3 1.8 fusion.311
  569.6 2.3 broadcast_select_fusion
  572.0 15.2 %while.105 = (s32[]{:T(128)}, f32[6,1,2,64]{3,2,1,0:T(2,128)S(1)}, bf16[6,1,2,64]{3,2,1,0:T(2,128)(2,1)}, bf16[6,1,64,64]{3,2,1,0:T(8,128)(2,1)}, f32[6,1,2]{2,0...) while((s32[]{:T(128)}, f32[6,1,2,64]{3,2,1,0:T(2,128)S(1)}, ...), condition=%wide.region_31.32_spmd, body=%wide.region_30.31_spmd.sunk | while | flops 49922 | bytes 56465 | solution.py:112
  592.1 16.6 %collective-permute-done.2 = f32[2,512,384]{1,2,0:T(8,128)} collective-permute-done((f32[2,512,384]{1,2,0:T(8,128)S(1)}, f32[2,512,384]{1,2,0:T(8,128)}, u32[]{:S(2)}, u32[]{:S(2)}) %collective-permute-start.2) | collective-permute-done | bytes 1572896 | tf_op jit(solution)/shard_map/ppermute | solution.py:20
  608.7 2.4 select_add_fusion
  612.1 1.8 broadcast_select_fusion.1
  616.4 2.2 select_n.334
  619.8 3.5 broadcast_select_fusion.4
  (460 shorter events, 253.3 us)
Async XLA Ops:
  0.6 5.1 copy-start.8
  3.7 136.5 %collective-permute-start = (bf16[2,256,384]{1,2,0:T(8,128)(2,1)}, bf16[2,256,384]{1,2,0:T(8,128)(2,1)}, u32[]{:S(2)}, u32[]{:S(2)}) collective-permute-start(bf16[2,256,384]{1,2,0:T(8,128)(2,1)} %pad_maximum_fusion.1), channel_id=1, source_target_pairs={{0,1},{1,0},{2,3},{3,2},{4,5},{5,4},{6,7},{7,6},{8,9},{9,8},{10,11... | collective-permute-start | bytes 1179656 | tf_op jit(solution)/shard_map/ppermute | solution.py:20
  4.2 140.3 %copy-start.41 = (pred[6,128]{1,0:T(8,128)(4,1)}, pred[6,128]{1,0:T(8,128)(4,1)S(1)}, u32[]{:S(2)}) copy-start(pred[6,128]{1,0:T(8,128)(4,1)S(1)} %iota_compare_fusion.1) | copy-start | bytes 2308
  4.3 264.0 %copy-start.45 = (pred[128,6]{0,1:T(8,128)(4,1)}, pred[128,6]{0,1:T(8,128)(4,1)S(1)}, u32[]{:S(2)}) copy-start(pred[128,6]{0,1:T(8,128)(4,1)S(1)} %iota_compare_fusion) | copy-start | bytes 2308
  7.0 49.1 %copy-start.1 = (bf16[256,384]{0,1:T(8,128)(2,1)}, bf16[256,384]{0,1:T(8,128)(2,1)S(1)}, u32[]{:S(2)}) copy-start(bf16[256,384]{0,1:T(8,128)(2,1)S(1)} %copy.346) | copy-start | bytes 589828
  7.3 95.4 %copy-start.47 = (pred[8,6]{1,0:T(8,128)(4,1)}, pred[8,6]{1,0:T(8,128)(4,1)S(1)}, u32[]{:S(2)}) copy-start(pred[8,6]{1,0:T(8,128)(4,1)S(1)} %iota_compare_fusion.2) | copy-start | bytes 148
  101.0 18.2 %copy-start.40 = (f32[6,1,2,64]{3,2,1,0:T(2,128)}, f32[6,1,2,64]{3,2,1,0:T(2,128)S(1)}, u32[]{:S(2)}) copy-start(f32[6,1,2,64]{3,2,1,0:T(2,128)S(1)} %get-tuple-element.362) | copy-start | bytes 9220
  101.0 18.2 %copy-start.43 = (bf16[6,1,2,64]{3,2,1,0:T(2,128)(2,1)}, bf16[6,1,2,64]{3,2,1,0:T(2,128)(2,1)S(1)}, u32[]{:S(2)}) copy-start(bf16[6,1,2,64]{3,2,1,0:T(2,128)(2,1)S(1)} %get-tuple-element.1543) | copy-start | bytes 4612
  102.7 93.0 %copy-start.31 = (f32[6,2]{1,0:T(8,128)}, f32[6,2]{1,0:T(8,128)S(1)}, u32[]{:S(2)}) copy-start(f32[6,2]{1,0:T(8,128)S(1)} %copy.345) | copy-start | bytes 148
  104.2 15.1 %copy-start.16 = (bf16[32,6,64]{2,1,0:T(8,128)(2,1)}, bf16[32,6,64]{2,1,0:T(8,128)(2,1)S(1)}, u32[]{:S(2)}) copy-start(bf16[32,6,64]{2,1,0:T(8,128)(2,1)S(1)} %get-tuple-element.708) | copy-start | bytes 73732
  104.2 29.6 %copy-start.18 = (bf16[32,6,64]{2,1,0:T(8,128)(2,1)}, bf16[32,6,64]{2,1,0:T(8,128)(2,1)S(1)}, u32[]{:S(2)}) copy-start(bf16[32,6,64]{2,1,0:T(8,128)(2,1)S(1)} %get-tuple-element.709) | copy-start | bytes 73732
  133.8 7.8 %copy-start.53 = (s32[6]{0:T(128)S(1)}, s32[6]{0:T(128)}, u32[]{:S(2)}) copy-start(s32[6]{0:T(128)} %copy-done.52) | copy-start | bytes 76
  133.8 11.5 %copy-start.49 = (pred[8,6]{0,1:T(8,128)(4,1)S(1)}, pred[8,6]{0,1:T(8,128)(4,1)}, u32[]{:S(2)}) copy-start(pred[8,6]{0,1:T(8,128)(4,1)} %copy.347) | copy-start | bytes 148
  138.2 57.5 %copy-start.42 = (f32[6,1,32]{2,0,1:T(8,128)}, f32[6,1,32]{2,0,1:T(8,128)S(1)}, u32[]{:S(2)}) copy-start(f32[6,1,32]{2,0,1:T(8,128)S(1)} %get-tuple-element.356) | copy-start | bytes 2308
  140.2 93.4 %copy-start.33 = (f32[6,32]{1,0:T(8,128)}, f32[6,32]{1,0:T(8,128)S(1)}, u32[]{:S(2)}) copy-start(f32[6,32]{1,0:T(8,128)S(1)} %bitcast_add_fusion.7) | copy-start | bytes 2308
  141.5 93.7 %copy-start.19 = (bf16[32,6,64]{2,1,0:T(8,128)(2,1)S(1)}, bf16[32,6,64]{2,1,0:T(8,128)(2,1)}, u32[]{:S(2)}) copy-start(bf16[32,6,64]{2,1,0:T(8,128)(2,1)} %copy-done.18) | copy-start | bytes 73732
  141.5 93.7 %copy-start.17 = (bf16[32,6,64]{2,1,0:T(8,128)(2,1)S(1)}, bf16[32,6,64]{2,1,0:T(8,128)(2,1)}, u32[]{:S(2)}) copy-start(bf16[32,6,64]{2,1,0:T(8,128)(2,1)} %copy-done.16) | copy-start | bytes 73732
  141.5 94.3 %copy-start.15 = (bf16[32,6,64]{2,1,0:T(8,128)(2,1)S(1)}, bf16[32,6,64]{2,1,0:T(8,128)(2,1)}, u32[]{:S(2)}) copy-start(bf16[32,6,64]{2,1,0:T(8,128)(2,1)} %copy-done.14) | copy-start | bytes 73732
  141.5 94.9 %copy-start.13 = (bf16[32,6,64]{2,1,0:T(8,128)(2,1)S(1)}, bf16[32,6,64]{2,1,0:T(8,128)(2,1)}, u32[]{:S(2)}) copy-start(bf16[32,6,64]{2,1,0:T(8,128)(2,1)} %get-tuple-element.706) | copy-start | bytes 73732
  141.5 127.4 %collective-permute-start.1 = (bf16[2,512,384]{1,2,0:T(8,128)(2,1)S(1)}, bf16[2,512,384]{1,2,0:T(8,128)(2,1)S(1)}, u32[]{:S(2)}, u32[]{:S(2)}) collective-permute-start(bf16[2,512,384]{1,2,0:T(8,128)(2,1)S(1)} %maximum_select_fusion.1), channel_id=1, source_target_pairs={{0,2},{1,3},{2,0},{3,1},{4,6},{5,7},{6,4},{7,5},{8,10},{9,11},{10,... | collective-permute-start | bytes 2359304 | tf_op jit(solution)/shard_map/ppermute | solution.py:20
  309.1 18.0 %copy-start.32 = (f32[6,2]{1,0:T(8,128)}, f32[6,2]{1,0:T(8,128)S(1)}, u32[]{:S(2)}) copy-start(f32[6,2]{1,0:T(8,128)S(1)} %select_reduce_fusion.7) | copy-start | bytes 148
  386.7 44.0 %copy-start.36 = (f32[6,2]{1,0:T(8,128)}, f32[6,2]{1,0:T(8,128)S(1)}, u32[]{:S(2)}) copy-start(f32[6,2]{1,0:T(8,128)S(1)} %select_reduce_fusion.6) | copy-start | bytes 148
  486.1 37.8 %copy-start.30 = (f32[6,256]{1,0:T(8,128)S(1)}, f32[6,256]{1,0:T(8,128)}, u32[]{:S(2)}) copy-start(f32[6,256]{1,0:T(8,128)} %copy-done.29) | copy-start | bytes 18436
  486.1 37.8 %copy-start.34 = (f32[6,1,256]{2,0,1:T(8,128)S(1)}, f32[6,1,256]{2,0,1:T(8,128)}, u32[]{:S(2)}) copy-start(f32[6,1,256]{2,0,1:T(8,128)} %select_n.320) | copy-start | bytes 18436
  486.1 37.8 %copy-start.35 = (f32[6,1,256]{2,0,1:T(8,128)S(1)}, f32[6,1,256]{2,0,1:T(8,128)}, u32[]{:S(2)}) copy-start(f32[6,1,256]{2,0,1:T(8,128)} %select_n.314) | copy-start | bytes 18436
  569.6 17.7 %copy-start.24 = (f32[6,1,32,64]{3,2,1,0:T(8,128)S(1)}, f32[6,1,32,64]{3,2,1,0:T(8,128)}, u32[]{:S(2)}) copy-start(f32[6,1,32,64]{3,2,1,0:T(8,128)} %get-tuple-element.364) | copy-start | bytes 147460
  569.6 18.3 %copy-start.23 = (f32[6,1,32,64]{3,2,1,0:T(8,128)S(1)}, f32[6,1,32,64]{3,2,1,0:T(8,128)}, u32[]{:S(2)}) copy-start(f32[6,1,32,64]{3,2,1,0:T(8,128)} %copy-done.22) | copy-start | bytes 147460
  569.6 19.4 %copy-start.38 = (f32[6,1,2,64]{3,2,1,0:T(2,128)S(1)}, f32[6,1,2,64]{3,2,1,0:T(2,128)}, u32[]{:S(2)}) copy-start(f32[6,1,2,64]{3,2,1,0:T(2,128)} %get-tuple-element.369) | copy-start | bytes 9220
  569.6 39.1 %copy-start = (f32[6,1,1024,64]{2,3,1,0:T(8,128)S(1)}, f32[6,1,1024,64]{2,3,1,0:T(8,128)}, u32[]{:S(2)}) copy-start(f32[6,1,1024,64]{2,3,1,0:T(8,128)} %get-tuple-element.367) | copy-start | bytes 4718596
  571.9 17.9 %copy-start.37 = (f32[6,1,2,64]{3,2,1,0:T(2,128)S(1)}, f32[6,1,2,64]{3,2,1,0:T(2,128)}, u32[]{:S(2)}) copy-start(f32[6,1,2,64]{3,2,1,0:T(2,128)} %get-tuple-element.371) | copy-start | bytes 9220
  572.0 36.8 %collective-permute-start.2 = (f32[2,512,384]{1,2,0:T(8,128)S(1)}, f32[2,512,384]{1,2,0:T(8,128)}, u32[]{:S(2)}, u32[]{:S(2)}) collective-permute-start(f32[2,512,384]{1,2,0:T(8,128)S(1)} %broadcast_select_fusion), channel_id=1, source_target_pairs={{0,2},{1,3},{2,0},{3,1},{4,6},{5,7},{6,4},{7,5},{8,10},{9,11},{10,... | collective-permute-start | bytes 4718600 | tf_op jit(solution)/shard_map/ppermute | solution.py:20
  612.1 14.1 %collective-permute-start.3 = (f32[2,256,384]{1,2,0:T(8,128)}, f32[2,256,384]{1,2,0:T(8,128)}, u32[]{:S(2)}, u32[]{:S(2)}) collective-permute-start(f32[2,256,384]{1,2,0:T(8,128)} %slice_select_fusion), channel_id=1, source_target_pairs={{0,1},{1,0},{2,3},{3,2},{4,5},{5,4},{6,7},{7,6},{8,9},{9,8},{10,11... | collective-permute-start | bytes 2359304 | tf_op jit(solution)/shard_map/ppermute | solution.py:20
  (26 other events, 54.4 us)
where the time goes:
time: 637 us; the launch traced here: 630 us
  blocking collectives  332 us (52%)
  matrix products  126 us (20%)
  local copies, waits for them, and re-layouts  111 us (17%)
  other arithmetic  40.4 us (6%)
  waiting for transfers between devices  16.6 us (3%)
    all_gather x2, blocking collectives, from_everyone(): lax.all_gather(second_part, ('ctxa', 'ctxb'), axis=1, tiled=True)  83.1 us
    all_gather x2, blocking collectives, from_everyone(): lax.all_gather(first_part, ('ctxa', 'ctxb'), axis=1, tiled=True)  80.5 us
    all_gather x1, blocking collectives, local(): lax.all_gather(level_sums[2], ('ctxa', 'ctxb'), axis=1, tiled=True)  40.8 us
    all_gather x1, blocking collectives, local(): lax.all_gather(dot_sets[2], ('ctxa', 'ctxb'), axis=1, tiled=True)  39.4 us
    dot_general x30, matrix products, level_backward(): jnp.einsum('sle,sie->sli', query_matrix, key_matrix, preferred_element_ty...  31.6 us
    all_gather x2, blocking collectives, from_segment(): lax.all_gather(first_part, 'ctxb', axis=1, tiled=True)  30.2 us
    all_gather x2, blocking collectives, from_segment(): lax.all_gather(second_part, 'ctxb', axis=1, tiled=True)  30 us
    dot_general x18, matrix products, level_backward(): jnp.einsum('axm,axh->amh', score_gradient, query_matrix, preferred_elemen...  27.2 us
  transfers between devices with their start and end apart: 4, of which 1 were waited for; matrix products, arithmetic and copies ran while one was open for 11% of the time, Pallas kernels for 0%

commit v1 on v0

v1 whole, which is shorter than its diff:
```python
from functools import partial

import jax
import jax.numpy as jnp
from jax import lax
from jax.experimental import pallas as pl
from jax.experimental.pallas import tpu as pltpu
from jax.sharding import PartitionSpec as P

HD = 64
PAIR = 2 * HD
GROUP = 4
MIDDLE = 8
UPPER = 128
LOW = -1e30
HIGH = 1e30
SCALE = HD**-0.5
F32 = jnp.float32
BF16 = jnp.bfloat16
STAT_ROWS = 16


def iota(shape, dim):
    return lax.broadcasted_iota(jnp.int32, shape, dim)


def dot_nt(a, b):
    return lax.dot_general(a, b, (((1,), (1,)), ((), ())), preferred_element_type=F32)


def dot_nn(a, b):
    return jnp.dot(a, b, preferred_element_type=F32)


def pair_slice(head):
    low = head // 2 * PAIR
    return slice(low, low + PAIR)


def half_mask(head):
    return iota((1, PAIR), 1) // HD == head % 2


def one_head(block, head, scale=1.0):
    return jnp.where(half_mask(head), block.astype(F32) * scale, 0.0).astype(BF16)


def lane_offsets(off_ref, heads, width):
    lane_head = iota((1, width), 1) // HD
    out = jnp.zeros((1, width), jnp.int32)
    for head in range(heads):
        out = jnp.where(lane_head == head, off_ref[head], out)
    return out


def row_offsets(off_ref, heads):
    rows = iota((STAT_ROWS, 1), 0)
    out = jnp.zeros((STAT_ROWS, 1), jnp.int32)
    for head in range(heads):
        out = jnp.where((rows == head) | (rows == head + heads), off_ref[head], out)
    return out


def pair_weights(rows, middle_offset):
    both = (iota((rows, rows), 0) % MIDDLE == middle_offset) & (
        iota((rows, rows), 1) % MIDDLE == middle_offset
    )
    return jnp.where(both, 2.0, 1.0)


def pack_kernel(off_ref, q_ref, k_ref, v_ref, g_ref, near_ref, spec_ref):
    rows, width = q_ref.shape
    heads = width // HD
    near_rows, spec_rows = rows // MIDDLE, rows // UPPER
    offsets = lane_offsets(off_ref, heads, width)
    token = iota((rows, width), 0)
    middle = token % MIDDLE == offsets % MIDDLE
    upper = token % UPPER == offsets
    for near_slot, spec_slot, ref in ((0, 1, k_ref), (1, 2, v_ref), (2, 0, q_ref), (3, 3, g_ref)):
        whole = ref[...].astype(F32)
        kept = jnp.where(middle, whole, 0.0).reshape(near_rows, MIDDLE, width).sum(axis=1)
        near_ref[near_slot * near_rows : (near_slot + 1) * near_rows, :] = kept.astype(BF16)
        top = jnp.where(upper, whole, 0.0).reshape(spec_rows, UPPER, width).sum(axis=1)
        spec_ref[spec_slot * spec_rows : (spec_slot + 1) * spec_rows, :] = top


def near_part(near_refs, slot, lanes):
    rows = near_refs[0].shape[0] // 4
    return jnp.concatenate([r[slot * rows : (slot + 1) * rows, lanes] for r in near_refs], axis=0)


def forward_kernel(near_count, off_ref, q_ref, g_ref, spec_ref, *refs):
    k_refs, v_refs = refs[:GROUP], refs[GROUP : 2 * GROUP]
    near_refs = refs[2 * GROUP : 2 * GROUP + near_count]
    out_ref = refs[-1]
    rows, width = q_ref.shape
    heads = width // HD
    log_sums, dots = [], []
    for head in range(heads):
        lanes = pair_slice(head)
        middle_offset = off_ref[head] % MIDDLE
        chosen = iota((1, rows), 1) % MIDDLE == middle_offset
        weight = pair_weights(rows, middle_offset)
        query = one_head(q_ref[:, lanes], head, SCALE)
        grad = one_head(g_ref[:, lanes], head)
        scores = [dot_nt(r[:, lanes], query) for r in k_refs]
        top = jnp.max(scores[0], axis=0, keepdims=True)
        for part in scores[1:]:
            top = jnp.maximum(top, jnp.max(part, axis=0, keepdims=True))
        if near_count:
            far_scores = dot_nt(near_part(near_refs, 0, lanes), query)
            far_scores = jnp.where(chosen, far_scores, LOW)
            top = jnp.maximum(top, jnp.max(far_scores, axis=0, keepdims=True))
        total = jnp.zeros((1, rows), F32)
        product = jnp.zeros((1, rows), F32)
        for part, v_ref in zip(scores, v_refs):
            weights = jnp.exp(part - top) * weight
            total = total + jnp.sum(weights, axis=0, keepdims=True)
            inner = dot_nt(v_ref[:, lanes], grad)
            product = product + jnp.sum(weights * inner, axis=0, keepdims=True)
        if near_count:
            weights = jnp.exp(far_scores - top)
            total = total + jnp.sum(weights, axis=0, keepdims=True)
            inner = dot_nt(near_part(near_refs, 1, lanes), grad)
            product = product + jnp.sum(weights * inner, axis=0, keepdims=True)
        log_sums.append(top + jnp.log(total))
        dots.append(product / total)
    pad = jnp.zeros((STAT_ROWS - 2 * heads, rows), F32)
    stats = jnp.concatenate(log_sums + dots + [pad], axis=0)
    out_ref[:, :rows] = stats
    offsets = row_offsets(off_ref, heads)
    token = iota((STAT_ROWS, rows), 1)
    kept = jnp.where(token % MIDDLE == offsets % MIDDLE, stats, 0.0)
    gather = jnp.where(iota((rows, PAIR), 0) // MIDDLE == iota((rows, PAIR), 1), 1.0, 0.0)
    out_ref[:, rows : rows + PAIR] = jnp.dot(
        kept, gather, precision=lax.Precision.HIGHEST, preferred_element_type=F32
    )
    base = rows + PAIR
    spec_rows = rows // UPPER
    out_ref[:, base:] = jnp.zeros((STAT_ROWS, width), F32)
    out_ref[: 4 * spec_rows, base:] = spec_ref[...]
    lane = iota((STAT_ROWS, width), 1)
    row = iota((STAT_ROWS, width), 0)
    place = iota((1, width), 1) % HD
    for index in range(spec_rows):
        value = jnp.sum(
            jnp.where(token == offsets + index * UPPER, stats, 0.0), axis=1, keepdims=True
        )
        line = jnp.zeros((1, width), F32)
        for kind in range(2):
            left = jnp.sum(
                jnp.where(lane // HD + kind * heads == row, value, 0.0), axis=0, keepdims=True
            )
            for term in range(3):
                rounded = left.astype(BF16).astype(F32)
                line = jnp.where(place == 3 * kind + term, rounded, line)
                left = left - rounded
        out_ref[4 * spec_rows + index : 4 * spec_rows + index + 1, base:] = line


def query_kernel(near_count, off_ref, q_ref, g_ref, pay_ref, *refs):
    k_refs, v_refs = refs[:GROUP], refs[GROUP : 2 * GROUP]
    near_refs = refs[2 * GROUP : 2 * GROUP + near_count]
    dq_ref, spec_ref = refs[-2:]
    rows, width = q_ref.shape
    heads = width // HD
    spec_rows = rows // UPPER
    columns = jnp.transpose(pay_ref[:, :rows])
    offsets = lane_offsets(off_ref, heads, width)
    for pair in range(heads // 2):
        lanes = slice(pair * PAIR, (pair + 1) * PAIR)
        grads, sums = [], []
        for head in (2 * pair, 2 * pair + 1):
            middle_offset = off_ref[head] % MIDDLE
            chosen = iota((rows, 1), 0) % MIDDLE == middle_offset
            weight = pair_weights(rows, middle_offset)
            query = one_head(q_ref[:, lanes], head, SCALE)
            grad = one_head(g_ref[:, lanes], head)
            log_sum = columns[:, head : head + 1]
            dot = columns[:, heads + head : heads + head + 1]
            grad_q = jnp.zeros((rows, PAIR), F32)
            key_sum = jnp.zeros((rows, PAIR), F32)
            for k_ref, v_ref in zip(k_refs, v_refs):
                keys = k_ref[:, lanes]
                probs = jnp.exp(dot_nt(query, keys) - log_sum) * weight
                inner = dot_nt(grad, v_ref[:, lanes]) - dot
                grad_q = grad_q + dot_nn((probs * inner).astype(BF16), keys)
                key_sum = key_sum + dot_nn(probs.astype(BF16), keys)
            if near_count:
                keys = near_part(near_refs, 0, lanes)
                scores = jnp.where(chosen, dot_nt(query, keys), LOW)
                probs = jnp.exp(scores - log_sum)
                inner = dot_nt(grad, near_part(near_refs, 1, lanes)) - dot
                grad_q = grad_q + dot_nn((probs * inner).astype(BF16), keys)
                key_sum = key_sum + dot_nn(probs.astype(BF16), keys)
            grads.append(grad_q)
            sums.append(key_sum)
        low = half_mask(0)
        grad_q = jnp.where(low, grads[0], grads[1]) * SCALE
        key_sum = jnp.where(low, sums[0], sums[1]) * SCALE
        special = iota((rows, PAIR), 0) % UPPER == offsets[:, lanes]
        dq_ref[:, lanes] = jnp.where(special, 0.0, grad_q)
        for slot, array in enumerate((grad_q, key_sum)):
            kept = jnp.where(special, array, 0.0).reshape(spec_rows, UPPER, PAIR).sum(axis=1)
            spec_ref[slot * spec_rows : (slot + 1) * spec_rows, lanes] = kept


def key_kernel(near_count, off_ref, k_ref, v_ref, *refs):
    q_refs, g_refs = refs[:GROUP], refs[GROUP : 2 * GROUP]
    near_refs = refs[2 * GROUP : 2 * GROUP + near_count]
    pay_refs = refs[2 * GROUP + near_count : -2]
    dk_ref, dv_ref = refs[-2:]
    rows, width = k_ref.shape
    heads = width // HD
    near_rows = rows // MIDDLE
    if near_count:
        far_stats = jnp.concatenate(
            [r[:, rows : rows + near_rows] for r in pay_refs[GROUP:]], axis=1
        )
    for pair in range(heads // 2):
        lanes = slice(pair * PAIR, (pair + 1) * PAIR)
        key_grads, value_grads = [], []
        for head in (2 * pair, 2 * pair + 1):
            middle_offset = off_ref[head] % MIDDLE
            chosen = iota((rows, 1), 0) % MIDDLE == middle_offset
            weight = pair_weights(rows, middle_offset)
            keys = one_head(k_ref[:, lanes], head, SCALE)
            values = one_head(v_ref[:, lanes], head)
            grad_k = jnp.zeros((rows, PAIR), F32)
            grad_v = jnp.zeros((rows, PAIR), F32)
            special = iota((1, rows), 1) % UPPER == off_ref[head]
            for q_ref, g_ref, pay_ref in zip(q_refs, g_refs, pay_refs):
                log_sum = jnp.where(special, HIGH, pay_ref[head : head + 1, :rows])
                dot = pay_ref[heads + head : heads + head + 1, :rows]
                queries, grads = q_ref[:, lanes], g_ref[:, lanes]
                probs = jnp.exp(dot_nt(keys, queries) - log_sum) * weight
                inner = dot_nt(values, grads) - dot
                grad_v = grad_v + dot_nn(probs.astype(BF16), grads)
                grad_k = grad_k + dot_nn((probs * inner).astype(BF16), queries)
            if near_count:
                queries = near_part(near_refs, 2, lanes)
                grads = near_part(near_refs, 3, lanes)
                count = near_count * near_rows
                special = iota((1, count), 1) % (UPPER // MIDDLE) == off_ref[head] // MIDDLE
                log_sum = jnp.where(special, HIGH, far_stats[head : head + 1, :])
                dot = far_stats[heads + head : heads + head + 1, :]
                scores = jnp.where(chosen, dot_nt(keys, queries), LOW)
                probs = jnp.exp(scores - log_sum)
                inner = dot_nt(values, grads) - dot
                grad_v = grad_v + dot_nn(probs.astype(BF16), grads)
                grad_k = grad_k + dot_nn((probs * inner).astype(BF16), queries)
            key_grads.append(grad_k)
            value_grads.append(grad_v)
        low = half_mask(0)
        dk_ref[:, lanes] = jnp.where(low, key_grads[0], key_grads[1]) * SCALE
        dv_ref[:, lanes] = jnp.where(low, value_grads[0], value_grads[1])


def collect_kernel(tok_rows, *refs):
    pay_refs, out_ref = refs[:-1], refs[-1]
    spec_rows = tok_rows // UPPER
    base = tok_rows + PAIR
    count = spec_rows * len(pay_refs)
    for kind in range(5):
        lines = [r[kind * spec_rows : (kind + 1) * spec_rows, base:] for r in pay_refs]
        out_ref[kind * count : (kind + 1) * count, :] = jnp.concatenate(lines, axis=0).astype(BF16)


def special_kernel(
    slots, off_ref, k_ref, v_ref, dq_in, spec_ref, dk_in, dv_in, *refs
):
    blocks = refs[:-3]
    dq_ref, dk_ref, dv_ref = refs[-3:]
    rows, width = k_ref.shape
    heads = width // HD
    spec_rows = rows // UPPER
    count = slots * spec_rows
    every = count * len(blocks)
    offsets = lane_offsets(off_ref, heads, width)

    def kind(index, lanes):
        return jnp.concatenate(
            [b[index * count : (index + 1) * count, lanes] for b in blocks], axis=0
        )

    column = iota((1, every), 1)
    same_group = jnp.where(column < GROUP * spec_rows, 1.0, 0.0)
    same_segment = jnp.where(column < count, 1.0, 0.0)
    row = iota((rows, 1), 0)
    low = half_mask(0)
    for pair in range(heads // 2):
        lanes = slice(pair * PAIR, (pair + 1) * PAIR)
        all_q, all_k, all_v, all_g, all_s = [kind(index, lanes) for index in range(5)]
        key_grads, value_grads, query_rows = [], [], []
        for head in (2 * pair, 2 * pair + 1):
            query = one_head(all_q, head, SCALE)
            grad = one_head(all_g, head)
            place = iota((1, PAIR), 1) - head % 2 * HD
            sum_place = jnp.where((place >= 0) & (place < 3), 1.0, 0.0)
            dot_place = jnp.where((place >= 3) & (place < 6), 1.0, 0.0)
            picks = jnp.where(iota((STAT_ROWS, PAIR), 0) == 0, sum_place, dot_place).astype(BF16)
            known = dot_nt(picks, all_s)
            scores = dot_nt(all_k, query)
            inner = dot_nt(all_v, grad)
            top = jnp.max(scores, axis=0, keepdims=True)
            weights = jnp.exp(scores - top)
            total = jnp.sum(weights, axis=0, keepdims=True)
            product = jnp.sum(weights * inner, axis=0, keepdims=True) / total
            log_sum = top + jnp.log(total)
            most = jnp.maximum(known[0:1], log_sum)
            joint = most + jnp.log(jnp.exp(known[0:1] - most) + jnp.exp(log_sum - most))
            dot = known[1:2] * jnp.exp(known[0:1] - joint) + product * jnp.exp(log_sum - joint)
            keys = one_head(k_ref[:, lanes], head, SCALE)
            values = one_head(v_ref[:, lanes], head)
            middle = jnp.where(row % MIDDLE == off_ref[head] % MIDDLE, 1.0, 0.0)
            upper = jnp.where(row % UPPER == off_ref[head], 1.0, 0.0)
            weight = same_group + middle * same_segment + upper
            scores = jnp.where(weight > 0.0, dot_nt(keys, all_q), LOW)
            probs = jnp.exp(scores - joint) * weight
            inner = dot_nt(values, all_g) - dot
            value_grads.append(dot_nn(probs.astype(BF16), all_g))
            key_grads.append(dot_nn((probs * inner).astype(BF16), all_q))
            stats = all_s[:count].astype(F32)
            known_sum = jnp.sum(stats * sum_place, axis=1, keepdims=True)
            known_dot = jnp.sum(stats * dot_place, axis=1, keepdims=True)
            scores = dot_nt(query[:count], all_k)
            inner = dot_nt(grad[:count], all_v)
            top = jnp.max(scores, axis=1, keepdims=True)
            weights = jnp.exp(scores - top)
            total = jnp.sum(weights, axis=1, keepdims=True)
            product = jnp.sum(weights * inner, axis=1, keepdims=True) / total
            log_sum = top + jnp.log(total)
            most = jnp.maximum(known_sum, log_sum)
            joint = most + jnp.log(jnp.exp(known_sum - most) + jnp.exp(log_sum - most))
            share = jnp.exp(known_sum - joint)
            dot = known_dot * share + product * jnp.exp(log_sum - joint)
            probs = jnp.exp(scores - joint)
            grad_q = dot_nn((probs * (inner - dot)).astype(BF16), all_k) * SCALE
            near_q = spec_ref[:spec_rows, lanes]
            key_sum = spec_ref[spec_rows : 2 * spec_rows, lanes]
            share, change = share[:spec_rows], (known_dot - dot)[:spec_rows]
            query_rows.append(share * (near_q + change * key_sum) + grad_q[:spec_rows])
        dk_ref[:, lanes] = (
            dk_in[:, lanes] + jnp.where(low, key_grads[0], key_grads[1]) * SCALE
        ).astype(BF16)
        dv_ref[:, lanes] = (
            dv_in[:, lanes] + jnp.where(low, value_grads[0], value_grads[1])
        ).astype(BF16)
        lines = jnp.where(low, query_rows[0], query_rows[1])
        spread = jnp.concatenate(
            [
                jnp.broadcast_to(lines[index : index + 1], (UPPER, PAIR))
                for index in range(spec_rows)
            ],
            axis=0,
        )
        special = row % UPPER == offsets[:, lanes]
        dq_ref[:, lanes] = (dq_in[:, lanes] + jnp.where(special, spread, 0.0)).astype(BF16)


def call(kernel, outs, *arrays, flops=0):
    smem = pl.BlockSpec(memory_space=pltpu.SMEM)
    vmem = pl.BlockSpec(memory_space=pltpu.VMEM)
    specs = [smem if a.dtype == jnp.int32 else vmem for a in arrays]
    return pl.pallas_call(
        kernel,
        out_shape=tuple(jax.ShapeDtypeStruct(shape, dtype) for shape, dtype in outs),
        in_specs=specs,
        out_specs=tuple(vmem for _ in outs),
        compiler_params=pltpu.CompilerParams(vmem_limit_bytes=48 * 1024 * 1024),
    )(*arrays)


def across(value, axis, mask):
    size = lax.axis_size(axis)
    return lax.ppermute(value, axis, [(source, source ^ mask) for source in range(size)])


def local(queries, key_matrix, value_matrix, grad_out, offsets):
    rows, width = queries.shape
    slots, outer = lax.axis_size("ctxb"), lax.axis_size("ctxa")
    near_count = slots - GROUP
    spec_rows = rows // UPPER

    def group(array):
        beside = across(array, "ctxb", 2)
        return [array, across(array, "ctxb", 1), beside, across(beside, "ctxb", 1)]

    k_parts, v_parts = group(key_matrix), group(value_matrix)
    near, spec = call(
        pack_kernel,
        [((4 * (rows // MIDDLE), width), BF16), ((4 * spec_rows, width), F32)],
        offsets, queries, key_matrix, value_matrix, grad_out,
    )
    near_parts = []
    for mask in range(GROUP, slots, 2):
        came = across(near, "ctxb", mask)
        near_parts += [came, across(came, "ctxb", 1)]
    q_parts, g_parts = group(queries), group(grad_out)
    (pay,) = call(
        partial(forward_kernel, near_count),
        [((STAT_ROWS, rows + PAIR + width), F32)],
        offsets, queries, grad_out, spec, *k_parts, *v_parts, *near_parts,
    )
    pays = []
    for mask in range(0, slots, 2):
        came = pay if mask == 0 else across(pay, "ctxb", mask)
        pays += [came, across(came, "ctxb", 1)]
    dq, dq_spec = call(
        partial(query_kernel, near_count),
        [((rows, width), F32), ((2 * spec_rows, width), F32)],
        offsets, queries, grad_out, pay, *k_parts, *v_parts, *near_parts,
    )
    (block,) = call(
        partial(collect_kernel, rows), [((5 * slots * spec_rows, width), BF16)], *pays
    )
    blocks = [block] + [across(block, "ctxa", mask) for mask in range(1, outer)]
    dk, dv = call(
        partial(key_kernel, near_count),
        [((rows, width), F32), ((rows, width), F32)],
        offsets, key_matrix, value_matrix, *q_parts, *g_parts, *near_parts, *pays,
    )
    return call(
        partial(special_kernel, slots),
        [((rows, width), BF16)] * 3,
        offsets, key_matrix, value_matrix, dq, dq_spec, dk, dv, *blocks,
    )


def solution(mesh):
    split = P(("ctxa", "ctxb"), None)
    return jax.shard_map(
        local,
        mesh=mesh,
        in_specs=(split, split, split, split, P()),
        out_specs=(split, split, split),
        check_vma=False,
    )
```

time: 637 us -> 69.8 us (0.11); the launches traced: 630 us -> 69.5 us
  blocking collectives: 332 us -> 0 us
  matrix products: 126 us -> 0 us
  local copies, waits for them, and re-layouts: 111 us -> 3.44 us
  other arithmetic: 40.4 us -> 0 us
  Pallas kernels: 0 us -> 25.3 us
  starting transfers between devices: 0.6 us -> 20.6 us
    all_gather x12 -> x0, blocking collectives: 332 us -> none  [the longest x2 83.1 us: from_everyone(): lax.all_gather(second_part, ('ctxa', 'ctxb'), axis=1, tiled=True)]
    dot_general x126 -> x0, matrix products: 126 us -> none  [the longest x30 31.6 us: level_backward(): jnp.einsum('sle,sie->sli', query_matrix, key_matrix, preferred_element_ty...]
    pallas_call x0 -> x6, Pallas kernels: none -> 25.3 us  [call(): pl.pallas_call(kernel, out_shape=tuple((jax.ShapeDtypeStruct(shape, dtype...]
    ppermute x4 -> x26, starting transfers between devices: 0.6 us -> 20.6 us  [across(): lax.ppermute(value, axis, [(source, source ^ mask) for source in range(si...]
    reduce_sum x26 -> x0, other arithmetic: 15.7 us -> none  [the longest x4 4.41 us: collect_scalar(): return jnp.sum(jnp.where(level_mask[:, None, :], shaped, 0.0), axis=2)]
    sub x18 -> x0, local copies, waits for them, and re-layouts: 15.4 us -> none  [level_backward(): probs = jnp.exp(attention_logits - log_sum[..., None])]
    broadcast_in_dim x14 -> x0, local copies, waits for them, and re-layouts: 13.3 us -> none  [the longest x4 7.32 us: place_rows(): jnp.where(level_mask.T[None, :, :, None], jnp.transpose(rows, (1, 0, 2))[...]
    dynamic_slice x18 -> x0, local copies, waits for them, and re-layouts: 12.4 us -> none  [by_heads(): results = lax.map(lambda grouped: kernel(*grouped), stacked)]
  transfers between devices with their start and end apart: 4 -> 26, of which waited for: 1 -> 8; matrix products, arithmetic and copies ran while one was open for 11% -> 0% of each run, Pallas kernels for 0% -> 27%
where the time goes in v1:
time: 69.8 us; the launch traced here: 69.5 us
  Pallas kernels  25.3 us (36%)
  starting transfers between devices  20.6 us (30%)
  waiting for transfers between devices  19.3 us (28%)
  local copies, waits for them, and re-layouts  3.44 us (5%)
  between operations  0.76 us (1%)
    pallas_call x6, Pallas kernels, call(): pl.pallas_call(kernel, out_shape=tuple((jax.ShapeDtypeStruct(shape, dtype...  25.3 us
    ppermute x26, starting transfers between devices, across(): lax.ppermute(value, axis, [(source, source ^ mask) for source in range(si...  20.6 us
    ppermute x26, waiting for transfers between devices, across(): lax.ppermute(value, axis, [(source, source ^ mask) for source in range(si...  19.3 us
    unnamed x12, local copies, waits for them, and re-layouts  3.44 us
  transfers between devices with their start and end apart: 26, of which 8 were waited for; matrix products, arithmetic and copies ran while one was open for 0% of the time, Pallas kernels for 27%

profile of v1, /device:TPU:0, one launch (start us, length us, event | category | flops | bytes accessed | tf_op | source)
XLA Modules:
  0.0 69.5 jit_solution(14159442948567412886)
XLA Ops:
  0.6 0.9 %copy-done = bf16[256,384]{1,0:T(8,128)(2,1)S(1)} copy-done((bf16[256,384]{1,0:T(8,128)(2,1)S(1)}, bf16[256,384]{1,0:T(8,128)(2,1)}, u32[]{:S(2)}) %copy-start) | copy-done | bytes 196632
  1.6 0.9 %copy-done.2 = bf16[256,384]{1,0:T(8,128)(2,1)S(1)} copy-done((bf16[256,384]{1,0:T(8,128)(2,1)S(1)}, bf16[256,384]{1,0:T(8,128)(2,1)}, u32[]{:S(2)}) %copy-start.2) | copy-done | bytes 196632
  2.5 0.9 %copy-done.4 = bf16[256,384]{1,0:T(8,128)(2,1)S(1)} copy-done((bf16[256,384]{1,0:T(8,128)(2,1)S(1)}, bf16[256,384]{1,0:T(8,128)(2,1)}, u32[]{:S(2)}) %copy-start.4) | copy-done | bytes 196632
  3.4 0.7 copy-done.5
  4.1 1.8 %shard_map.76 = (bf16[128,384]{1,0:T(8,128)(2,1)S(1)}, f32[8,384]{1,0:T(8,128)S(1)}) custom-call(s32[6]{0:T(128)S(1)} %copy-done.5, bf16[256,384]{1,0:T(8,128)(2,1)} %refs_0_.5, bf16[256,384]{1,0:T(8,128)(2,1)S(1)} %copy-done, bf16[256,384]{1,0:T(8,128)(2,1)S(1)} %copy-done.2, bf16[256,384]{1,0:T(8,128)(2,1)S(1)} %copy-done.4), custom_call_target="tpu_custom_call" | custom-call | tf_op jit(solution)/shard_map/pallas_call | solution.py:365
  5.9 4.1 %collective-permute-start.6 = (bf16[128,384]{1,0:T(8,128)(2,1)S(1)}, bf16[128,384]{1,0:T(8,128)(2,1)S(1)}, u32[]{:S(2)}, u32[]{:S(2)}) collective-permute-start(bf16[128,384]{1,0:T(8,128)(2,1)S(1)} %get-tuple-element.10), channel_id=1, source_target_pairs={{0,4},{1,5},{2,6},{3,7},{4,0},{5,1},{6,2},{7,3},{8,12},{9,13},{10,... | collective-permute-start | bytes 294920 | tf_op jit(solution)/shard_map/ppermute | solution.py:376
  10.0 1.6 %collective-permute-start.1 = (bf16[256,384]{1,0:T(8,128)(2,1)S(1)}, bf16[256,384]{1,0:T(8,128)(2,1)S(1)}, u32[]{:S(2)}, u32[]{:S(2)}) collective-permute-start(bf16[256,384]{1,0:T(8,128)(2,1)S(1)} %copy-done), channel_id=1, source_target_pairs={{0,2},{1,3},{2,0},{3,1},{4,6},{5,7},{6,4},{7,5},{8,10},{9,11},{10,... | collective-permute-start | bytes 589832 | tf_op jit(solution)/shard_map/ppermute | solution.py:376
  11.6 0.4 collective-permute-start.4
  12.0 0.5 collective-permute-start.3
  12.5 2.3 %collective-permute-done.6.refs_8_ = bf16[128,384]{1,0:T(8,128)(2,1)S(1)} collective-permute-done((bf16[128,384]{1,0:T(8,128)(2,1)S(1)}, bf16[128,384]{1,0:T(8,128)(2,1)S(1)}, u32[]{:S(2)}, u32[]{:S(2)}) %collective-permute-start.6) | collective-permute-done | bytes 98336 | tf_op jit(solution)/shard_map/ppermute | solution.py:376
  14.8 3.8 %collective-permute-start.8 = (bf16[128,384]{1,0:T(8,128)(2,1)S(1)}, bf16[128,384]{1,0:T(8,128)(2,1)S(1)}, u32[]{:S(2)}, u32[]{:S(2)}) collective-permute-start(bf16[128,384]{1,0:T(8,128)(2,1)S(1)} %get-tuple-element.10), channel_id=1, source_target_pairs={{0,6},{1,7},{2,4},{3,5},{4,2},{5,3},{6,0},{7,1},{8,14},{9,15},{10,... | collective-permute-start | bytes 294920 | tf_op jit(solution)/shard_map/ppermute | solution.py:376
  18.5 5.9 %collective-permute-done.8.refs_10_ = bf16[128,384]{1,0:T(8,128)(2,1)S(1)} collective-permute-done((bf16[128,384]{1,0:T(8,128)(2,1)S(1)}, bf16[128,384]{1,0:T(8,128)(2,1)S(1)}, u32[]{:S(2)}, u32[]{:S(2)}) %collective-permute-start.8) | collective-permute-done | bytes 98336 | tf_op jit(solution)/shard_map/ppermute | solution.py:376
  24.4 0.5 collective-permute-start.2
  25.0 2.0 %collective-permute-start.14 = (bf16[256,384]{1,0:T(8,128)(2,1)S(1)}, bf16[256,384]{1,0:T(8,128)(2,1)S(1)}, u32[]{:S(2)}, u32[]{:S(2)}) collective-permute-start(bf16[256,384]{1,0:T(8,128)(2,1)S(1)} %copy-done.4), channel_id=1, source_target_pairs={{0,2},{1,3},{2,0},{3,1},{4,6},{5,7},{6,4},{7,5},{8,10},{9,11},{10,... | collective-permute-start | bytes 589832 | tf_op jit(solution)/shard_map/ppermute | solution.py:376
  27.1 1.3 %collective-permute-done.9.refs_11_ = bf16[128,384]{1,0:T(8,128)(2,1)S(1)} collective-permute-done((bf16[128,384]{1,0:T(8,128)(2,1)S(1)}, bf16[128,384]{1,0:T(8,128)(2,1)S(1)}, u32[]{:S(2)}, u32[]{:S(2)}) %collective-permute-start.9) | collective-permute-done | bytes 98336 | tf_op jit(solution)/shard_map/ppermute | solution.py:376
  28.4 4.7 %shard_map.77.pay_ref.refs_12_.refs_0_ = f32[16,768]{1,0:T(8,128)S(1)} custom-call(s32[6]{0:T(128)S(1)} %copy-done.5, bf16[256,384]{1,0:T(8,128)(2,1)} %refs_0_.5, bf16[256,384]{1,0:T(8,128)(2,1)S(1)} %copy-done.4, f32[8,384]{1,0:T(8,128)S(1)} %get-tuple-element.9.spec_ref, bf16[256,384]{1,0:T(8,128)(2,1)S(1)} %copy-done, ...), custom_call_target="tpu_custom_call" | custom-call | tf_op jit(solution)/shard_map/pallas_call | solution.py:365
  33.4 0.3 collective-permute-start.10
  33.6 0.3 collective-permute-start.13
  33.9 3.2 %collective-permute-done.14.refs_6_ = bf16[256,384]{1,0:T(8,128)(2,1)S(1)} collective-permute-done((bf16[256,384]{1,0:T(8,128)(2,1)S(1)}, bf16[256,384]{1,0:T(8,128)(2,1)S(1)}, u32[]{:S(2)}, u32[]{:S(2)}) %collective-permute-start.14) | collective-permute-done | bytes 196640 | tf_op jit(solution)/shard_map/ppermute | solution.py:376
  37.1 1.2 %collective-permute-start.19 = (f32[16,768]{1,0:T(8,128)S(1)}, f32[16,768]{1,0:T(8,128)S(1)}, u32[]{:S(2)}, u32[]{:S(2)}) collective-permute-start(f32[16,768]{1,0:T(8,128)S(1)} %shard_map.77.pay_ref.refs_12_.refs_0_), channel_id=1, source_target_pairs={{0,4},{1,5},{2,6},{3,7},{4,0},{5,1},{6,2},{7,3},{8,12},{9,13},{10,... | collective-permute-start | bytes 147464 | tf_op jit(solution)/shard_map/ppermute | solution.py:376
  38.3 1.3 %collective-permute-start.21 = (f32[16,768]{1,0:T(8,128)S(1)}, f32[16,768]{1,0:T(8,128)S(1)}, u32[]{:S(2)}, u32[]{:S(2)}) collective-permute-start(f32[16,768]{1,0:T(8,128)S(1)} %shard_map.77.pay_ref.refs_12_.refs_0_), channel_id=1, source_target_pairs={{0,6},{1,7},{2,4},{3,5},{4,2},{5,3},{6,0},{7,1},{8,14},{9,15},{10,... | collective-permute-start | bytes 147464 | tf_op jit(solution)/shard_map/ppermute | solution.py:376
  39.6 3.6 %collective-permute-done.19.refs_16_.refs_4_ = f32[16,768]{1,0:T(8,128)S(1)} collective-permute-done((f32[16,768]{1,0:T(8,128)S(1)}, f32[16,768]{1,0:T(8,128)S(1)}, u32[]{:S(2)}, u32[]{:S(2)}) %collective-permute-start.19) | collective-permute-done | bytes 49184 | tf_op jit(solution)/shard_map/ppermute | solution.py:376
  43.2 1.0 %collective-permute-done.21.refs_18_.refs_6_ = f32[16,768]{1,0:T(8,128)S(1)} collective-permute-done((f32[16,768]{1,0:T(8,128)S(1)}, f32[16,768]{1,0:T(8,128)S(1)}, u32[]{:S(2)}, u32[]{:S(2)}) %collective-permute-start.21) | collective-permute-done | bytes 49184 | tf_op jit(solution)/shard_map/ppermute | solution.py:376
  44.3 0.5 collective-permute-start.20
  44.8 1.0 %collective-permute-done.20.refs_17_.refs_5_ = f32[16,768]{1,0:T(8,128)S(1)} collective-permute-done((f32[16,768]{1,0:T(8,128)S(1)}, f32[16,768]{1,0:T(8,128)S(1)}, u32[]{:S(2)}, u32[]{:S(2)}) %collective-permute-start.20) | collective-permute-done | bytes 49184 | tf_op jit(solution)/shard_map/ppermute | solution.py:376
  46.0 1.0 %collective-permute-done.22.refs_19_.refs_7_ = f32[16,768]{1,0:T(8,128)S(1)} collective-permute-done((f32[16,768]{1,0:T(8,128)S(1)}, f32[16,768]{1,0:T(8,128)S(1)}, u32[]{:S(2)}, u32[]{:S(2)}) %collective-permute-start.22) | collective-permute-done | bytes 49184 | tf_op jit(solution)/shard_map/ppermute | solution.py:376
  47.1 1.6 %collective-permute-start.23 = (bf16[80,384]{1,0:T(8,128)(2,1)S(1)}, bf16[80,384]{1,0:T(8,128)(2,1)S(1)}, u32[]{:S(2)}, u32[]{:S(2)}) collective-permute-start(bf16[80,384]{1,0:T(8,128)(2,1)S(1)} %shard_map.80.refs_0_), channel_id=1, source_target_pairs={{0,8},{8,0},{16,24},{24,16},{1,9},{9,1},{17,25},{25,17},{2,10},{10... | collective-permute-start | bytes 184328 | tf_op jit(solution)/shard_map/ppermute | solution.py:376
  48.6 1.5 %collective-permute-start.24 = (bf16[80,384]{1,0:T(8,128)(2,1)S(1)}, bf16[80,384]{1,0:T(8,128)(2,1)S(1)}, u32[]{:S(2)}, u32[]{:S(2)}) collective-permute-start(bf16[80,384]{1,0:T(8,128)(2,1)S(1)} %shard_map.80.refs_0_), channel_id=1, source_target_pairs={{0,16},{8,24},{16,0},{24,8},{1,17},{9,25},{17,1},{25,9},{2,18},{10... | collective-permute-start | bytes 184328 | tf_op jit(solution)/shard_map/ppermute | solution.py:376
  50.1 0.5 collective-permute-start.25
  50.6 7.1 %shard_map.78 = (f32[256,384]{1,0:T(8,128)S(1)}, f32[4,384]{1,0:T(4,128)S(1)}) custom-call(s32[6]{0:T(128)S(1)} %copy-done.5, bf16[256,384]{1,0:T(8,128)(2,1)} %refs_0_.5, bf16[256,384]{1,0:T(8,128)(2,1)S(1)} %copy-done.4, f32[16,768]{1,0:T(8,128)S(1)} %shard_map.77.pay_ref.refs_12_.refs_0_, bf16[256,384]{1,0:T(8,128)(2,1)S(1)} %copy-done.1, ...), custom_call_target="tpu_custom_call" | custom-call | tf_op jit(solution)/shard_map/pallas_call | solution.py:365
  57.8 7.1 %shard_map.79 = (f32[256,384]{1,0:T(8,128)S(1)}, f32[256,384]{1,0:T(8,128)S(1)}) custom-call(s32[6]{0:T(128)S(1)} %copy-done.5, bf16[256,384]{1,0:T(8,128)(2,1)S(1)} %copy-done.1, bf16[256,384]{1,0:T(8,128)(2,1)S(1)} %copy-done.3, bf16[256,384]{1,0:T(8,128)(2,1)} %refs_0_.5, bf16[256,384]{1,0:T(8,128)(2,1)S(1)} %collective-permute-done.10.refs_1_, ...), custom_call_target="tpu_custom_call" | custom-call | tf_op jit(solution)/shard_map/pallas_call | solution.py:365
  64.9 4.6 %shard_map.81 = (bf16[256,384]{1,0:T(8,128)(2,1)}, bf16[256,384]{1,0:T(8,128)(2,1)}, bf16[256,384]{1,0:T(8,128)(2,1)}) custom-call(s32[6]{0:T(128)S(1)} %copy-done.5, bf16[256,384]{1,0:T(8,128)(2,1)S(1)} %copy-done.1, bf16[256,384]{1,0:T(8,128)(2,1)S(1)} %copy-done.3, f32[256,384]{1,0:T(8,128)S(1)} %get-tuple-element.11.dq_in, ...), custom_call_target="tpu_custom_call" | custom-call | tf_op jit(solution)/shard_map/pallas_call | solution.py:365
  (38 shorter events, 0.8 us)
Async XLA Ops:
  0.6 0.9 %copy-start = (bf16[256,384]{1,0:T(8,128)(2,1)S(1)}, bf16[256,384]{1,0:T(8,128)(2,1)}, u32[]{:S(2)}) copy-start(bf16[256,384]{1,0:T(8,128)(2,1)} %k_ref.5) | copy-start | bytes 589828
  1.6 0.9 %copy-start.2 = (bf16[256,384]{1,0:T(8,128)(2,1)S(1)}, bf16[256,384]{1,0:T(8,128)(2,1)}, u32[]{:S(2)}) copy-start(bf16[256,384]{1,0:T(8,128)(2,1)} %v_ref.5) | copy-start | bytes 589828
  2.5 0.9 %copy-start.4 = (bf16[256,384]{1,0:T(8,128)(2,1)S(1)}, bf16[256,384]{1,0:T(8,128)(2,1)}, u32[]{:S(2)}) copy-start(bf16[256,384]{1,0:T(8,128)(2,1)} %refs_4_.5) | copy-start | bytes 589828
  3.4 0.7 copy-start.5
  5.9 8.9 %collective-permute-start.6 = (bf16[128,384]{1,0:T(8,128)(2,1)S(1)}, bf16[128,384]{1,0:T(8,128)(2,1)S(1)}, u32[]{:S(2)}, u32[]{:S(2)}) collective-permute-start(bf16[128,384]{1,0:T(8,128)(2,1)S(1)} %get-tuple-element.10), channel_id=1, source_target_pairs={{0,4},{1,5},{2,6},{3,7},{4,0},{5,1},{6,2},{7,3},{8,12},{9,13},{10,... | collective-permute-start | bytes 294920 | tf_op jit(solution)/shard_map/ppermute | solution.py:376
  10.0 14.4 %collective-permute-start.1 = (bf16[256,384]{1,0:T(8,128)(2,1)S(1)}, bf16[256,384]{1,0:T(8,128)(2,1)S(1)}, u32[]{:S(2)}, u32[]{:S(2)}) collective-permute-start(bf16[256,384]{1,0:T(8,128)(2,1)S(1)} %copy-done), channel_id=1, source_target_pairs={{0,2},{1,3},{2,0},{3,1},{4,6},{5,7},{6,4},{7,5},{8,10},{9,11},{10,... | collective-permute-start | bytes 589832 | tf_op jit(solution)/shard_map/ppermute | solution.py:376
  11.6 13.4 %collective-permute-start.4 = (bf16[256,384]{1,0:T(8,128)(2,1)S(1)}, bf16[256,384]{1,0:T(8,128)(2,1)S(1)}, u32[]{:S(2)}, u32[]{:S(2)}) collective-permute-start(bf16[256,384]{1,0:T(8,128)(2,1)S(1)} %copy-done.2), channel_id=1, source_target_pairs={{0,2},{1,3},{2,0},{3,1},{4,6},{5,7},{6,4},{7,5},{8,10},{9,11},{10,... | collective-permute-start | bytes 589832 | tf_op jit(solution)/shard_map/ppermute | solution.py:376
  12.0 13.0 %collective-permute-start = (bf16[256,384]{1,0:T(8,128)(2,1)S(1)}, bf16[256,384]{1,0:T(8,128)(2,1)S(1)}, u32[]{:S(2)}, u32[]{:S(2)}) collective-permute-start(bf16[256,384]{1,0:T(8,128)(2,1)S(1)} %copy-done), channel_id=1, source_target_pairs={{0,1},{1,0},{2,3},{3,2},{4,5},{5,4},{6,7},{7,6},{8,9},{9,8},{10,11... | collective-permute-start | bytes 589832 | tf_op jit(solution)/shard_map/ppermute | solution.py:376
  12.0 13.0 %collective-permute-start.3 = (bf16[256,384]{1,0:T(8,128)(2,1)S(1)}, bf16[256,384]{1,0:T(8,128)(2,1)S(1)}, u32[]{:S(2)}, u32[]{:S(2)}) collective-permute-start(bf16[256,384]{1,0:T(8,128)(2,1)S(1)} %copy-done.2), channel_id=1, source_target_pairs={{0,1},{1,0},{2,3},{3,2},{4,5},{5,4},{6,7},{7,6},{8,9},{9,8},{10,11... | collective-permute-start | bytes 589832 | tf_op jit(solution)/shard_map/ppermute | solution.py:376
  14.8 9.6 %collective-permute-start.8 = (bf16[128,384]{1,0:T(8,128)(2,1)S(1)}, bf16[128,384]{1,0:T(8,128)(2,1)S(1)}, u32[]{:S(2)}, u32[]{:S(2)}) collective-permute-start(bf16[128,384]{1,0:T(8,128)(2,1)S(1)} %get-tuple-element.10), channel_id=1, source_target_pairs={{0,6},{1,7},{2,4},{3,5},{4,2},{5,3},{6,0},{7,1},{8,14},{9,15},{10,... | collective-permute-start | bytes 294920 | tf_op jit(solution)/shard_map/ppermute | solution.py:376
  24.4 2.6 %collective-permute-start.7 = (bf16[128,384]{1,0:T(8,128)(2,1)S(1)}, bf16[128,384]{1,0:T(8,128)(2,1)S(1)}, u32[]{:S(2)}, u32[]{:S(2)}) collective-permute-start(bf16[128,384]{1,0:T(8,128)(2,1)S(1)} %collective-permute-done.6.refs_8_), channel_id=1, source_target_pairs={{0,1},{1,0},{2,3},{3,2},{4,5},{5,4},{6,7},{7,6},{8,9},{9,8},{10,11... | collective-permute-start | bytes 294920 | tf_op jit(solution)/shard_map/ppermute | solution.py:376
  24.4 3.9 %collective-permute-start.2 = (bf16[256,384]{1,0:T(8,128)(2,1)S(1)}, bf16[256,384]{1,0:T(8,128)(2,1)S(1)}, u32[]{:S(2)}, u32[]{:S(2)}) collective-permute-start(bf16[256,384]{1,0:T(8,128)(2,1)S(1)} %collective-permute-done.1.refs_2_), channel_id=1, source_target_pairs={{0,1},{1,0},{2,3},{3,2},{4,5},{5,4},{6,7},{7,6},{8,9},{9,8},{10,11... | collective-permute-start | bytes 589832 | tf_op jit(solution)/shard_map/ppermute | solution.py:376
  24.9 3.4 %collective-permute-start.5 = (bf16[256,384]{1,0:T(8,128)(2,1)S(1)}, bf16[256,384]{1,0:T(8,128)(2,1)S(1)}, u32[]{:S(2)}, u32[]{:S(2)}) collective-permute-start(bf16[256,384]{1,0:T(8,128)(2,1)S(1)} %collective-permute-done.4.refs_6_), channel_id=1, source_target_pairs={{0,1},{1,0},{2,3},{3,2},{4,5},{5,4},{6,7},{7,6},{8,9},{9,8},{10,11... | collective-permute-start | bytes 589832 | tf_op jit(solution)/shard_map/ppermute | solution.py:376
  25.0 8.6 %collective-permute-start.11 = (bf16[256,384]{1,0:T(8,128)(2,1)}, bf16[256,384]{1,0:T(8,128)(2,1)S(1)}, u32[]{:S(2)}, u32[]{:S(2)}) collective-permute-start(bf16[256,384]{1,0:T(8,128)(2,1)} %refs_0_.5), channel_id=1, source_target_pairs={{0,2},{1,3},{2,0},{3,1},{4,6},{5,7},{6,4},{7,5},{8,10},{9,11},{10,... | collective-permute-start | bytes 589832 | tf_op jit(solution)/shard_map/ppermute | solution.py:376
  25.0 12.0 %collective-permute-start.14 = (bf16[256,384]{1,0:T(8,128)(2,1)S(1)}, bf16[256,384]{1,0:T(8,128)(2,1)S(1)}, u32[]{:S(2)}, u32[]{:S(2)}) collective-permute-start(bf16[256,384]{1,0:T(8,128)(2,1)S(1)} %copy-done.4), channel_id=1, source_target_pairs={{0,2},{1,3},{2,0},{3,1},{4,6},{5,7},{6,4},{7,5},{8,10},{9,11},{10,... | collective-permute-start | bytes 589832 | tf_op jit(solution)/shard_map/ppermute | solution.py:376
  27.1 1.3 %collective-permute-start.9 = (bf16[128,384]{1,0:T(8,128)(2,1)S(1)}, bf16[128,384]{1,0:T(8,128)(2,1)S(1)}, u32[]{:S(2)}, u32[]{:S(2)}) collective-permute-start(bf16[128,384]{1,0:T(8,128)(2,1)S(1)} %collective-permute-done.8.refs_10_), channel_id=1, source_target_pairs={{0,1},{1,0},{2,3},{3,2},{4,5},{5,4},{6,7},{7,6},{8,9},{9,8},{10,11... | collective-permute-start | bytes 294920 | tf_op jit(solution)/shard_map/ppermute | solution.py:376
  33.0 17.6 %copy-start.1 = (bf16[256,384]{1,0:T(8,128)(2,1)S(1)}, bf16[256,384]{1,0:T(8,128)(2,1)}, u32[]{:S(2)}) copy-start(bf16[256,384]{1,0:T(8,128)(2,1)} %k_ref.5) | copy-start | bytes 589828
  33.0 17.6 %copy-start.3 = (bf16[256,384]{1,0:T(8,128)(2,1)S(1)}, bf16[256,384]{1,0:T(8,128)(2,1)}, u32[]{:S(2)}) copy-start(bf16[256,384]{1,0:T(8,128)(2,1)} %v_ref.5) | copy-start | bytes 589828
  33.1 5.2 %collective-permute-start.16 = (f32[16,768]{1,0:T(8,128)S(1)}, f32[16,768]{1,0:T(8,128)S(1)}, u32[]{:S(2)}, u32[]{:S(2)}) collective-permute-start(f32[16,768]{1,0:T(8,128)S(1)} %shard_map.77.pay_ref.refs_12_.refs_0_), channel_id=1, source_target_pairs={{0,1},{1,0},{2,3},{3,2},{4,5},{5,4},{6,7},{7,6},{8,9},{9,8},{10,11... | collective-permute-start | bytes 147464 | tf_op jit(solution)/shard_map/ppermute | solution.py:376
  33.3 6.3 %collective-permute-start.17 = (f32[16,768]{1,0:T(8,128)S(1)}, f32[16,768]{1,0:T(8,128)S(1)}, u32[]{:S(2)}, u32[]{:S(2)}) collective-permute-start(f32[16,768]{1,0:T(8,128)S(1)} %shard_map.77.pay_ref.refs_12_.refs_0_), channel_id=1, source_target_pairs={{0,2},{1,3},{2,0},{3,1},{4,6},{5,7},{6,4},{7,5},{8,10},{9,11},{10,... | collective-permute-start | bytes 147464 | tf_op jit(solution)/shard_map/ppermute | solution.py:376
  33.4 15.2 %collective-permute-start.10 = (bf16[256,384]{1,0:T(8,128)(2,1)}, bf16[256,384]{1,0:T(8,128)(2,1)S(1)}, u32[]{:S(2)}, u32[]{:S(2)}) collective-permute-start(bf16[256,384]{1,0:T(8,128)(2,1)} %refs_0_.5), channel_id=1, source_target_pairs={{0,1},{1,0},{2,3},{3,2},{4,5},{5,4},{6,7},{7,6},{8,9},{9,8},{10,11... | collective-permute-start | bytes 589832 | tf_op jit(solution)/shard_map/ppermute | solution.py:376
  33.6 16.5 %collective-permute-start.13 = (bf16[256,384]{1,0:T(8,128)(2,1)S(1)}, bf16[256,384]{1,0:T(8,128)(2,1)S(1)}, u32[]{:S(2)}, u32[]{:S(2)}) collective-permute-start(bf16[256,384]{1,0:T(8,128)(2,1)S(1)} %copy-done.4), channel_id=1, source_target_pairs={{0,1},{1,0},{2,3},{3,2},{4,5},{5,4},{6,7},{7,6},{8,9},{9,8},{10,11... | collective-permute-start | bytes 589832 | tf_op jit(solution)/shard_map/ppermute | solution.py:376
  37.1 6.2 %collective-permute-start.19 = (f32[16,768]{1,0:T(8,128)S(1)}, f32[16,768]{1,0:T(8,128)S(1)}, u32[]{:S(2)}, u32[]{:S(2)}) collective-permute-start(f32[16,768]{1,0:T(8,128)S(1)} %shard_map.77.pay_ref.refs_12_.refs_0_), channel_id=1, source_target_pairs={{0,4},{1,5},{2,6},{3,7},{4,0},{5,1},{6,2},{7,3},{8,12},{9,13},{10,... | collective-permute-start | bytes 147464 | tf_op jit(solution)/shard_map/ppermute | solution.py:376
  38.3 6.0 %collective-permute-start.21 = (f32[16,768]{1,0:T(8,128)S(1)}, f32[16,768]{1,0:T(8,128)S(1)}, u32[]{:S(2)}, u32[]{:S(2)}) collective-permute-start(f32[16,768]{1,0:T(8,128)S(1)} %shard_map.77.pay_ref.refs_12_.refs_0_), channel_id=1, source_target_pairs={{0,6},{1,7},{2,4},{3,5},{4,2},{5,3},{6,0},{7,1},{8,14},{9,15},{10,... | collective-permute-start | bytes 147464 | tf_op jit(solution)/shard_map/ppermute | solution.py:376
  39.6 4.7 %collective-permute-start.18 = (f32[16,768]{1,0:T(8,128)S(1)}, f32[16,768]{1,0:T(8,128)S(1)}, u32[]{:S(2)}, u32[]{:S(2)}) collective-permute-start(f32[16,768]{1,0:T(8,128)S(1)} %collective-permute-done.17.refs_14_.refs_2_), channel_id=1, source_target_pairs={{0,1},{1,0},{2,3},{3,2},{4,5},{5,4},{6,7},{7,6},{8,9},{9,8},{10,11... | collective-permute-start | bytes 147464 | tf_op jit(solution)/shard_map/ppermute | solution.py:376
  43.2 14.5 %collective-permute-start.12 = (bf16[256,384]{1,0:T(8,128)(2,1)S(1)}, bf16[256,384]{1,0:T(8,128)(2,1)S(1)}, u32[]{:S(2)}, u32[]{:S(2)}) collective-permute-start(bf16[256,384]{1,0:T(8,128)(2,1)S(1)} %collective-permute-done.11.refs_2_), channel_id=1, source_target_pairs={{0,1},{1,0},{2,3},{3,2},{4,5},{5,4},{6,7},{7,6},{8,9},{9,8},{10,11... | collective-permute-start | bytes 589832 | tf_op jit(solution)/shard_map/ppermute | solution.py:376
  44.3 13.5 %collective-permute-start.15 = (bf16[256,384]{1,0:T(8,128)(2,1)S(1)}, bf16[256,384]{1,0:T(8,128)(2,1)S(1)}, u32[]{:S(2)}, u32[]{:S(2)}) collective-permute-start(bf16[256,384]{1,0:T(8,128)(2,1)S(1)} %collective-permute-done.14.refs_6_), channel_id=1, source_target_pairs={{0,1},{1,0},{2,3},{3,2},{4,5},{5,4},{6,7},{7,6},{8,9},{9,8},{10,11... | collective-permute-start | bytes 589832 | tf_op jit(solution)/shard_map/ppermute | solution.py:376
  44.3 1.5 %collective-permute-start.20 = (f32[16,768]{1,0:T(8,128)S(1)}, f32[16,768]{1,0:T(8,128)S(1)}, u32[]{:S(2)}, u32[]{:S(2)}) collective-permute-start(f32[16,768]{1,0:T(8,128)S(1)} %collective-permute-done.19.refs_16_.refs_4_), channel_id=1, source_target_pairs={{0,1},{1,0},{2,3},{3,2},{4,5},{5,4},{6,7},{7,6},{8,9},{9,8},{10,11... | collective-permute-start | bytes 147464 | tf_op jit(solution)/shard_map/ppermute | solution.py:376
  45.8 1.2 %collective-permute-start.22 = (f32[16,768]{1,0:T(8,128)S(1)}, f32[16,768]{1,0:T(8,128)S(1)}, u32[]{:S(2)}, u32[]{:S(2)}) collective-permute-start(f32[16,768]{1,0:T(8,128)S(1)} %collective-permute-done.21.refs_18_.refs_6_), channel_id=1, source_target_pairs={{0,1},{1,0},{2,3},{3,2},{4,5},{5,4},{6,7},{7,6},{8,9},{9,8},{10,11... | collective-permute-start | bytes 147464 | tf_op jit(solution)/shard_map/ppermute | solution.py:376
  47.1 17.8 %collective-permute-start.23 = (bf16[80,384]{1,0:T(8,128)(2,1)S(1)}, bf16[80,384]{1,0:T(8,128)(2,1)S(1)}, u32[]{:S(2)}, u32[]{:S(2)}) collective-permute-start(bf16[80,384]{1,0:T(8,128)(2,1)S(1)} %shard_map.80.refs_0_), channel_id=1, source_target_pairs={{0,8},{8,0},{16,24},{24,16},{1,9},{9,1},{17,25},{25,17},{2,10},{10... | collective-permute-start | bytes 184328 | tf_op jit(solution)/shard_map/ppermute | solution.py:376
  48.6 16.3 %collective-permute-start.24 = (bf16[80,384]{1,0:T(8,128)(2,1)S(1)}, bf16[80,384]{1,0:T(8,128)(2,1)S(1)}, u32[]{:S(2)}, u32[]{:S(2)}) collective-permute-start(bf16[80,384]{1,0:T(8,128)(2,1)S(1)} %shard_map.80.refs_0_), channel_id=1, source_target_pairs={{0,16},{8,24},{16,0},{24,8},{1,17},{9,25},{17,1},{25,9},{2,18},{10... | collective-permute-start | bytes 184328 | tf_op jit(solution)/shard_map/ppermute | solution.py:376
  50.1 14.8 %collective-permute-start.25 = (bf16[80,384]{1,0:T(8,128)(2,1)S(1)}, bf16[80,384]{1,0:T(8,128)(2,1)S(1)}, u32[]{:S(2)}, u32[]{:S(2)}) collective-permute-start(bf16[80,384]{1,0:T(8,128)(2,1)S(1)} %shard_map.80.refs_0_), channel_id=1, source_target_pairs={{0,24},{8,16},{16,8},{24,0},{1,25},{9,17},{17,9},{25,1},{2,26},{10... | collective-permute-start | bytes 184328 | tf_op jit(solution)/shard_map/ppermute | solution.py:376

commit v2 on v1

v2 whole, which is shorter than its diff:
```python
from functools import partial

import jax
import jax.numpy as jnp
from jax import lax
from jax.experimental import pallas as pl
from jax.experimental.pallas import tpu as pltpu
from jax.sharding import PartitionSpec as P

HD = 64
PAIR = 2 * HD
GROUP = 4
MIDDLE = 8
UPPER = 128
LOW = -1e30
HIGH = 1e30
SCALE = HD**-0.5
F32 = jnp.float32
BF16 = jnp.bfloat16
STAT_ROWS = 16
SPEC_PAD = 16
KV_ARRAYS = 6


def iota(shape, dim):
    return lax.broadcasted_iota(jnp.int32, shape, dim)


def dot_nt(a, b):
    return lax.dot_general(a, b, (((1,), (1,)), ((), ())), preferred_element_type=F32)


def dot_nn(a, b):
    return jnp.dot(a, b, preferred_element_type=F32)


def pair_slice(head):
    low = head // 2 * PAIR
    return slice(low, low + PAIR)


def half_mask(head):
    return iota((1, PAIR), 1) // HD == head % 2


def one_head(block, head, scale=1.0):
    return jnp.where(half_mask(head), block.astype(F32) * scale, 0.0).astype(BF16)


def lane_offsets(off_ref, heads, width):
    lane_head = iota((1, width), 1) // HD
    out = jnp.zeros((1, width), jnp.int32)
    for head in range(heads):
        out = jnp.where(lane_head == head, off_ref[head], out)
    return out


def row_offsets(off_ref, heads):
    rows = iota((STAT_ROWS, 1), 0)
    out = jnp.zeros((STAT_ROWS, 1), jnp.int32)
    for head in range(heads):
        out = jnp.where((rows == head) | (rows == head + heads), off_ref[head], out)
    return out


def pair_weights(rows, middle_offset):
    both = (iota((rows, rows), 0) % MIDDLE == middle_offset) & (
        iota((rows, rows), 1) % MIDDLE == middle_offset
    )
    return jnp.where(both, 2.0, 1.0)


def pack_kernel(
    off_in, q_ref, k_ref, v_ref, g_ref, near_kv_ref, near_qg_ref, spec_ref,
    off_ref, buffer, sems, off_sem,
):
    rows, width = q_ref.shape
    heads = width // HD
    near_rows, spec_rows = rows // MIDDLE, rows // UPPER
    places = (
        (k_ref, 0, near_kv_ref, 0, 1),
        (v_ref, 1, near_kv_ref, 1, 2),
        (q_ref, 2, near_qg_ref, 0, 0),
        (g_ref, 3, near_qg_ref, 1, 3),
    )
    off_copy = pltpu.make_async_copy(off_in, off_ref, off_sem)
    off_copy.start()
    copies = [
        pltpu.make_async_copy(source, buffer.at[index], sems.at[index])
        for source, index, _, _, _ in places
    ]
    for copy in copies:
        copy.start()
    off_copy.wait()
    offsets = lane_offsets(off_ref, heads, width)
    middle = iota((rows, width), 0) % MIDDLE == offsets % MIDDLE
    index = iota((near_rows, width), 0)
    gather = jnp.where(
        iota((near_rows, rows), 1) // MIDDLE == iota((near_rows, rows), 0), 1.0, 0.0
    ).astype(BF16)
    spec_ref[...] = jnp.zeros(spec_ref.shape, BF16)
    for (_, source, near_ref, slot, kind), copy in zip(places, copies):
        copy.wait()
        whole = buffer[source].astype(F32)
        kept = dot_nn(gather, jnp.where(middle, whole, 0.0).astype(BF16))
        near_ref[slot * near_rows : (slot + 1) * near_rows, :] = kept.astype(BF16)
        step = UPPER // MIDDLE
        top = jnp.where(index % step == offsets // MIDDLE, kept, 0.0)
        top = top.reshape(spec_rows, step, width).sum(axis=1)
        pad = jnp.zeros((SPEC_PAD - spec_rows, width), F32)
        spec_ref[kind * SPEC_PAD : (kind + 1) * SPEC_PAD, :] = jnp.concatenate(
            [top, pad], axis=0
        ).astype(BF16)


def split_terms(value):
    terms = []
    for _ in range(3):
        terms.append(value.astype(BF16).astype(F32))
        value = value - terms[-1]
    return terms


def halves(ref):
    rows = ref.shape[0] // 2
    return ref.at[:rows], ref.at[rows:]


def key_value_refs(refs):
    own, beside = halves(refs[0]), halves(refs[1])
    rows = own[0].shape[0]
    next_k = [r.at[:rows] for r in refs[2:4]]
    near = []
    for low in range(rows, refs[2].shape[0], 2 * (rows // MIDDLE)):
        near += [r.at[low : low + 2 * (rows // MIDDLE)] for r in refs[2:4]]
    return (own[0], beside[0], *next_k), (own[1], beside[1], *refs[4:6]), near


def chunks(refs, rows):
    first, second = refs
    pieces = []
    for low in range(0, first.shape[0], rows):
        pieces += [first.at[low : low + rows], second.at[low : low + rows]]
    return pieces


def near_part(near_refs, slot, lanes):
    rows = near_refs[0].shape[0] // 2
    return jnp.concatenate([r[slot * rows : (slot + 1) * rows, lanes] for r in near_refs], axis=0)


def merge_kernel(first_ref, second_ref, _, out_ref):
    rows = first_ref.shape[0]
    out_ref[:rows, :] = first_ref[...]
    out_ref[rows:, :] = second_ref[...]


def forward_kernel(near_count, off_ref, qg_ref, spec_ref, own_near_ref, *refs):
    k_refs, v_refs, near_refs = key_value_refs(refs[:KV_ARRAYS])
    out_ref, far_ref = refs[-2:]
    rows, width = k_refs[0].shape
    heads = width // HD
    log_sums, dots = [], []
    for head in range(heads):
        lanes = pair_slice(head)
        middle_offset = off_ref[head] % MIDDLE
        chosen = iota((1, rows), 1) % MIDDLE == middle_offset
        weight = pair_weights(rows, middle_offset)
        query = one_head(qg_ref[:rows, lanes], head, SCALE)
        grad = one_head(qg_ref[rows:, lanes], head)
        scores = [dot_nt(r[:, lanes], query) for r in k_refs]
        top = jnp.max(scores[0], axis=0, keepdims=True)
        for part in scores[1:]:
            top = jnp.maximum(top, jnp.max(part, axis=0, keepdims=True))
        if near_count:
            far_scores = dot_nt(near_part(near_refs, 0, lanes), query)
            far_scores = jnp.where(chosen, far_scores, LOW)
            top = jnp.maximum(top, jnp.max(far_scores, axis=0, keepdims=True))
        total = jnp.zeros((1, rows), F32)
        product = jnp.zeros((1, rows), F32)
        for part, v_ref in zip(scores, v_refs):
            weights = jnp.exp(part - top) * weight
            total = total + jnp.sum(weights, axis=0, keepdims=True)
            inner = dot_nt(v_ref[:, lanes], grad)
            product = product + jnp.sum(weights * inner, axis=0, keepdims=True)
        if near_count:
            weights = jnp.exp(far_scores - top)
            total = total + jnp.sum(weights, axis=0, keepdims=True)
            inner = dot_nt(near_part(near_refs, 1, lanes), grad)
            product = product + jnp.sum(weights * inner, axis=0, keepdims=True)
        log_sums.append(top + jnp.log(total))
        dots.append(product / total)
    pad = jnp.zeros((STAT_ROWS - 2 * heads, rows), F32)
    stats = jnp.concatenate(log_sums + dots + [pad], axis=0)
    out_ref[:, :rows] = stats
    offsets = row_offsets(off_ref, heads)
    token = iota((STAT_ROWS, rows), 1)
    spec_rows = rows // UPPER
    lane = iota((STAT_ROWS, width), 1)
    row = iota((STAT_ROWS, width), 0)
    place = iota((1, width), 1) % HD
    lines = [
        spec_ref[kind * SPEC_PAD : kind * SPEC_PAD + spec_rows, :].astype(F32) for kind in range(4)
    ]
    for index in range(spec_rows):
        value = jnp.sum(
            jnp.where(token == offsets + index * UPPER, stats, 0.0), axis=1, keepdims=True
        )
        line = jnp.zeros((1, width), F32)
        for kind in range(2):
            spread = jnp.sum(
                jnp.where(lane // HD + kind * heads == row, value, 0.0), axis=0, keepdims=True
            )
            for index_of, term in enumerate(split_terms(spread)):
                line = jnp.where(place == 3 * kind + index_of, term, line)
        lines.append(line)
    lines.append(jnp.zeros((STAT_ROWS - 5 * spec_rows, width), F32))
    block = jnp.concatenate(lines, axis=0)
    out_ref[:, rows:] = block
    near_rows = own_near_ref.shape[0]
    far_ref[:near_rows, :] = own_near_ref[...]
    far_ref[near_rows : near_rows + STAT_ROWS, :] = block.astype(BF16)
    kept = jnp.where(token % MIDDLE == offsets % MIDDLE, stats, 0.0)
    gather = jnp.where(iota((rows, PAIR), 0) // MIDDLE == iota((rows, PAIR), 1), 1.0, 0.0)
    gather = gather.astype(BF16)
    for index, term in enumerate(split_terms(kept)):
        far_ref[near_rows + STAT_ROWS :, index * PAIR : (index + 1) * PAIR] = dot_nn(
            term.astype(BF16), gather
        ).astype(BF16)


def query_kernel(near_count, off_ref, qg_ref, spec_in, pay_ref, *refs):
    k_refs, v_refs, near_refs = key_value_refs(refs[:KV_ARRAYS])
    dq_ref, spec_ref = refs[-2:]
    rows, width = k_refs[0].shape
    heads = width // HD
    spec_rows = rows // UPPER
    full = rows + SPEC_PAD
    columns = jnp.transpose(pay_ref[:, :rows])
    offsets = lane_offsets(off_ref, heads, width)
    column = iota((1, STAT_ROWS), 1)
    column_offsets = jnp.zeros((1, STAT_ROWS), jnp.int32)
    for head in range(heads):
        column_offsets = jnp.where(
            (column == head) | (column == head + heads), off_ref[head], column_offsets
        )
    token = iota((rows, STAT_ROWS), 0)
    lines = [
        jnp.sum(
            jnp.where(token == column_offsets + index * UPPER, columns, 0.0),
            axis=0,
            keepdims=True,
        )
        for index in range(spec_rows)
    ]
    lines.append(jnp.zeros((SPEC_PAD - spec_rows, STAT_ROWS), F32))
    columns = jnp.concatenate([columns] + lines, axis=0)
    for pair in range(heads // 2):
        lanes = slice(pair * PAIR, (pair + 1) * PAIR)
        both_q = jnp.concatenate([qg_ref[:rows, lanes], spec_in[:SPEC_PAD, lanes]], axis=0)
        both_g = jnp.concatenate([qg_ref[rows:, lanes], spec_in[3 * SPEC_PAD :, lanes]], axis=0)
        keys = [r[:, lanes] for r in k_refs]
        if near_count:
            keys.append(near_part(near_refs, 0, lanes))
        every_key = jnp.concatenate(keys, axis=0)
        results = []
        for head in (2 * pair, 2 * pair + 1):
            middle_offset = off_ref[head] % MIDDLE
            row = iota((full, 1), 0)
            chosen = (row % MIDDLE == middle_offset) | (row >= rows)
            chosen_key = iota((1, rows), 1) % MIDDLE == middle_offset
            weight = jnp.where(chosen & chosen_key, 2.0, 1.0)
            query = one_head(both_q, head, SCALE)
            grad = one_head(both_g, head)
            log_sum = columns[:, head : head + 1]
            dot = columns[:, heads + head : heads + head + 1]
            parts = []
            for key, v_ref in zip(keys, v_refs):
                probs = jnp.exp(dot_nt(query, key) - log_sum) * weight
                inner = dot_nt(grad, v_ref[:, lanes]) - dot
                parts.append(
                    jnp.concatenate([(probs * inner).astype(BF16), probs[rows:].astype(BF16)], axis=0)
                )
            if near_count:
                scores = jnp.where(chosen, dot_nt(query, keys[-1]), LOW)
                probs = jnp.exp(scores - log_sum)
                inner = dot_nt(grad, near_part(near_refs, 1, lanes)) - dot
                parts.append(
                    jnp.concatenate([(probs * inner).astype(BF16), probs[rows:].astype(BF16)], axis=0)
                )
            results.append(dot_nn(jnp.concatenate(parts, axis=1), every_key))
        result = jnp.where(half_mask(0), results[0], results[1]) * SCALE
        special = iota((rows, PAIR), 0) % UPPER == offsets[:, lanes]
        dq_ref[:, lanes] = jnp.where(special, 0.0, result[:rows])
        spec_ref[:spec_rows, lanes] = result[rows : rows + spec_rows]
        spec_ref[spec_rows:, lanes] = result[full : full + spec_rows]


def stack_kernel(*refs):
    out, low = refs[-1], 0
    for ref in refs[:-1]:
        rows = ref.shape[0]
        out[low : low + rows, :] = ref[...]
        low += rows


def far_chunks(tok_rows, refs):
    return chunks(refs, 2 * (tok_rows // MIDDLE) + 2 * STAT_ROWS) if refs else []


def relay_kernel(first_ref, *refs):
    pay_refs, far_refs, (pay_out, far_out) = refs[:2], refs[2:-2], refs[-2:]
    for parts, out in ((pay_refs, pay_out), (far_refs, far_out)):
        for index, ref in enumerate(parts):
            rows = ref.shape[0]
            out[index * rows : (index + 1) * rows, :] = ref[...]


def key_kernel(near_count, off_ref, kv_ref, *refs):
    k_ref, v_ref = halves(kv_ref)
    qg_refs = refs[:GROUP]
    pay_refs = chunks(refs[GROUP : GROUP + 2], STAT_ROWS)
    far_refs = far_chunks(k_ref.shape[0], refs[GROUP + 2 : -2])
    dk_ref, dv_ref = refs[-2:]
    rows, width = k_ref.shape
    heads = width // HD
    near_rows = rows // MIDDLE
    if near_count:
        first = 2 * near_rows + STAT_ROWS
        far_stats = []
        for r in far_refs:
            lines = r[first : first + STAT_ROWS, :].astype(F32)
            line = lines[:, :PAIR] + lines[:, PAIR : 2 * PAIR] + lines[:, 2 * PAIR : 3 * PAIR]
            far_stats.append(line[:, :near_rows])
        far_stats = jnp.concatenate(far_stats, axis=1)
    for pair in range(heads // 2):
        lanes = slice(pair * PAIR, (pair + 1) * PAIR)
        queries = [r[:rows, lanes] for r in qg_refs]
        grads = [r[rows:, lanes] for r in qg_refs]
        if near_count:
            queries.append(
                jnp.concatenate([r[:near_rows, lanes] for r in far_refs], axis=0)
            )
            grads.append(
                jnp.concatenate([r[near_rows : 2 * near_rows, lanes] for r in far_refs], axis=0)
            )
        every_query = jnp.concatenate(queries, axis=0)
        every_grad = jnp.concatenate(grads, axis=0)
        key_grads, value_grads = [], []
        for head in (2 * pair, 2 * pair + 1):
            middle_offset = off_ref[head] % MIDDLE
            chosen = iota((rows, 1), 0) % MIDDLE == middle_offset
            weight = pair_weights(rows, middle_offset)
            keys = one_head(k_ref[:, lanes], head, SCALE)
            values = one_head(v_ref[:, lanes], head)
            special = iota((1, rows), 1) % UPPER == off_ref[head]
            prob_parts, score_parts = [], []
            for query, grad, pay_ref in zip(queries, grads, pay_refs):
                log_sum = jnp.where(special, HIGH, pay_ref[head : head + 1, :rows])
                dot = pay_ref[heads + head : heads + head + 1, :rows]
                probs = jnp.exp(dot_nt(keys, query) - log_sum) * weight
                inner = dot_nt(values, grad) - dot
                prob_parts.append(probs.astype(BF16))
                score_parts.append((probs * inner).astype(BF16))
            if near_count:
                count = near_count * near_rows
                special = iota((1, count), 1) % (UPPER // MIDDLE) == off_ref[head] // MIDDLE
                log_sum = jnp.where(special, HIGH, far_stats[head : head + 1, :])
                dot = far_stats[heads + head : heads + head + 1, :]
                scores = jnp.where(chosen, dot_nt(keys, queries[-1]), LOW)
                probs = jnp.exp(scores - log_sum)
                inner = dot_nt(values, grads[-1]) - dot
                prob_parts.append(probs.astype(BF16))
                score_parts.append((probs * inner).astype(BF16))
            key_grads.append(dot_nn(jnp.concatenate(score_parts, axis=1), every_query))
            value_grads.append(dot_nn(jnp.concatenate(prob_parts, axis=1), every_grad))
        low = half_mask(0)
        dk_ref[:, lanes] = jnp.where(low, key_grads[0], key_grads[1]) * SCALE
        dv_ref[:, lanes] = jnp.where(low, value_grads[0], value_grads[1])


def collect_kernel(tok_rows, *refs):
    out_ref = refs[-1]
    pay_refs = chunks(refs[:2], STAT_ROWS)
    far_refs = far_chunks(tok_rows, refs[2:-1])
    spec_rows = tok_rows // UPPER
    first = 2 * (tok_rows // MIDDLE)
    count = spec_rows * (len(pay_refs) + len(far_refs))
    blocks = [r[:, tok_rows:] for r in pay_refs]
    blocks += [r[first : first + STAT_ROWS, :].astype(F32) for r in far_refs]
    for kind in range(5):
        lines = [b[kind * spec_rows : (kind + 1) * spec_rows] for b in blocks]
        out_ref[kind * count : (kind + 1) * count, :] = jnp.concatenate(lines, axis=0).astype(BF16)


def special_kernel(slots, off_ref, kv_ref, dq_in, spec_ref, dk_in, dv_in, *refs):
    k_ref, v_ref = halves(kv_ref)
    blocks = refs[:-3]
    dq_ref, dk_ref, dv_ref = refs[-3:]
    rows, width = k_ref.shape
    heads = width // HD
    spec_rows = rows // UPPER
    count = slots * spec_rows
    every = count * len(blocks)
    offsets = lane_offsets(off_ref, heads, width)

    def kind(index, lanes):
        return jnp.concatenate(
            [b[index * count : (index + 1) * count, lanes] for b in blocks], axis=0
        )

    def two(block, scale=1.0):
        return jnp.concatenate([one_head(block, 0, scale), one_head(block, 1, scale)], axis=0)

    column = iota((1, 2 * every), 1)
    second = column >= every
    column = column % every
    same_group = jnp.where(column < GROUP * spec_rows, 1.0, 0.0)
    same_segment = jnp.where(column < count, 1.0, 0.0)
    row = iota((rows, 1), 0)
    low = half_mask(0)
    place = iota((8, PAIR), 1) % HD
    first_term = jnp.where(iota((8, PAIR), 0) == 0, 0, 3)
    picks = jnp.where((place >= first_term) & (place < first_term + 3), 1.0, 0.0).astype(BF16)
    for pair in range(heads // 2):
        lanes = slice(pair * PAIR, (pair + 1) * PAIR)
        all_q, all_k, all_v, all_g, all_s = [kind(index, lanes) for index in range(5)]
        query, grad = two(all_q, SCALE), two(all_g)
        known = dot_nt(picks, two(all_s))
        known_sum, known_dot = known[0:1], known[1:2]
        scores = dot_nt(all_k, query)
        inner = dot_nt(all_v, grad)
        top = jnp.max(scores, axis=0, keepdims=True)
        weights = jnp.exp(scores - top)
        total = jnp.sum(weights, axis=0, keepdims=True)
        product = jnp.sum(weights * inner, axis=0, keepdims=True) / total
        log_sum = top + jnp.log(total)
        most = jnp.maximum(known_sum, log_sum)
        joint = most + jnp.log(jnp.exp(known_sum - most) + jnp.exp(log_sum - most))
        share = jnp.exp(known_sum - joint)
        dot = known_dot * share + product * jnp.exp(log_sum - joint)
        probs = jnp.exp(scores - joint)
        grad_q = SCALE * lax.dot_general(
            (probs * (inner - dot)).astype(BF16),
            all_k,
            (((0,), (0,)), ((), ())),
            preferred_element_type=F32,
        )
        change = known_dot - dot
        lines = []
        for index in range(spec_rows):
            other = every + index
            ratio = jnp.where(low, share[:, index : index + 1], share[:, other : other + 1])
            moved = jnp.where(low, change[:, index : index + 1], change[:, other : other + 1])
            top_q = jnp.where(low, grad_q[index : index + 1], grad_q[other : other + 1])
            near_q = spec_ref[index : index + 1, lanes]
            key_sum = spec_ref[spec_rows + index : spec_rows + index + 1, lanes]
            line = ratio * (near_q + moved * key_sum) + top_q
            lines.append(jnp.broadcast_to(line, (UPPER, PAIR)))
        special = row % UPPER == offsets[:, lanes]
        dq_ref[:, lanes] = (
            dq_in[:, lanes] + jnp.where(special, jnp.concatenate(lines, axis=0), 0.0)
        ).astype(BF16)
        offset = jnp.where(second, off_ref[2 * pair + 1], off_ref[2 * pair])
        middle = row % MIDDLE == offset % MIDDLE
        upper = row % UPPER == offset
        weight = same_group + jnp.where(middle, same_segment, 0.0) + jnp.where(upper, 1.0, 0.0)
        scores = jnp.where(weight > 0.0, dot_nt(k_ref[:, lanes], query), LOW)
        probs = jnp.exp(scores - joint) * weight
        inner = dot_nt(v_ref[:, lanes], grad) - dot
        dk_ref[:, lanes] = (
            dk_in[:, lanes] + dot_nn((probs * inner).astype(BF16), query)
        ).astype(BF16)
        dv_ref[:, lanes] = (dv_in[:, lanes] + dot_nn(probs.astype(BF16), grad)).astype(BF16)


def call(kernel, outs, *arrays, us=1.0, raw=False, scratch=(), vmem_mib=40):
    smem = pl.BlockSpec(memory_space=pltpu.SMEM)
    vmem = pl.BlockSpec(memory_space=pltpu.VMEM)
    space = pl.BlockSpec(memory_space=pltpu.HBM) if raw else vmem
    specs = [smem if a.dtype == jnp.int32 and not raw else space for a in arrays]
    return pl.pallas_call(
        kernel,
        out_shape=tuple(jax.ShapeDtypeStruct(shape, dtype) for shape, dtype in outs),
        in_specs=specs,
        out_specs=tuple(vmem for _ in outs),
        scratch_shapes=scratch,
        cost_estimate=pl.CostEstimate(
            flops=int(us * 1.15e9), bytes_accessed=0, transcendentals=0
        ),
        compiler_params=pltpu.CompilerParams(vmem_limit_bytes=vmem_mib * 1024 * 1024),
    )(*arrays)


def across(value, axis, mask):
    size = lax.axis_size(axis)
    return lax.ppermute(value, axis, [(source, source ^ mask) for source in range(size)])


def local(queries, key_matrix, value_matrix, grad_out, offsets):
    rows, width = queries.shape
    slots, outer = lax.axis_size("ctxb"), lax.axis_size("ctxa")
    near_count = slots - GROUP
    near_rows, spec_rows = rows // MIDDLE, rows // UPPER

    next_k, next_v = across(key_matrix, "ctxb", 2), across(value_matrix, "ctxb", 2)
    near_kv, near_qg, spec = call(
        pack_kernel,
        [
            ((2 * near_rows, width), BF16),
            ((2 * near_rows, width), BF16),
            ((4 * SPEC_PAD, width), BF16),
        ],
        offsets, queries, key_matrix, value_matrix, grad_out,
        us=1.3, raw=True, vmem_mib=60,
        scratch=[
            pltpu.SMEM(offsets.shape, jnp.int32),
            pltpu.VMEM((4, rows, width), BF16),
            pltpu.SemaphoreType.DMA((4,)),
            pltpu.SemaphoreType.DMA,
        ],
    )
    near_came = [across(near_kv, "ctxb", mask) for mask in range(GROUP, slots, 2)]
    both = [((2 * rows, width), BF16)]
    (kv,) = call(merge_kernel, both, key_matrix, value_matrix, near_kv, us=0.3)
    (stacked,) = call(
        stack_kernel,
        [((rows + 2 * near_rows * len(near_came), width), BF16)],
        next_k, *near_came, us=0.2,
    )
    kv_parts = [kv, across(kv, "ctxb", 1), stacked, across(stacked, "ctxb", 1)]
    kv_parts += [next_v, across(next_v, "ctxb", 1)]
    (qg,) = call(merge_kernel, both, queries, grad_out, stacked, us=0.3)
    next_qg = across(qg, "ctxb", 2)
    core_qg = across(qg, "ctxb", 1)
    pay, far = call(
        partial(forward_kernel, near_count),
        [
            ((STAT_ROWS, rows + width), F32),
            ((2 * near_rows + 2 * STAT_ROWS, width), BF16),
        ],
        offsets, qg, spec, near_qg, *kv_parts, us=4.7,
    )
    dq, dq_spec = call(
        partial(query_kernel, near_count),
        [((rows, width), F32), ((2 * spec_rows, width), F32)],
        offsets, qg, spec, pay, *kv_parts, us=5.0,
    )
    pays_far = [pay, across(pay, "ctxb", 2)]
    far_came = [across(far, "ctxb", mask) for mask in range(GROUP, slots, 2)]
    held = call(
        relay_kernel,
        [((2 * STAT_ROWS, rows + width), F32)]
        + [((far.shape[0] * len(far_came), width), BF16)],
        dq_spec, *pays_far, *far_came, us=0.2,
    )
    pays, fars = [(part, across(part, "ctxb", 1)) for part in held]
    qg_parts = [qg, core_qg, next_qg, across(next_qg, "ctxb", 1)]
    (block,) = call(
        partial(collect_kernel, rows), [((5 * slots * spec_rows, width), BF16)], *pays, *fars,
        us=0.3,
    )
    blocks = [block] + [across(block, "ctxa", mask) for mask in range(1, outer)]
    dk, dv = call(
        partial(key_kernel, near_count),
        [((rows, width), F32), ((rows, width), F32)],
        offsets, kv, *qg_parts, *pays, *fars, us=5.0,
    )
    return call(
        partial(special_kernel, slots),
        [((rows, width), BF16)] * 3,
        offsets, kv, dq, dq_spec, dk, dv, *blocks, us=3.0,
    )


def solution(mesh):
    split = P(("ctxa", "ctxb"), None)
    return jax.shard_map(
        local,
        mesh=mesh,
        in_specs=(split, split, split, split, P()),
        out_specs=(split, split, split),
        check_vma=False,
    )
```

time: 69.8 us -> 49.8 us (0.71)
  waiting for transfers between devices: 19.3 us -> 12.3 us
  Pallas kernels: 25.3 us -> 18.8 us
  starting transfers between devices: 20.6 us -> 16.1 us
  local copies, waits for them, and re-layouts: 3.44 us -> 1.47 us
    ppermute x26 -> x18, waiting for transfers between devices: 19.3 us -> 12.3 us  [across(): lax.ppermute(value, axis, [(source, source ^ mask) for source in range(si...]
    pallas_call x6 -> x10, Pallas kernels: 25.3 us -> 18.8 us  [call(): pl.pallas_call(kernel, out_shape=tuple((jax.ShapeDtypeStruct(shape, dtype...]
    ppermute x26 -> x18, starting transfers between devices: 20.6 us -> 16.1 us  [across(): lax.ppermute(value, axis, [(source, source ^ mask) for source in range(si...]
    unnamed x12 -> x16, local copies, waits for them, and re-layouts: 3.44 us -> 1.47 us
  transfers between devices with their start and end apart: 26 -> 18, of which waited for: 8 -> 5; matrix products, arithmetic and copies ran while one was open for 0% -> 0% of each run, Pallas kernels for 27% -> 32%
where the time goes in v2:
time: 49.8 us; the launch traced here: 49.6 us
  Pallas kernels  18.8 us (38%)
  starting transfers between devices  16.1 us (32%)
  waiting for transfers between devices  12.3 us (25%)
  local copies, waits for them, and re-layouts  1.47 us (3%)
  between operations  0.85 us (2%)
    pallas_call x10, Pallas kernels, call(): pl.pallas_call(kernel, out_shape=tuple((jax.ShapeDtypeStruct(shape, dtype...  18.8 us
    ppermute x18, starting transfers between devices, across(): lax.ppermute(value, axis, [(source, source ^ mask) for source in range(si...  16.1 us
    ppermute x18, waiting for transfers between devices, across(): lax.ppermute(value, axis, [(source, source ^ mask) for source in range(si...  12.3 us
    unnamed x16, local copies, waits for them, and re-layouts  1.47 us
  transfers between devices with their start and end apart: 18, of which 5 were waited for; matrix products, arithmetic and copies ran while one was open for 0% of the time, Pallas kernels for 32%

profile of v2, /device:TPU:0, one launch (start us, length us, event | category | flops | bytes accessed | tf_op | source)
XLA Modules:
  0.0 49.6 jit_solution(11675175272756802104)
XLA Ops:
  0.7 3.1 %collective-permute-start = (bf16[256,384]{1,0:T(8,128)(2,1)}, bf16[256,384]{1,0:T(8,128)(2,1)S(1)}, u32[]{:S(2)}, u32[]{:S(2)}) collective-permute-start(bf16[256,384]{1,0:T(8,128)(2,1)} %first_ref.2), channel_id=1, source_target_pairs={{0,2},{1,3},{2,0},{3,1},{4,6},{5,7},{6,4},{7,5},{8,10},{9,11},{10,... | collective-permute-start | bytes 589832 | tf_op jit(solution)/shard_map/ppermute | solution.py:497
  3.7 0.1 collective-permute-start.5
  3.8 2.3 %shard_map.76 = (bf16[64,384]{1,0:T(8,128)(2,1)}, bf16[64,384]{1,0:T(8,128)(2,1)}, bf16[64,384]{1,0:T(8,128)(2,1)}) custom-call(s32[6]{0:T(128)} %off_ref.7, bf16[256,384]{1,0:T(8,128)(2,1)} %first_ref.3, bf16[256,384]{1,0:T(8,128)(2,1)} %first_ref.2, bf16[256,384]{1,0:T(8,128)(2,1)} %second_ref.2, bf16[256,384]{1,0:T(8,128)(2,1)} %second_ref.3), custom_call_target="tpu_custom_call" | custom-call | flops 1495000064 | tf_op jit(solution)/shard_map/pallas_call | solution.py:482
  6.1 0.0 copy-start.4
  6.1 0.8 %copy-done.4 = bf16[64,384]{1,0:T(8,128)(2,1)S(1)} copy-done((bf16[64,384]{1,0:T(8,128)(2,1)S(1)}, bf16[64,384]{1,0:T(8,128)(2,1)}, u32[]{:S(2)}) %copy-start.4) | copy-done | bytes 49176
  7.0 0.0 copy-start.3
  7.0 0.1 collective-permute-start.3
  7.0 3.0 %collective-permute-start.1 = (bf16[64,384]{1,0:T(8,128)(2,1)S(1)}, bf16[64,384]{1,0:T(8,128)(2,1)S(1)}, u32[]{:S(2)}, u32[]{:S(2)}) collective-permute-start(bf16[64,384]{1,0:T(8,128)(2,1)S(1)} %copy-done.4), channel_id=1, source_target_pairs={{0,4},{1,5},{2,6},{3,7},{4,0},{5,1},{6,2},{7,3},{8,12},{9,13},{10,... | collective-permute-start | bytes 147464 | tf_op jit(solution)/shard_map/ppermute | solution.py:497
  10.1 1.3 %collective-permute-start.2 = (bf16[64,384]{1,0:T(8,128)(2,1)S(1)}, bf16[64,384]{1,0:T(8,128)(2,1)S(1)}, u32[]{:S(2)}, u32[]{:S(2)}) collective-permute-start(bf16[64,384]{1,0:T(8,128)(2,1)S(1)} %copy-done.4), channel_id=1, source_target_pairs={{0,6},{1,7},{2,4},{3,5},{4,2},{5,3},{6,0},{7,1},{8,14},{9,15},{10,... | collective-permute-start | bytes 147464 | tf_op jit(solution)/shard_map/ppermute | solution.py:497
  11.4 2.5 %collective-permute-done.1.refs_1_ = bf16[64,384]{1,0:T(8,128)(2,1)S(1)} collective-permute-done((bf16[64,384]{1,0:T(8,128)(2,1)S(1)}, bf16[64,384]{1,0:T(8,128)(2,1)S(1)}, u32[]{:S(2)}, u32[]{:S(2)}) %collective-permute-start.1) | collective-permute-done | bytes 49184 | tf_op jit(solution)/shard_map/ppermute | solution.py:497
  13.9 3.5 %collective-permute-done.2.refs_2_ = bf16[64,384]{1,0:T(8,128)(2,1)S(1)} collective-permute-done((bf16[64,384]{1,0:T(8,128)(2,1)S(1)}, bf16[64,384]{1,0:T(8,128)(2,1)S(1)}, u32[]{:S(2)}, u32[]{:S(2)}) %collective-permute-start.2) | collective-permute-done | bytes 49184 | tf_op jit(solution)/shard_map/ppermute | solution.py:497
  17.4 0.0 copy-start.6
  17.4 0.1 collective-permute-start.4
  17.5 0.5 collective-permute-start.6
  18.0 0.2 collective-permute-start.7
  18.2 0.0 collective-permute-start.8
  18.2 1.1 %collective-permute-done.6.refs_5_ = bf16[256,384]{1,0:T(8,128)(2,1)S(1)} collective-permute-done((bf16[256,384]{1,0:T(8,128)(2,1)S(1)}, bf16[256,384]{1,0:T(8,128)(2,1)S(1)}, u32[]{:S(2)}, u32[]{:S(2)}) %collective-permute-start.6) | collective-permute-done | bytes 196640 | tf_op jit(solution)/shard_map/ppermute | solution.py:497
  19.4 0.6 %copy-done.5 = s32[6]{0:T(128)S(1)} copy-done((s32[6]{0:T(128)S(1)}, s32[6]{0:T(128)}, u32[]{:S(2)}) %copy-start.5) | copy-done | bytes 48
  20.0 4.3 %shard_map.80 = (f32[16,640]{1,0:T(8,128)S(1)}, bf16[96,384]{1,0:T(8,128)(2,1)S(1)}) custom-call(s32[6]{0:T(128)S(1)} %copy-done.5, bf16[512,384]{1,0:T(8,128)(2,1)S(1)} %shard_map.79.qg_ref.refs_0_, bf16[64,384]{1,0:T(8,128)(2,1)S(1)} %copy-done.6, bf16[64,384]{1,0:T(8,128)(2,1)S(1)} %copy-done.7, bf16[512,384]{1,0:T(8,128)(2,1)S(1)} %shard_map.77.refs_0_.kv_ref, ...), custom_call_target="tpu_custom_call" | custom-call | flops 5405000192 | tf_op jit(solution)/shard_map/pallas_call | solution.py:482
  24.3 1.1 %collective-permute-start.11 = (bf16[96,384]{1,0:T(8,128)(2,1)S(1)}, bf16[96,384]{1,0:T(8,128)(2,1)S(1)}, u32[]{:S(2)}, u32[]{:S(2)}) collective-permute-start(bf16[96,384]{1,0:T(8,128)(2,1)S(1)} %get-tuple-element.20), channel_id=1, source_target_pairs={{0,4},{1,5},{2,6},{3,7},{4,0},{5,1},{6,2},{7,3},{8,12},{9,13},{10,... | collective-permute-start | bytes 221192 | tf_op jit(solution)/shard_map/ppermute | solution.py:497
  25.3 2.3 %collective-permute-start.12 = (bf16[96,384]{1,0:T(8,128)(2,1)S(1)}, bf16[96,384]{1,0:T(8,128)(2,1)S(1)}, u32[]{:S(2)}, u32[]{:S(2)}) collective-permute-start(bf16[96,384]{1,0:T(8,128)(2,1)S(1)} %get-tuple-element.20), channel_id=1, source_target_pairs={{0,6},{1,7},{2,4},{3,5},{4,2},{5,3},{6,0},{7,1},{8,14},{9,15},{10,... | collective-permute-start | bytes 221192 | tf_op jit(solution)/shard_map/ppermute | solution.py:497
  27.6 0.2 collective-permute-start.10
  27.8 4.1 %collective-permute-done.8.refs_2_ = bf16[512,384]{1,0:T(8,128)(2,1)S(1)} collective-permute-done((bf16[512,384]{1,0:T(8,128)(2,1)S(1)}, bf16[512,384]{1,0:T(8,128)(2,1)S(1)}, u32[]{:S(2)}, u32[]{:S(2)}) %collective-permute-start.8) | collective-permute-done | bytes 393248 | tf_op jit(solution)/shard_map/ppermute | solution.py:497
  31.9 4.6 %shard_map.81 = (f32[256,384]{1,0:T(8,128)S(1)}, f32[4,384]{1,0:T(4,128)S(1)}) custom-call(s32[6]{0:T(128)S(1)} %copy-done.5, bf16[512,384]{1,0:T(8,128)(2,1)S(1)} %shard_map.79.qg_ref.refs_0_, bf16[64,384]{1,0:T(8,128)(2,1)S(1)} %copy-done.6, f32[16,640]{1,0:T(8,128)S(1)} %get-tuple-element.17.pay_ref.refs_0_, ...), custom_call_target="tpu_custom_call" | custom-call | flops 5750000128 | tf_op jit(solution)/shard_map/pallas_call | solution.py:482
  36.6 0.6 %collective-permute-start.14 = (bf16[192,384]{1,0:T(8,128)(2,1)S(1)}, bf16[192,384]{1,0:T(8,128)(2,1)S(1)}, u32[]{:S(2)}, u32[]{:S(2)}) collective-permute-start(bf16[192,384]{1,0:T(8,128)(2,1)S(1)} %get-tuple-element.22.refs_6_.refs_2_), channel_id=1, source_target_pairs={{0,1},{1,0},{2,3},{3,2},{4,5},{5,4},{6,7},{7,6},{8,9},{9,8},{10,11... | collective-permute-start | bytes 442376 | tf_op jit(solution)/shard_map/ppermute | solution.py:497
  37.2 0.1 collective-permute-start.13
  37.2 1.2 %collective-permute-done.13.refs_5_.refs_1_ = f32[32,640]{1,0:T(8,128)S(1)} collective-permute-done((f32[32,640]{1,0:T(8,128)S(1)}, f32[32,640]{1,0:T(8,128)S(1)}, u32[]{:S(2)}, u32[]{:S(2)}) %collective-permute-start.13) | collective-permute-done | bytes 81952 | tf_op jit(solution)/shard_map/ppermute | solution.py:497
  38.5 1.6 %collective-permute-start.15 = (bf16[80,384]{1,0:T(8,128)(2,1)S(1)}, bf16[80,384]{1,0:T(8,128)(2,1)S(1)}, u32[]{:S(2)}, u32[]{:S(2)}) collective-permute-start(bf16[80,384]{1,0:T(8,128)(2,1)S(1)} %shard_map.84.refs_0_), channel_id=1, source_target_pairs={{0,8},{8,0},{16,24},{24,16},{1,9},{9,1},{17,25},{25,17},{2,10},{10... | collective-permute-start | bytes 184328 | tf_op jit(solution)/shard_map/ppermute | solution.py:497
  40.0 1.5 %collective-permute-start.16 = (bf16[80,384]{1,0:T(8,128)(2,1)S(1)}, bf16[80,384]{1,0:T(8,128)(2,1)S(1)}, u32[]{:S(2)}, u32[]{:S(2)}) collective-permute-start(bf16[80,384]{1,0:T(8,128)(2,1)S(1)} %shard_map.84.refs_0_), channel_id=1, source_target_pairs={{0,16},{8,24},{16,0},{24,8},{1,17},{9,25},{17,1},{25,9},{2,18},{10... | collective-permute-start | bytes 184328 | tf_op jit(solution)/shard_map/ppermute | solution.py:497
  41.6 0.5 collective-permute-start.17
  42.0 4.7 %shard_map.83 = (f32[256,384]{1,0:T(8,128)S(1)}, f32[256,384]{1,0:T(8,128)S(1)}) custom-call(s32[6]{0:T(128)S(1)} %copy-done.5, bf16[512,384]{1,0:T(8,128)(2,1)S(1)} %shard_map.77.refs_0_.kv_ref, bf16[512,384]{1,0:T(8,128)(2,1)S(1)} %shard_map.79.qg_ref.refs_0_, bf16[512,384]{1,0:T(8,128)(2,1)S(1)} %collective-permute-done.7.refs_1_, ...), custom_call_target="tpu_custom_call" | custom-call | flops 5750000128 | tf_op jit(solution)/shard_map/pallas_call | solution.py:482
  46.8 2.9 %shard_map.85 = (bf16[256,384]{1,0:T(8,128)(2,1)}, bf16[256,384]{1,0:T(8,128)(2,1)}, bf16[256,384]{1,0:T(8,128)(2,1)}) custom-call(s32[6]{0:T(128)S(1)} %copy-done.5, bf16[512,384]{1,0:T(8,128)(2,1)S(1)} %shard_map.77.refs_0_.kv_ref, f32[256,384]{1,0:T(8,128)S(1)} %get-tuple-element.18.dq_in, f32[4,384]{1,0:T(4,128)S(1)} %get-tuple-element.19.first_ref.spec_ref, ...), custom_call_target="tpu_custom_call" | custom-call | flops 3449999872 | tf_op jit(solution)/shard_map/pallas_call | solution.py:482
  (30 shorter events, 0.2 us)
Async XLA Ops:
  0.6 5.5 %copy-start = (bf16[256,384]{1,0:T(8,128)(2,1)S(1)}, bf16[256,384]{1,0:T(8,128)(2,1)}, u32[]{:S(2)}) copy-start(bf16[256,384]{1,0:T(8,128)(2,1)} %first_ref.2) | copy-start | bytes 589828
  0.6 5.5 %copy-start.1 = (bf16[256,384]{1,0:T(8,128)(2,1)S(1)}, bf16[256,384]{1,0:T(8,128)(2,1)}, u32[]{:S(2)}) copy-start(bf16[256,384]{1,0:T(8,128)(2,1)} %second_ref.2) | copy-start | bytes 589828
  0.7 16.7 %collective-permute-start = (bf16[256,384]{1,0:T(8,128)(2,1)}, bf16[256,384]{1,0:T(8,128)(2,1)S(1)}, u32[]{:S(2)}, u32[]{:S(2)}) collective-permute-start(bf16[256,384]{1,0:T(8,128)(2,1)} %first_ref.2), channel_id=1, source_target_pairs={{0,2},{1,3},{2,0},{3,1},{4,6},{5,7},{6,4},{7,5},{8,10},{9,11},{10,... | collective-permute-start | bytes 589832 | tf_op jit(solution)/shard_map/ppermute | solution.py:497
  3.7 13.8 %collective-permute-start.5 = (bf16[256,384]{1,0:T(8,128)(2,1)}, bf16[256,384]{1,0:T(8,128)(2,1)S(1)}, u32[]{:S(2)}, u32[]{:S(2)}) collective-permute-start(bf16[256,384]{1,0:T(8,128)(2,1)} %second_ref.2), channel_id=1, source_target_pairs={{0,2},{1,3},{2,0},{3,1},{4,6},{5,7},{6,4},{7,5},{8,10},{9,11},{10,... | collective-permute-start | bytes 589832 | tf_op jit(solution)/shard_map/ppermute | solution.py:497
  6.1 0.8 %copy-start.4 = (bf16[64,384]{1,0:T(8,128)(2,1)S(1)}, bf16[64,384]{1,0:T(8,128)(2,1)}, u32[]{:S(2)}) copy-start(bf16[64,384]{1,0:T(8,128)(2,1)} %get-tuple-element.14._) | copy-start | bytes 147460
  6.9 11.1 %copy-start.2 = (bf16[256,384]{1,0:T(8,128)(2,1)S(1)}, bf16[256,384]{1,0:T(8,128)(2,1)}, u32[]{:S(2)}) copy-start(bf16[256,384]{1,0:T(8,128)(2,1)} %first_ref.3) | copy-start | bytes 589828
  7.0 11.0 %copy-start.3 = (bf16[256,384]{1,0:T(8,128)(2,1)S(1)}, bf16[256,384]{1,0:T(8,128)(2,1)}, u32[]{:S(2)}) copy-start(bf16[256,384]{1,0:T(8,128)(2,1)} %second_ref.3) | copy-start | bytes 589828
  7.0 11.3 %collective-permute-start.3 = (bf16[512,384]{1,0:T(8,128)(2,1)S(1)}, bf16[512,384]{1,0:T(8,128)(2,1)S(1)}, u32[]{:S(2)}, u32[]{:S(2)}) collective-permute-start(bf16[512,384]{1,0:T(8,128)(2,1)S(1)} %shard_map.77.refs_0_.kv_ref), channel_id=1, source_target_pairs={{0,1},{1,0},{2,3},{3,2},{4,5},{5,4},{6,7},{7,6},{8,9},{9,8},{10,11... | collective-permute-start | bytes 1179656 | tf_op jit(solution)/shard_map/ppermute | solution.py:497
  7.0 6.9 %collective-permute-start.1 = (bf16[64,384]{1,0:T(8,128)(2,1)S(1)}, bf16[64,384]{1,0:T(8,128)(2,1)S(1)}, u32[]{:S(2)}, u32[]{:S(2)}) collective-permute-start(bf16[64,384]{1,0:T(8,128)(2,1)S(1)} %copy-done.4), channel_id=1, source_target_pairs={{0,4},{1,5},{2,6},{3,7},{4,0},{5,1},{6,2},{7,3},{8,12},{9,13},{10,... | collective-permute-start | bytes 147464 | tf_op jit(solution)/shard_map/ppermute | solution.py:497
  10.1 7.3 %collective-permute-start.2 = (bf16[64,384]{1,0:T(8,128)(2,1)S(1)}, bf16[64,384]{1,0:T(8,128)(2,1)S(1)}, u32[]{:S(2)}, u32[]{:S(2)}) collective-permute-start(bf16[64,384]{1,0:T(8,128)(2,1)S(1)} %copy-done.4), channel_id=1, source_target_pairs={{0,6},{1,7},{2,4},{3,5},{4,2},{5,3},{6,0},{7,1},{8,14},{9,15},{10,... | collective-permute-start | bytes 147464 | tf_op jit(solution)/shard_map/ppermute | solution.py:497
  17.4 2.0 %copy-start.6 = (bf16[64,384]{1,0:T(8,128)(2,1)S(1)}, bf16[64,384]{1,0:T(8,128)(2,1)}, u32[]{:S(2)}) copy-start(bf16[64,384]{1,0:T(8,128)(2,1)} %get-tuple-element.15.spec_ref.spec_in) | copy-start | bytes 147460
  17.4 2.0 %copy-start.7 = (bf16[64,384]{1,0:T(8,128)(2,1)S(1)}, bf16[64,384]{1,0:T(8,128)(2,1)}, u32[]{:S(2)}) copy-start(bf16[64,384]{1,0:T(8,128)(2,1)} %get-tuple-element.16.own_near_ref) | copy-start | bytes 147460
  17.4 1.9 %collective-permute-start.4 = (bf16[384,384]{1,0:T(8,128)(2,1)S(1)}, bf16[384,384]{1,0:T(8,128)(2,1)S(1)}, u32[]{:S(2)}, u32[]{:S(2)}) collective-permute-start(bf16[384,384]{1,0:T(8,128)(2,1)S(1)} %shard_map.78._.refs_2_), channel_id=1, source_target_pairs={{0,1},{1,0},{2,3},{3,2},{4,5},{5,4},{6,7},{7,6},{8,9},{9,8},{10,11... | collective-permute-start | bytes 884744 | tf_op jit(solution)/shard_map/ppermute | solution.py:497
  17.5 1.8 %collective-permute-start.6 = (bf16[256,384]{1,0:T(8,128)(2,1)S(1)}, bf16[256,384]{1,0:T(8,128)(2,1)S(1)}, u32[]{:S(2)}, u32[]{:S(2)}) collective-permute-start(bf16[256,384]{1,0:T(8,128)(2,1)S(1)} %collective-permute-done.5.refs_4_), channel_id=1, source_target_pairs={{0,1},{1,0},{2,3},{3,2},{4,5},{5,4},{6,7},{7,6},{8,9},{9,8},{10,11... | collective-permute-start | bytes 589832 | tf_op jit(solution)/shard_map/ppermute | solution.py:497
  18.0 24.0 %collective-permute-start.7 = (bf16[512,384]{1,0:T(8,128)(2,1)S(1)}, bf16[512,384]{1,0:T(8,128)(2,1)S(1)}, u32[]{:S(2)}, u32[]{:S(2)}) collective-permute-start(bf16[512,384]{1,0:T(8,128)(2,1)S(1)} %shard_map.79.qg_ref.refs_0_), channel_id=1, source_target_pairs={{0,1},{1,0},{2,3},{3,2},{4,5},{5,4},{6,7},{7,6},{8,9},{9,8},{10,11... | collective-permute-start | bytes 1179656 | tf_op jit(solution)/shard_map/ppermute | solution.py:497
  18.2 13.7 %collective-permute-start.8 = (bf16[512,384]{1,0:T(8,128)(2,1)S(1)}, bf16[512,384]{1,0:T(8,128)(2,1)S(1)}, u32[]{:S(2)}, u32[]{:S(2)}) collective-permute-start(bf16[512,384]{1,0:T(8,128)(2,1)S(1)} %shard_map.79.qg_ref.refs_0_), channel_id=1, source_target_pairs={{0,2},{1,3},{2,0},{3,1},{4,6},{5,7},{6,4},{7,5},{8,10},{9,11},{10,... | collective-permute-start | bytes 1179656 | tf_op jit(solution)/shard_map/ppermute | solution.py:497
  19.4 0.7 %copy-start.5 = (s32[6]{0:T(128)S(1)}, s32[6]{0:T(128)}, u32[]{:S(2)}) copy-start(s32[6]{0:T(128)} %off_ref.7) | copy-start | bytes 76
  24.3 12.3 %collective-permute-start.11 = (bf16[96,384]{1,0:T(8,128)(2,1)S(1)}, bf16[96,384]{1,0:T(8,128)(2,1)S(1)}, u32[]{:S(2)}, u32[]{:S(2)}) collective-permute-start(bf16[96,384]{1,0:T(8,128)(2,1)S(1)} %get-tuple-element.20), channel_id=1, source_target_pairs={{0,4},{1,5},{2,6},{3,7},{4,0},{5,1},{6,2},{7,3},{8,12},{9,13},{10,... | collective-permute-start | bytes 221192 | tf_op jit(solution)/shard_map/ppermute | solution.py:497
  25.3 11.2 %collective-permute-start.12 = (bf16[96,384]{1,0:T(8,128)(2,1)S(1)}, bf16[96,384]{1,0:T(8,128)(2,1)S(1)}, u32[]{:S(2)}, u32[]{:S(2)}) collective-permute-start(bf16[96,384]{1,0:T(8,128)(2,1)S(1)} %get-tuple-element.20), channel_id=1, source_target_pairs={{0,6},{1,7},{2,4},{3,5},{4,2},{5,3},{6,0},{7,1},{8,14},{9,15},{10,... | collective-permute-start | bytes 221192 | tf_op jit(solution)/shard_map/ppermute | solution.py:497
  27.6 9.0 %collective-permute-start.10 = (f32[16,640]{1,0:T(8,128)S(1)}, f32[16,640]{1,0:T(8,128)S(1)}, u32[]{:S(2)}, u32[]{:S(2)}) collective-permute-start(f32[16,640]{1,0:T(8,128)S(1)} %get-tuple-element.17.pay_ref.refs_0_), channel_id=1, source_target_pairs={{0,2},{1,3},{2,0},{3,1},{4,6},{5,7},{6,4},{7,5},{8,10},{9,11},{10,... | collective-permute-start | bytes 122888 | tf_op jit(solution)/shard_map/ppermute | solution.py:497
  31.9 10.2 %collective-permute-start.9 = (bf16[512,384]{1,0:T(8,128)(2,1)S(1)}, bf16[512,384]{1,0:T(8,128)(2,1)S(1)}, u32[]{:S(2)}, u32[]{:S(2)}) collective-permute-start(bf16[512,384]{1,0:T(8,128)(2,1)S(1)} %collective-permute-done.8.refs_2_), channel_id=1, source_target_pairs={{0,1},{1,0},{2,3},{3,2},{4,5},{5,4},{6,7},{7,6},{8,9},{9,8},{10,11... | collective-permute-start | bytes 1179656 | tf_op jit(solution)/shard_map/ppermute | solution.py:497
  36.6 1.9 %collective-permute-start.14 = (bf16[192,384]{1,0:T(8,128)(2,1)S(1)}, bf16[192,384]{1,0:T(8,128)(2,1)S(1)}, u32[]{:S(2)}, u32[]{:S(2)}) collective-permute-start(bf16[192,384]{1,0:T(8,128)(2,1)S(1)} %get-tuple-element.22.refs_6_.refs_2_), channel_id=1, source_target_pairs={{0,1},{1,0},{2,3},{3,2},{4,5},{5,4},{6,7},{7,6},{8,9},{9,8},{10,11... | collective-permute-start | bytes 442376 | tf_op jit(solution)/shard_map/ppermute | solution.py:497
  37.2 1.3 %collective-permute-start.13 = (f32[32,640]{1,0:T(8,128)S(1)}, f32[32,640]{1,0:T(8,128)S(1)}, u32[]{:S(2)}, u32[]{:S(2)}) collective-permute-start(f32[32,640]{1,0:T(8,128)S(1)} %get-tuple-element.21.refs_4_.refs_0_), channel_id=1, source_target_pairs={{0,1},{1,0},{2,3},{3,2},{4,5},{5,4},{6,7},{7,6},{8,9},{9,8},{10,11... | collective-permute-start | bytes 245768 | tf_op jit(solution)/shard_map/ppermute | solution.py:497
  38.5 8.3 %collective-permute-start.15 = (bf16[80,384]{1,0:T(8,128)(2,1)S(1)}, bf16[80,384]{1,0:T(8,128)(2,1)S(1)}, u32[]{:S(2)}, u32[]{:S(2)}) collective-permute-start(bf16[80,384]{1,0:T(8,128)(2,1)S(1)} %shard_map.84.refs_0_), channel_id=1, source_target_pairs={{0,8},{8,0},{16,24},{24,16},{1,9},{9,1},{17,25},{25,17},{2,10},{10... | collective-permute-start | bytes 184328 | tf_op jit(solution)/shard_map/ppermute | solution.py:497
  40.0 6.7 %collective-permute-start.16 = (bf16[80,384]{1,0:T(8,128)(2,1)S(1)}, bf16[80,384]{1,0:T(8,128)(2,1)S(1)}, u32[]{:S(2)}, u32[]{:S(2)}) collective-permute-start(bf16[80,384]{1,0:T(8,128)(2,1)S(1)} %shard_map.84.refs_0_), channel_id=1, source_target_pairs={{0,16},{8,24},{16,0},{24,8},{1,17},{9,25},{17,1},{25,9},{2,18},{10... | collective-permute-start | bytes 184328 | tf_op jit(solution)/shard_map/ppermute | solution.py:497
  41.6 5.2 %collective-permute-start.17 = (bf16[80,384]{1,0:T(8,128)(2,1)S(1)}, bf16[80,384]{1,0:T(8,128)(2,1)S(1)}, u32[]{:S(2)}, u32[]{:S(2)}) collective-permute-start(bf16[80,384]{1,0:T(8,128)(2,1)S(1)} %shard_map.84.refs_0_), channel_id=1, source_target_pairs={{0,24},{8,16},{16,8},{24,0},{1,25},{9,17},{17,9},{25,1},{2,26},{10... | collective-permute-start | bytes 184328 | tf_op jit(solution)/shard_map/ppermute | solution.py:497

commit v3 on v2

--- a/solution.py
+++ b/solution.py
@@ -121,19 +121,17 @@
     return terms
 
 
-def halves(ref):
-    rows = ref.shape[0] // 2
-    return ref.at[:rows], ref.at[rows:]
+def next_refs(refs, rows):
+    near_rows = 2 * (rows // MIDDLE)
+    near = []
+    for low in range(2 * rows, refs[0].shape[0], near_rows):
+        near += [r.at[low : low + near_rows] for r in refs]
+    return [r.at[:rows] for r in refs], [r.at[rows : 2 * rows] for r in refs], near
 
 
 def key_value_refs(refs):
-    own, beside = halves(refs[0]), halves(refs[1])
-    rows = own[0].shape[0]
-    next_k = [r.at[:rows] for r in refs[2:4]]
-    near = []
-    for low in range(rows, refs[2].shape[0], 2 * (rows // MIDDLE)):
-        near += [r.at[low : low + 2 * (rows // MIDDLE)] for r in refs[2:4]]
-    return (own[0], beside[0], *next_k), (own[1], beside[1], *refs[4:6]), near
+    keys, values, near = next_refs(refs[4:], refs[0].shape[0])
+    return [refs[0], refs[2]] + keys, [refs[1], refs[3]] + values, near
 
 
 def chunks(refs, rows):
@@ -155,10 +153,46 @@
     out_ref[rows:, :] = second_ref[...]
 
 
-def forward_kernel(near_count, off_ref, qg_ref, spec_ref, own_near_ref, *refs):
-    k_refs, v_refs, near_refs = key_value_refs(refs[:KV_ARRAYS])
+def softmax_terms(scores, inners, weights, top, total, product):
+    new_top = top
+    for part in scores:
+        peak = jnp.max(part, axis=0, keepdims=True)
+        new_top = peak if new_top is None else jnp.maximum(new_top, peak)
+    if top is not None:
+        scale = jnp.exp(top - new_top)
+        total, product = total * scale, product * scale
+    for part, inner, weight in zip(scores, inners, weights):
+        probs = jnp.exp(part - new_top)
+        if weight is not None:
+            probs = probs * weight
+        part_total = jnp.sum(probs, axis=0, keepdims=True)
+        part_product = jnp.sum(probs * inner(), axis=0, keepdims=True)
+        total = part_total if total is None else total + part_total
+        product = part_product if product is None else product + part_product
+    return new_top, total, product
+
+
+def first_kernel(off_ref, q_ref, g_ref, *refs):
+    kv_refs, out_ref = refs[:-1], refs[-1]
+    rows, width = q_ref.shape
+    heads = width // HD
+    for head in range(heads):
+        lanes = pair_slice(head)
+        weight = pair_weights(rows, off_ref[head] % MIDDLE)
+        query = one_head(q_ref[:, lanes], head, SCALE)
+        grad = one_head(g_ref[:, lanes], head)
+        scores = [dot_nt(r[:, lanes], query) for r in kv_refs[::2]]
+        inners = [partial(lambda r: dot_nt(r[:, lanes], grad), r) for r in kv_refs[1::2]]
+        terms = softmax_terms(scores, inners, [weight] * len(scores), None, None, None)
+        for index, term in enumerate(terms):
+            row = index * heads + head
+            out_ref[row : row + 1, :] = term
+
+
+def forward_kernel(near_count, off_ref, q_ref, g_ref, known_ref, spec_ref, own_near_ref, *refs):
+    k_refs, v_refs, near_refs = next_refs(refs[:-2], q_ref.shape[0])
     out_ref, far_ref = refs[-2:]
-    rows, width = k_refs[0].shape
+    rows, width = q_ref.shape
     heads = width // HD
     log_sums, dots = [], []
     for head in range(heads):
@@ -166,28 +200,18 @@
         middle_offset = off_ref[head] % MIDDLE
         chosen = iota((1, rows), 1) % MIDDLE == middle_offset
         weight = pair_weights(rows, middle_offset)
-        query = one_head(qg_ref[:rows, lanes], head, SCALE)
-        grad = one_head(qg_ref[rows:, lanes], head)
+        query = one_head(q_ref[:, lanes], head, SCALE)
+        grad = one_head(g_ref[:, lanes], head)
         scores = [dot_nt(r[:, lanes], query) for r in k_refs]
-        top = jnp.max(scores[0], axis=0, keepdims=True)
-        for part in scores[1:]:
-            top = jnp.maximum(top, jnp.max(part, axis=0, keepdims=True))
+        inners = [partial(lambda r: dot_nt(r[:, lanes], grad), r) for r in v_refs]
+        weights = [weight] * len(scores)
         if near_count:
             far_scores = dot_nt(near_part(near_refs, 0, lanes), query)
-            far_scores = jnp.where(chosen, far_scores, LOW)
-            top = jnp.maximum(top, jnp.max(far_scores, axis=0, keepdims=True))
-        total = jnp.zeros((1, rows), F32)
-        product = jnp.zeros((1, rows), F32)
-        for part, v_ref in zip(scores, v_refs):
-            weights = jnp.exp(part - top) * weight
-            total = total + jnp.sum(weights, axis=0, keepdims=True)
-            inner = dot_nt(v_ref[:, lanes], grad)
-            product = product + jnp.sum(weights * inner, axis=0, keepdims=True)
-        if near_count:
-            weights = jnp.exp(far_scores - top)
-            total = total + jnp.sum(weights, axis=0, keepdims=True)
-            inner = dot_nt(near_part(near_refs, 1, lanes), grad)
-            product = product + jnp.sum(weights * inner, axis=0, keepdims=True)
+            scores.append(jnp.where(chosen, far_scores, LOW))
+            inners.append(lambda: dot_nt(near_part(near_refs, 1, lanes), grad))
+            weights.append(None)
+        known = [known_ref[i * heads + head : i * heads + head + 1, :] for i in range(3)]
+        top, total, product = softmax_terms(scores, inners, weights, *known)
         log_sums.append(top + jnp.log(total))
         dots.append(product / total)
     pad = jnp.zeros((STAT_ROWS - 2 * heads, rows), F32)
@@ -296,7 +320,7 @@
         spec_ref[spec_rows:, lanes] = result[full : full + spec_rows]
 
 
-def stack_kernel(*refs):
+def stack_kernel(first_ref, *refs):
     out, low = refs[-1], 0
     for ref in refs[:-1]:
         rows = ref.shape[0]
@@ -309,15 +333,14 @@
 
 
 def relay_kernel(first_ref, *refs):
-    pay_refs, far_refs, (pay_out, far_out) = refs[:2], refs[2:-2], refs[-2:]
-    for parts, out in ((pay_refs, pay_out), (far_refs, far_out)):
+    qg_ref, pay_refs, far_refs = refs[0], refs[1:3], refs[3:-3]
+    for parts, out in zip(((qg_ref,), pay_refs, far_refs), refs[-3:]):
         for index, ref in enumerate(parts):
             rows = ref.shape[0]
             out[index * rows : (index + 1) * rows, :] = ref[...]
 
 
-def key_kernel(near_count, off_ref, kv_ref, *refs):
-    k_ref, v_ref = halves(kv_ref)
+def key_kernel(near_count, off_ref, k_ref, v_ref, *refs):
     qg_refs = refs[:GROUP]
     pay_refs = chunks(refs[GROUP : GROUP + 2], STAT_ROWS)
     far_refs = far_chunks(k_ref.shape[0], refs[GROUP + 2 : -2])
@@ -393,8 +416,7 @@
         out_ref[kind * count : (kind + 1) * count, :] = jnp.concatenate(lines, axis=0).astype(BF16)
 
 
-def special_kernel(slots, off_ref, kv_ref, dq_in, spec_ref, dk_in, dv_in, *refs):
-    k_ref, v_ref = halves(kv_ref)
+def special_kernel(slots, off_ref, k_ref, v_ref, dq_in, spec_ref, dk_in, dv_in, *refs):
     blocks = refs[:-3]
     dq_ref, dk_ref, dv_ref = refs[-3:]
     rows, width = k_ref.shape
@@ -504,6 +526,7 @@
     near_rows, spec_rows = rows // MIDDLE, rows // UPPER
 
     next_k, next_v = across(key_matrix, "ctxb", 2), across(value_matrix, "ctxb", 2)
+    core_k, core_v = across(key_matrix, "ctxb", 1), across(value_matrix, "ctxb", 1)
     near_kv, near_qg, spec = call(
         pack_kernel,
         [
@@ -522,14 +545,18 @@
     )
     near_came = [across(near_kv, "ctxb", mask) for mask in range(GROUP, slots, 2)]
     both = [((2 * rows, width), BF16)]
-    (kv,) = call(merge_kernel, both, key_matrix, value_matrix, near_kv, us=0.3)
+    own_kv = [key_matrix, value_matrix, core_k, core_v]
+    term_rows = -(-3 * (width // HD) // 8) * 8
+    (known,) = call(
+        first_kernel, [((term_rows, rows), F32)],
+        offsets, queries, grad_out, *own_kv, us=2.2,
+    )
     (stacked,) = call(
         stack_kernel,
-        [((rows + 2 * near_rows * len(near_came), width), BF16)],
-        next_k, *near_came, us=0.2,
-    )
-    kv_parts = [kv, across(kv, "ctxb", 1), stacked, across(stacked, "ctxb", 1)]
-    kv_parts += [next_v, across(next_v, "ctxb", 1)]
+        [((2 * rows + 2 * near_rows * len(near_came), width), BF16)],
+        known, next_k, next_v, *near_came, us=0.2,
+    )
+    kv_parts = own_kv + [stacked, across(stacked, "ctxb", 1)]
     (qg,) = call(merge_kernel, both, queries, grad_out, stacked, us=0.3)
     next_qg = across(qg, "ctxb", 2)
     core_qg = across(qg, "ctxb", 1)
@@ -539,7 +566,7 @@
             ((STAT_ROWS, rows + width), F32),
             ((2 * near_rows + 2 * STAT_ROWS, width), BF16),
         ],
-        offsets, qg, spec, near_qg, *kv_parts, us=4.7,
+        offsets, queries, grad_out, known, spec, near_qg, *kv_parts[4:], us=2.5,
     )
     dq, dq_spec = call(
         partial(query_kernel, near_count),
@@ -550,12 +577,15 @@
     far_came = [across(far, "ctxb", mask) for mask in range(GROUP, slots, 2)]
     held = call(
         relay_kernel,
-        [((2 * STAT_ROWS, rows + width), F32)]
-        + [((far.shape[0] * len(far_came), width), BF16)],
-        dq_spec, *pays_far, *far_came, us=0.2,
-    )
-    pays, fars = [(part, across(part, "ctxb", 1)) for part in held]
-    qg_parts = [qg, core_qg, next_qg, across(next_qg, "ctxb", 1)]
+        [
+            ((2 * rows, width), BF16),
+            ((2 * STAT_ROWS, rows + width), F32),
+            ((far.shape[0] * len(far_came), width), BF16),
+        ],
+        dq_spec, next_qg, *pays_far, *far_came, us=0.3,
+    )
+    next_qgs, pays, fars = [(part, across(part, "ctxb", 1)) for part in held]
+    qg_parts = [qg, core_qg, *next_qgs]
     (block,) = call(
         partial(collect_kernel, rows), [((5 * slots * spec_rows, width), BF16)], *pays, *fars,
         us=0.3,
@@ -564,12 +594,12 @@
     dk, dv = call(
         partial(key_kernel, near_count),
         [((rows, width), F32), ((rows, width), F32)],
-        offsets, kv, *qg_parts, *pays, *fars, us=5.0,
+        offsets, key_matrix, value_matrix, *qg_parts, *pays, *fars, us=5.0,
     )
     return call(
         partial(special_kernel, slots),
         [((rows, width), BF16)] * 3,
-        offsets, kv, dq, dq_spec, dk, dv, *blocks, us=3.0,
+        offsets, key_matrix, value_matrix, dq, dq_spec, dk, dv, *blocks, us=3.0,
     )
 
 

time: 49.8 us -> 47.5 us (0.954)
  waiting for transfers between devices: 12.3 us -> 10.8 us
  local copies, waits for them, and re-layouts: 1.47 us -> 0.04 us
    ppermute x18, waiting for transfers between devices: 12.3 us -> 10.8 us  [across(): lax.ppermute(value, axis, [(source, source ^ mask) for source in range(si...]
    unnamed x16 -> x14, local copies, waits for them, and re-layouts: 1.47 us -> 0.04 us
  transfers between devices with their start and end apart: 18 -> 18, of which waited for: 5 -> 6; matrix products, arithmetic and copies ran while one was open for 0% -> 0% of each run, Pallas kernels for 32% -> 34%
where the time goes in v3:
time: 47.5 us; the launch traced here: 47.4 us
  Pallas kernels  19.2 us (40%)
  starting transfers between devices  16.5 us (35%)
  waiting for transfers between devices  10.8 us (23%)
  between operations  0.82 us (2%)
    pallas_call x10, Pallas kernels, call(): pl.pallas_call(kernel, out_shape=tuple((jax.ShapeDtypeStruct(shape, dtype...  19.2 us
    ppermute x18, starting transfers between devices, across(): lax.ppermute(value, axis, [(source, source ^ mask) for source in range(si...  16.5 us
    ppermute x18, waiting for transfers between devices, across(): lax.ppermute(value, axis, [(source, source ^ mask) for source in range(si...  10.8 us
  transfers between devices with their start and end apart: 18, of which 6 were waited for; matrix products, arithmetic and copies ran while one was open for 0% of the time, Pallas kernels for 34%

profile of v3, /device:TPU:0, one launch (start us, length us, event | category | flops | bytes accessed | tf_op | source)
XLA Modules:
  0.0 47.4 jit_solution(6439752083477720670)
XLA Ops:
  0.7 0.5 %collective-permute-start = (bf16[256,384]{1,0:T(8,128)(2,1)}, bf16[256,384]{1,0:T(8,128)(2,1)S(1)}, u32[]{:S(2)}, u32[]{:S(2)}) collective-permute-start(bf16[256,384]{1,0:T(8,128)(2,1)} %k_ref.5), channel_id=1, source_target_pairs={{0,1},{1,0},{2,3},{3,2},{4,5},{5,4},{6,7},{7,6},{8,9},{9,8},{10,11... | collective-permute-start | bytes 589832 | tf_op jit(solution)/shard_map/ppermute | solution.py:519
  1.2 0.1 collective-permute-start.1
  1.3 3.0 %collective-permute-start.2 = (bf16[256,384]{1,0:T(8,128)(2,1)}, bf16[256,384]{1,0:T(8,128)(2,1)S(1)}, u32[]{:S(2)}, u32[]{:S(2)}) collective-permute-start(bf16[256,384]{1,0:T(8,128)(2,1)} %k_ref.5), channel_id=1, source_target_pairs={{0,2},{1,3},{2,0},{3,1},{4,6},{5,7},{6,4},{7,5},{8,10},{9,11},{10,... | collective-permute-start | bytes 589832 | tf_op jit(solution)/shard_map/ppermute | solution.py:519
  4.3 0.0 collective-permute-start.3
  4.3 2.3 %shard_map.77 = (bf16[64,384]{1,0:T(8,128)(2,1)}, bf16[64,384]{1,0:T(8,128)(2,1)}, bf16[64,384]{1,0:T(8,128)(2,1)}) custom-call(s32[6]{0:T(128)} %off_ref.9, bf16[256,384]{1,0:T(8,128)(2,1)} %q_ref.5, bf16[256,384]{1,0:T(8,128)(2,1)} %k_ref.5, bf16[256,384]{1,0:T(8,128)(2,1)} %v_ref.5, bf16[256,384]{1,0:T(8,128)(2,1)} %g_ref.5), custom_call_target="tpu_custom_call" | custom-call | flops 1495000064 | tf_op jit(solution)/shard_map/pallas_call | solution.py:504
  6.6 0.0 copy-start.4
  6.6 3.1 %collective-permute-start.4 = (bf16[64,384]{1,0:T(8,128)(2,1)}, bf16[64,384]{1,0:T(8,128)(2,1)S(1)}, u32[]{:S(2)}, u32[]{:S(2)}) collective-permute-start(bf16[64,384]{1,0:T(8,128)(2,1)} %get-tuple-element.15), channel_id=1, source_target_pairs={{0,4},{1,5},{2,6},{3,7},{4,0},{5,1},{6,2},{7,3},{8,12},{9,13},{10,... | collective-permute-start | bytes 147464 | tf_op jit(solution)/shard_map/ppermute | solution.py:519
  9.7 1.3 %collective-permute-start.5 = (bf16[64,384]{1,0:T(8,128)(2,1)}, bf16[64,384]{1,0:T(8,128)(2,1)S(1)}, u32[]{:S(2)}, u32[]{:S(2)}) collective-permute-start(bf16[64,384]{1,0:T(8,128)(2,1)} %get-tuple-element.15), channel_id=1, source_target_pairs={{0,6},{1,7},{2,4},{3,5},{4,2},{5,3},{6,0},{7,1},{8,14},{9,15},{10,... | collective-permute-start | bytes 147464 | tf_op jit(solution)/shard_map/ppermute | solution.py:519
  11.0 1.9 %shard_map.76.first_ref.known_ref = f32[24,256]{1,0:T(8,128)S(1)} custom-call(s32[6]{0:T(128)S(1)} %copy-done.4, bf16[256,384]{1,0:T(8,128)(2,1)S(1)} %copy-done, bf16[256,384]{1,0:T(8,128)(2,1)S(1)} %copy-done.1, bf16[256,384]{1,0:T(8,128)(2,1)S(1)} %copy-done.2, bf16[256,384]{1,0:T(8,128)(2,1)S(1)} %copy-done.3, ...), custom_call_target="tpu_custom_call" | custom-call | flops 2529999872 | tf_op jit(solution)/shard_map/pallas_call | solution.py:504
  13.0 1.8 %collective-permute-done.4.refs_2_ = bf16[64,384]{1,0:T(8,128)(2,1)S(1)} collective-permute-done((bf16[64,384]{1,0:T(8,128)(2,1)}, bf16[64,384]{1,0:T(8,128)(2,1)S(1)}, u32[]{:S(2)}, u32[]{:S(2)}) %collective-permute-start.4) | collective-permute-done | bytes 49184 | tf_op jit(solution)/shard_map/ppermute | solution.py:519
  14.8 3.4 %collective-permute-done.5.refs_3_ = bf16[64,384]{1,0:T(8,128)(2,1)S(1)} collective-permute-done((bf16[64,384]{1,0:T(8,128)(2,1)}, bf16[64,384]{1,0:T(8,128)(2,1)S(1)}, u32[]{:S(2)}, u32[]{:S(2)}) %collective-permute-start.5) | collective-permute-done | bytes 49184 | tf_op jit(solution)/shard_map/ppermute | solution.py:519
  18.2 0.1 collective-permute-start.6
  18.3 0.6 %collective-permute-start.7 = (bf16[512,384]{1,0:T(8,128)(2,1)S(1)}, bf16[512,384]{1,0:T(8,128)(2,1)S(1)}, u32[]{:S(2)}, u32[]{:S(2)}) collective-permute-start(bf16[512,384]{1,0:T(8,128)(2,1)S(1)} %shard_map.79.qg_ref.refs_0_), channel_id=1, source_target_pairs={{0,1},{1,0},{2,3},{3,2},{4,5},{5,4},{6,7},{7,6},{8,9},{9,8},{10,11... | collective-permute-start | bytes 1179656 | tf_op jit(solution)/shard_map/ppermute | solution.py:519
  18.9 0.0 collective-permute-start.8
  18.9 1.2 %collective-permute-done.6.refs_1_.refs_5_ = bf16[640,384]{1,0:T(8,128)(2,1)S(1)} collective-permute-done((bf16[640,384]{1,0:T(8,128)(2,1)S(1)}, bf16[640,384]{1,0:T(8,128)(2,1)S(1)}, u32[]{:S(2)}, u32[]{:S(2)}) %collective-permute-start.6) | collective-permute-done | bytes 491552 | tf_op jit(solution)/shard_map/ppermute | solution.py:519
  20.1 2.7 %shard_map.80 = (f32[16,640]{1,0:T(8,128)S(1)}, bf16[96,384]{1,0:T(8,128)(2,1)S(1)}) custom-call(s32[6]{0:T(128)S(1)} %copy-done.4, bf16[256,384]{1,0:T(8,128)(2,1)S(1)} %copy-done, bf16[256,384]{1,0:T(8,128)(2,1)S(1)} %copy-done.1, f32[24,256]{1,0:T(8,128)S(1)} %shard_map.76.first_ref.known_ref, bf16[64,384]{1,0:T(8,128)(2,1)S(1)} %copy-done.5, ...), custom_call_target="tpu_custom_call" | custom-call | flops 2875000064 | tf_op jit(solution)/shard_map/pallas_call | solution.py:504
  22.8 1.0 %collective-permute-start.10 = (bf16[96,384]{1,0:T(8,128)(2,1)S(1)}, bf16[96,384]{1,0:T(8,128)(2,1)S(1)}, u32[]{:S(2)}, u32[]{:S(2)}) collective-permute-start(bf16[96,384]{1,0:T(8,128)(2,1)S(1)} %get-tuple-element.21), channel_id=1, source_target_pairs={{0,4},{1,5},{2,6},{3,7},{4,0},{5,1},{6,2},{7,3},{8,12},{9,13},{10,... | collective-permute-start | bytes 221192 | tf_op jit(solution)/shard_map/ppermute | solution.py:519
  23.8 2.2 %collective-permute-start.11 = (bf16[96,384]{1,0:T(8,128)(2,1)S(1)}, bf16[96,384]{1,0:T(8,128)(2,1)S(1)}, u32[]{:S(2)}, u32[]{:S(2)}) collective-permute-start(bf16[96,384]{1,0:T(8,128)(2,1)S(1)} %get-tuple-element.21), channel_id=1, source_target_pairs={{0,6},{1,7},{2,4},{3,5},{4,2},{5,3},{6,0},{7,1},{8,14},{9,15},{10,... | collective-permute-start | bytes 221192 | tf_op jit(solution)/shard_map/ppermute | solution.py:519
  26.1 0.3 collective-permute-start.9
  26.4 4.6 %shard_map.81 = (f32[256,384]{1,0:T(8,128)S(1)}, f32[4,384]{1,0:T(4,128)S(1)}) custom-call(s32[6]{0:T(128)S(1)} %copy-done.4, bf16[512,384]{1,0:T(8,128)(2,1)S(1)} %shard_map.79.qg_ref.refs_0_, bf16[64,384]{1,0:T(8,128)(2,1)S(1)} %copy-done.5, f32[16,640]{1,0:T(8,128)S(1)} %get-tuple-element.18.pay_ref.refs_1_, bf16[256,384]{1,0:T(8,128)(2,1)S(1)} %copy-done.2, ...), custom_call_target="tpu_custom_call" | custom-call | flops 5750000128 | tf_op jit(solution)/shard_map/pallas_call | solution.py:504
  31.1 2.5 %collective-permute-done.8.refs_0_ = bf16[512,384]{1,0:T(8,128)(2,1)S(1)} collective-permute-done((bf16[512,384]{1,0:T(8,128)(2,1)S(1)}, bf16[512,384]{1,0:T(8,128)(2,1)S(1)}, u32[]{:S(2)}, u32[]{:S(2)}) %collective-permute-start.8) | collective-permute-done | bytes 393248 | tf_op jit(solution)/shard_map/ppermute | solution.py:519
  33.6 0.4 collective-permute-done.9.refs_2_
  34.0 0.1 shard_map.82
  34.1 0.1 collective-permute-start.12
  34.2 0.5 %collective-permute-start.14 = (bf16[192,384]{1,0:T(8,128)(2,1)S(1)}, bf16[192,384]{1,0:T(8,128)(2,1)S(1)}, u32[]{:S(2)}, u32[]{:S(2)}) collective-permute-start(bf16[192,384]{1,0:T(8,128)(2,1)S(1)} %get-tuple-element.24.refs_6_.refs_2_), channel_id=1, source_target_pairs={{0,1},{1,0},{2,3},{3,2},{4,5},{5,4},{6,7},{7,6},{8,9},{9,8},{10,11... | collective-permute-start | bytes 442376 | tf_op jit(solution)/shard_map/ppermute | solution.py:519
  34.7 0.1 collective-permute-start.13
  34.8 1.5 %collective-permute-done.13.refs_5_.refs_1_ = f32[32,640]{1,0:T(8,128)S(1)} collective-permute-done((f32[32,640]{1,0:T(8,128)S(1)}, f32[32,640]{1,0:T(8,128)S(1)}, u32[]{:S(2)}, u32[]{:S(2)}) %collective-permute-start.13) | collective-permute-done | bytes 81952 | tf_op jit(solution)/shard_map/ppermute | solution.py:519
  36.3 1.6 %collective-permute-start.15 = (bf16[80,384]{1,0:T(8,128)(2,1)S(1)}, bf16[80,384]{1,0:T(8,128)(2,1)S(1)}, u32[]{:S(2)}, u32[]{:S(2)}) collective-permute-start(bf16[80,384]{1,0:T(8,128)(2,1)S(1)} %shard_map.84.refs_0_), channel_id=1, source_target_pairs={{0,8},{8,0},{16,24},{24,16},{1,9},{9,1},{17,25},{25,17},{2,10},{10... | collective-permute-start | bytes 184328 | tf_op jit(solution)/shard_map/ppermute | solution.py:519
  37.8 1.5 %collective-permute-start.16 = (bf16[80,384]{1,0:T(8,128)(2,1)S(1)}, bf16[80,384]{1,0:T(8,128)(2,1)S(1)}, u32[]{:S(2)}, u32[]{:S(2)}) collective-permute-start(bf16[80,384]{1,0:T(8,128)(2,1)S(1)} %shard_map.84.refs_0_), channel_id=1, source_target_pairs={{0,16},{8,24},{16,0},{24,8},{1,17},{9,25},{17,1},{25,9},{2,18},{10... | collective-permute-start | bytes 184328 | tf_op jit(solution)/shard_map/ppermute | solution.py:519
  39.3 0.5 %collective-permute-start.17 = (bf16[80,384]{1,0:T(8,128)(2,1)S(1)}, bf16[80,384]{1,0:T(8,128)(2,1)S(1)}, u32[]{:S(2)}, u32[]{:S(2)}) collective-permute-start(bf16[80,384]{1,0:T(8,128)(2,1)S(1)} %shard_map.84.refs_0_), channel_id=1, source_target_pairs={{0,24},{8,16},{16,8},{24,0},{1,25},{9,17},{17,9},{25,1},{2,26},{10... | collective-permute-start | bytes 184328 | tf_op jit(solution)/shard_map/ppermute | solution.py:519
  39.8 4.7 %shard_map.83 = (f32[256,384]{1,0:T(8,128)S(1)}, f32[256,384]{1,0:T(8,128)S(1)}) custom-call(s32[6]{0:T(128)S(1)} %copy-done.4, bf16[256,384]{1,0:T(8,128)(2,1)S(1)} %copy-done.2, bf16[256,384]{1,0:T(8,128)(2,1)S(1)} %copy-done.3, bf16[512,384]{1,0:T(8,128)(2,1)S(1)} %shard_map.79.qg_ref.refs_0_, bf16[512,384]{1,0:T(8,128)(2,1)S(1)} %collective-permute-done.7.refs_1_, ...), custom_call_target="tpu_custom_call" | custom-call | flops 5750000128 | tf_op jit(solution)/shard_map/pallas_call | solution.py:504
  44.5 2.9 %shard_map.85 = (bf16[256,384]{1,0:T(8,128)(2,1)}, bf16[256,384]{1,0:T(8,128)(2,1)}, bf16[256,384]{1,0:T(8,128)(2,1)}) custom-call(s32[6]{0:T(128)S(1)} %copy-done.4, bf16[256,384]{1,0:T(8,128)(2,1)S(1)} %copy-done.2, bf16[256,384]{1,0:T(8,128)(2,1)S(1)} %copy-done.3, f32[256,384]{1,0:T(8,128)S(1)} %get-tuple-element.19.dq_in, ...), custom_call_target="tpu_custom_call" | custom-call | flops 3449999872 | tf_op jit(solution)/shard_map/pallas_call | solution.py:504
  (28 shorter events, 0.2 us)
Async XLA Ops:
  0.6 10.4 %copy-start.2 = (bf16[256,384]{1,0:T(8,128)(2,1)S(1)}, bf16[256,384]{1,0:T(8,128)(2,1)}, u32[]{:S(2)}) copy-start(bf16[256,384]{1,0:T(8,128)(2,1)} %k_ref.5) | copy-start | bytes 589828
  0.6 10.4 %copy-start.3 = (bf16[256,384]{1,0:T(8,128)(2,1)S(1)}, bf16[256,384]{1,0:T(8,128)(2,1)}, u32[]{:S(2)}) copy-start(bf16[256,384]{1,0:T(8,128)(2,1)} %v_ref.5) | copy-start | bytes 589828
  0.7 10.4 %copy-start = (bf16[256,384]{1,0:T(8,128)(2,1)S(1)}, bf16[256,384]{1,0:T(8,128)(2,1)}, u32[]{:S(2)}) copy-start(bf16[256,384]{1,0:T(8,128)(2,1)} %q_ref.5) | copy-start | bytes 589828
  0.7 10.4 %copy-start.1 = (bf16[256,384]{1,0:T(8,128)(2,1)S(1)}, bf16[256,384]{1,0:T(8,128)(2,1)}, u32[]{:S(2)}) copy-start(bf16[256,384]{1,0:T(8,128)(2,1)} %g_ref.5) | copy-start | bytes 589828
  0.7 9.0 %collective-permute-start = (bf16[256,384]{1,0:T(8,128)(2,1)}, bf16[256,384]{1,0:T(8,128)(2,1)S(1)}, u32[]{:S(2)}, u32[]{:S(2)}) collective-permute-start(bf16[256,384]{1,0:T(8,128)(2,1)} %k_ref.5), channel_id=1, source_target_pairs={{0,1},{1,0},{2,3},{3,2},{4,5},{5,4},{6,7},{7,6},{8,9},{9,8},{10,11... | collective-permute-start | bytes 589832 | tf_op jit(solution)/shard_map/ppermute | solution.py:519
  1.2 9.8 %collective-permute-start.1 = (bf16[256,384]{1,0:T(8,128)(2,1)}, bf16[256,384]{1,0:T(8,128)(2,1)S(1)}, u32[]{:S(2)}, u32[]{:S(2)}) collective-permute-start(bf16[256,384]{1,0:T(8,128)(2,1)} %v_ref.5), channel_id=1, source_target_pairs={{0,1},{1,0},{2,3},{3,2},{4,5},{5,4},{6,7},{7,6},{8,9},{9,8},{10,11... | collective-permute-start | bytes 589832 | tf_op jit(solution)/shard_map/ppermute | solution.py:519
  1.3 16.9 %collective-permute-start.2 = (bf16[256,384]{1,0:T(8,128)(2,1)}, bf16[256,384]{1,0:T(8,128)(2,1)S(1)}, u32[]{:S(2)}, u32[]{:S(2)}) collective-permute-start(bf16[256,384]{1,0:T(8,128)(2,1)} %k_ref.5), channel_id=1, source_target_pairs={{0,2},{1,3},{2,0},{3,1},{4,6},{5,7},{6,4},{7,5},{8,10},{9,11},{10,... | collective-permute-start | bytes 589832 | tf_op jit(solution)/shard_map/ppermute | solution.py:519
  4.3 13.9 %collective-permute-start.3 = (bf16[256,384]{1,0:T(8,128)(2,1)}, bf16[256,384]{1,0:T(8,128)(2,1)S(1)}, u32[]{:S(2)}, u32[]{:S(2)}) collective-permute-start(bf16[256,384]{1,0:T(8,128)(2,1)} %v_ref.5), channel_id=1, source_target_pairs={{0,2},{1,3},{2,0},{3,1},{4,6},{5,7},{6,4},{7,5},{8,10},{9,11},{10,... | collective-permute-start | bytes 589832 | tf_op jit(solution)/shard_map/ppermute | solution.py:519
  6.6 4.5 %copy-start.4 = (s32[6]{0:T(128)S(1)}, s32[6]{0:T(128)}, u32[]{:S(2)}) copy-start(s32[6]{0:T(128)} %off_ref.9) | copy-start | bytes 76
  6.6 8.2 %collective-permute-start.4 = (bf16[64,384]{1,0:T(8,128)(2,1)}, bf16[64,384]{1,0:T(8,128)(2,1)S(1)}, u32[]{:S(2)}, u32[]{:S(2)}) collective-permute-start(bf16[64,384]{1,0:T(8,128)(2,1)} %get-tuple-element.15), channel_id=1, source_target_pairs={{0,4},{1,5},{2,6},{3,7},{4,0},{5,1},{6,2},{7,3},{8,12},{9,13},{10,... | collective-permute-start | bytes 147464 | tf_op jit(solution)/shard_map/ppermute | solution.py:519
  9.7 8.5 %collective-permute-start.5 = (bf16[64,384]{1,0:T(8,128)(2,1)}, bf16[64,384]{1,0:T(8,128)(2,1)S(1)}, u32[]{:S(2)}, u32[]{:S(2)}) collective-permute-start(bf16[64,384]{1,0:T(8,128)(2,1)} %get-tuple-element.15), channel_id=1, source_target_pairs={{0,6},{1,7},{2,4},{3,5},{4,2},{5,3},{6,0},{7,1},{8,14},{9,15},{10,... | collective-permute-start | bytes 147464 | tf_op jit(solution)/shard_map/ppermute | solution.py:519
  18.2 2.0 %copy-start.5 = (bf16[64,384]{1,0:T(8,128)(2,1)S(1)}, bf16[64,384]{1,0:T(8,128)(2,1)}, u32[]{:S(2)}) copy-start(bf16[64,384]{1,0:T(8,128)(2,1)} %get-tuple-element.16.spec_ref.spec_in) | copy-start | bytes 147460
  18.2 1.9 %copy-start.6 = (bf16[64,384]{1,0:T(8,128)(2,1)S(1)}, bf16[64,384]{1,0:T(8,128)(2,1)}, u32[]{:S(2)}) copy-start(bf16[64,384]{1,0:T(8,128)(2,1)} %get-tuple-element.17.own_near_ref) | copy-start | bytes 147460
  18.2 1.9 %collective-permute-start.6 = (bf16[640,384]{1,0:T(8,128)(2,1)S(1)}, bf16[640,384]{1,0:T(8,128)(2,1)S(1)}, u32[]{:S(2)}, u32[]{:S(2)}) collective-permute-start(bf16[640,384]{1,0:T(8,128)(2,1)S(1)} %shard_map.78._.refs_0_.refs_4_), channel_id=1, source_target_pairs={{0,1},{1,0},{2,3},{3,2},{4,5},{5,4},{6,7},{7,6},{8,9},{9,8},{10,11... | collective-permute-start | bytes 1474568 | tf_op jit(solution)/shard_map/ppermute | solution.py:519
  18.3 21.5 %collective-permute-start.7 = (bf16[512,384]{1,0:T(8,128)(2,1)S(1)}, bf16[512,384]{1,0:T(8,128)(2,1)S(1)}, u32[]{:S(2)}, u32[]{:S(2)}) collective-permute-start(bf16[512,384]{1,0:T(8,128)(2,1)S(1)} %shard_map.79.qg_ref.refs_0_), channel_id=1, source_target_pairs={{0,1},{1,0},{2,3},{3,2},{4,5},{5,4},{6,7},{7,6},{8,9},{9,8},{10,11... | collective-permute-start | bytes 1179656 | tf_op jit(solution)/shard_map/ppermute | solution.py:519
  18.9 14.7 %collective-permute-start.8 = (bf16[512,384]{1,0:T(8,128)(2,1)S(1)}, bf16[512,384]{1,0:T(8,128)(2,1)S(1)}, u32[]{:S(2)}, u32[]{:S(2)}) collective-permute-start(bf16[512,384]{1,0:T(8,128)(2,1)S(1)} %shard_map.79.qg_ref.refs_0_), channel_id=1, source_target_pairs={{0,2},{1,3},{2,0},{3,1},{4,6},{5,7},{6,4},{7,5},{8,10},{9,11},{10,... | collective-permute-start | bytes 1179656 | tf_op jit(solution)/shard_map/ppermute | solution.py:519
  22.8 11.2 %collective-permute-start.10 = (bf16[96,384]{1,0:T(8,128)(2,1)S(1)}, bf16[96,384]{1,0:T(8,128)(2,1)S(1)}, u32[]{:S(2)}, u32[]{:S(2)}) collective-permute-start(bf16[96,384]{1,0:T(8,128)(2,1)S(1)} %get-tuple-element.21), channel_id=1, source_target_pairs={{0,4},{1,5},{2,6},{3,7},{4,0},{5,1},{6,2},{7,3},{8,12},{9,13},{10,... | collective-permute-start | bytes 221192 | tf_op jit(solution)/shard_map/ppermute | solution.py:519
  23.8 10.2 %collective-permute-start.11 = (bf16[96,384]{1,0:T(8,128)(2,1)S(1)}, bf16[96,384]{1,0:T(8,128)(2,1)S(1)}, u32[]{:S(2)}, u32[]{:S(2)}) collective-permute-start(bf16[96,384]{1,0:T(8,128)(2,1)S(1)} %get-tuple-element.21), channel_id=1, source_target_pairs={{0,6},{1,7},{2,4},{3,5},{4,2},{5,3},{6,0},{7,1},{8,14},{9,15},{10,... | collective-permute-start | bytes 221192 | tf_op jit(solution)/shard_map/ppermute | solution.py:519
  26.1 8.0 %collective-permute-start.9 = (f32[16,640]{1,0:T(8,128)S(1)}, f32[16,640]{1,0:T(8,128)S(1)}, u32[]{:S(2)}, u32[]{:S(2)}) collective-permute-start(f32[16,640]{1,0:T(8,128)S(1)} %get-tuple-element.18.pay_ref.refs_1_), channel_id=1, source_target_pairs={{0,2},{1,3},{2,0},{3,1},{4,6},{5,7},{6,4},{7,5},{8,10},{9,11},{10,... | collective-permute-start | bytes 122888 | tf_op jit(solution)/shard_map/ppermute | solution.py:519
  34.1 5.7 %collective-permute-start.12 = (bf16[512,384]{1,0:T(8,128)(2,1)S(1)}, bf16[512,384]{1,0:T(8,128)(2,1)S(1)}, u32[]{:S(2)}, u32[]{:S(2)}) collective-permute-start(bf16[512,384]{1,0:T(8,128)(2,1)S(1)} %get-tuple-element.22.refs_2_), channel_id=1, source_target_pairs={{0,1},{1,0},{2,3},{3,2},{4,5},{5,4},{6,7},{7,6},{8,9},{9,8},{10,11... | collective-permute-start | bytes 1179656 | tf_op jit(solution)/shard_map/ppermute | solution.py:519
  34.2 2.0 %collective-permute-start.14 = (bf16[192,384]{1,0:T(8,128)(2,1)S(1)}, bf16[192,384]{1,0:T(8,128)(2,1)S(1)}, u32[]{:S(2)}, u32[]{:S(2)}) collective-permute-start(bf16[192,384]{1,0:T(8,128)(2,1)S(1)} %get-tuple-element.24.refs_6_.refs_2_), channel_id=1, source_target_pairs={{0,1},{1,0},{2,3},{3,2},{4,5},{5,4},{6,7},{7,6},{8,9},{9,8},{10,11... | collective-permute-start | bytes 442376 | tf_op jit(solution)/shard_map/ppermute | solution.py:519
  34.7 1.5 %collective-permute-start.13 = (f32[32,640]{1,0:T(8,128)S(1)}, f32[32,640]{1,0:T(8,128)S(1)}, u32[]{:S(2)}, u32[]{:S(2)}) collective-permute-start(f32[32,640]{1,0:T(8,128)S(1)} %get-tuple-element.23.refs_4_.refs_0_), channel_id=1, source_target_pairs={{0,1},{1,0},{2,3},{3,2},{4,5},{5,4},{6,7},{7,6},{8,9},{9,8},{10,11... | collective-permute-start | bytes 245768 | tf_op jit(solution)/shard_map/ppermute | solution.py:519
  36.3 8.2 %collective-permute-start.15 = (bf16[80,384]{1,0:T(8,128)(2,1)S(1)}, bf16[80,384]{1,0:T(8,128)(2,1)S(1)}, u32[]{:S(2)}, u32[]{:S(2)}) collective-permute-start(bf16[80,384]{1,0:T(8,128)(2,1)S(1)} %shard_map.84.refs_0_), channel_id=1, source_target_pairs={{0,8},{8,0},{16,24},{24,16},{1,9},{9,1},{17,25},{25,17},{2,10},{10... | collective-permute-start | bytes 184328 | tf_op jit(solution)/shard_map/ppermute | solution.py:519
  37.8 6.7 %collective-permute-start.16 = (bf16[80,384]{1,0:T(8,128)(2,1)S(1)}, bf16[80,384]{1,0:T(8,128)(2,1)S(1)}, u32[]{:S(2)}, u32[]{:S(2)}) collective-permute-start(bf16[80,384]{1,0:T(8,128)(2,1)S(1)} %shard_map.84.refs_0_), channel_id=1, source_target_pairs={{0,16},{8,24},{16,0},{24,8},{1,17},{9,25},{17,1},{25,9},{2,18},{10... | collective-permute-start | bytes 184328 | tf_op jit(solution)/shard_map/ppermute | solution.py:519
  39.3 5.2 %collective-permute-start.17 = (bf16[80,384]{1,0:T(8,128)(2,1)S(1)}, bf16[80,384]{1,0:T(8,128)(2,1)S(1)}, u32[]{:S(2)}, u32[]{:S(2)}) collective-permute-start(bf16[80,384]{1,0:T(8,128)(2,1)S(1)} %shard_map.84.refs_0_), channel_id=1, source_target_pairs={{0,24},{8,16},{16,8},{24,0},{1,25},{9,17},{17,9},{25,1},{2,26},{10... | collective-permute-start | bytes 184328 | tf_op jit(solution)/shard_map/ppermute | solution.py:519

commit v4 on v3

--- a/solution.py
+++ b/solution.py
@@ -63,11 +63,17 @@
     return out
 
 
-def pair_weights(rows, middle_offset):
-    both = (iota((rows, rows), 0) % MIDDLE == middle_offset) & (
-        iota((rows, rows), 1) % MIDDLE == middle_offset
+def pair_weights(columns, middle_offset):
+    both = (iota((MIDDLE, columns), 0) == middle_offset) & (
+        iota((MIDDLE, columns), 1) % MIDDLE == middle_offset
     )
     return jnp.where(both, 2.0, 1.0)
+
+
+def weighted(probs, weight):
+    rows, columns = probs.shape
+    tiles = probs.reshape(rows // MIDDLE, MIDDLE, columns)
+    return (tiles * weight[None]).reshape(rows, columns)
 
 
 def pack_kernel(
@@ -164,7 +170,7 @@
     for part, inner, weight in zip(scores, inners, weights):
         probs = jnp.exp(part - new_top)
         if weight is not None:
-            probs = probs * weight
+            probs = weighted(probs, weight)
         part_total = jnp.sum(probs, axis=0, keepdims=True)
         part_product = jnp.sum(probs * inner(), axis=0, keepdims=True)
         total = part_total if total is None else total + part_total
@@ -292,15 +298,18 @@
             middle_offset = off_ref[head] % MIDDLE
             row = iota((full, 1), 0)
             chosen = (row % MIDDLE == middle_offset) | (row >= rows)
-            chosen_key = iota((1, rows), 1) % MIDDLE == middle_offset
-            weight = jnp.where(chosen & chosen_key, 2.0, 1.0)
+            weight = pair_weights(rows, middle_offset)
+            row_weight = jnp.where(iota((1, rows), 1) % MIDDLE == middle_offset, 2.0, 1.0)
             query = one_head(both_q, head, SCALE)
             grad = one_head(both_g, head)
             log_sum = columns[:, head : head + 1]
             dot = columns[:, heads + head : heads + head + 1]
             parts = []
             for key, v_ref in zip(keys, v_refs):
-                probs = jnp.exp(dot_nt(query, key) - log_sum) * weight
+                probs = jnp.exp(dot_nt(query, key) - log_sum)
+                probs = jnp.concatenate(
+                    [weighted(probs[:rows], weight), probs[rows:] * row_weight], axis=0
+                )
                 inner = dot_nt(grad, v_ref[:, lanes]) - dot
                 parts.append(
                     jnp.concatenate([(probs * inner).astype(BF16), probs[rows:].astype(BF16)], axis=0)
@@ -333,11 +342,15 @@
 
 
 def relay_kernel(first_ref, *refs):
-    qg_ref, pay_refs, far_refs = refs[0], refs[1:3], refs[3:-3]
-    for parts, out in zip(((qg_ref,), pay_refs, far_refs), refs[-3:]):
+    pay_refs, far_refs = refs[:2], refs[2:-2]
+    for parts, out in zip((pay_refs, far_refs), refs[-2:]):
         for index, ref in enumerate(parts):
             rows = ref.shape[0]
             out[index * rows : (index + 1) * rows, :] = ref[...]
+
+
+def copy_kernel(_, in_ref, out_ref):
+    out_ref[...] = in_ref[...]
 
 
 def key_kernel(near_count, off_ref, k_ref, v_ref, *refs):
@@ -381,7 +394,7 @@
             for query, grad, pay_ref in zip(queries, grads, pay_refs):
                 log_sum = jnp.where(special, HIGH, pay_ref[head : head + 1, :rows])
                 dot = pay_ref[heads + head : heads + head + 1, :rows]
-                probs = jnp.exp(dot_nt(keys, query) - log_sum) * weight
+                probs = weighted(jnp.exp(dot_nt(keys, query) - log_sum), weight)
                 inner = dot_nt(values, grad) - dot
                 prob_parts.append(probs.astype(BF16))
                 score_parts.append((probs * inner).astype(BF16))
@@ -444,6 +457,7 @@
     place = iota((8, PAIR), 1) % HD
     first_term = jnp.where(iota((8, PAIR), 0) == 0, 0, 3)
     picks = jnp.where((place >= first_term) & (place < first_term + 3), 1.0, 0.0).astype(BF16)
+    states = []
     for pair in range(heads // 2):
         lanes = slice(pair * PAIR, (pair + 1) * PAIR)
         all_q, all_k, all_v, all_g, all_s = [kind(index, lanes) for index in range(5)]
@@ -461,6 +475,21 @@
         joint = most + jnp.log(jnp.exp(known_sum - most) + jnp.exp(log_sum - most))
         share = jnp.exp(known_sum - joint)
         dot = known_dot * share + product * jnp.exp(log_sum - joint)
+        states.append((lanes, query, grad, all_k, scores, inner, joint, share, dot, known_dot - dot))
+    for pair, state in enumerate(states):
+        lanes, query, grad, _, _, _, joint, _, dot, _ = state
+        offset = jnp.where(second, off_ref[2 * pair + 1], off_ref[2 * pair])
+        middle = row % MIDDLE == offset % MIDDLE
+        upper = row % UPPER == offset
+        weight = same_group + jnp.where(middle, same_segment, 0.0) + jnp.where(upper, 1.0, 0.0)
+        scores = jnp.where(weight > 0.0, dot_nt(k_ref[:, lanes], query), LOW)
+        probs = jnp.exp(scores - joint) * weight
+        inner = dot_nt(v_ref[:, lanes], grad) - dot
+        dk_ref[:, lanes] = (
+            dk_in[:, lanes] + dot_nn((probs * inner).astype(BF16), query)
+        ).astype(BF16)
+        dv_ref[:, lanes] = (dv_in[:, lanes] + dot_nn(probs.astype(BF16), grad)).astype(BF16)
+    for lanes, _, _, all_k, scores, inner, joint, share, dot, change in states:
         probs = jnp.exp(scores - joint)
         grad_q = SCALE * lax.dot_general(
             (probs * (inner - dot)).astype(BF16),
@@ -468,7 +497,6 @@
             (((0,), (0,)), ((), ())),
             preferred_element_type=F32,
         )
-        change = known_dot - dot
         lines = []
         for index in range(spec_rows):
             other = every + index
@@ -483,17 +511,6 @@
         dq_ref[:, lanes] = (
             dq_in[:, lanes] + jnp.where(special, jnp.concatenate(lines, axis=0), 0.0)
         ).astype(BF16)
-        offset = jnp.where(second, off_ref[2 * pair + 1], off_ref[2 * pair])
-        middle = row % MIDDLE == offset % MIDDLE
-        upper = row % UPPER == offset
-        weight = same_group + jnp.where(middle, same_segment, 0.0) + jnp.where(upper, 1.0, 0.0)
-        scores = jnp.where(weight > 0.0, dot_nt(k_ref[:, lanes], query), LOW)
-        probs = jnp.exp(scores - joint) * weight
-        inner = dot_nt(v_ref[:, lanes], grad) - dot
-        dk_ref[:, lanes] = (
-            dk_in[:, lanes] + dot_nn((probs * inner).astype(BF16), query)
-        ).astype(BF16)
-        dv_ref[:, lanes] = (dv_in[:, lanes] + dot_nn(probs.astype(BF16), grad)).astype(BF16)
 
 
 def call(kernel, outs, *arrays, us=1.0, raw=False, scratch=(), vmem_mib=40):
@@ -578,18 +595,18 @@
     held = call(
         relay_kernel,
         [
-            ((2 * rows, width), BF16),
             ((2 * STAT_ROWS, rows + width), F32),
             ((far.shape[0] * len(far_came), width), BF16),
         ],
-        dq_spec, next_qg, *pays_far, *far_came, us=0.3,
-    )
-    next_qgs, pays, fars = [(part, across(part, "ctxb", 1)) for part in held]
-    qg_parts = [qg, core_qg, *next_qgs]
+        dq_spec, *pays_far, *far_came, us=0.3,
+    )
+    pays, fars = [(part, across(part, "ctxb", 1)) for part in held]
     (block,) = call(
         partial(collect_kernel, rows), [((5 * slots * spec_rows, width), BF16)], *pays, *fars,
         us=0.3,
     )
+    (next_qg,) = call(copy_kernel, [((2 * rows, width), BF16)], block, next_qg, us=0.2)
+    qg_parts = [qg, core_qg, next_qg, across(next_qg, "ctxb", 1)]
     blocks = [block] + [across(block, "ctxa", mask) for mask in range(1, outer)]
     dk, dv = call(
         partial(key_kernel, near_count),

time: 47.5 us -> 46.6 us (0.981)
  Pallas kernels: 19.2 us -> 18.4 us
    pallas_call x10 -> x11, Pallas kernels: 19.2 us -> 18.4 us  [call(): pl.pallas_call(kernel, out_shape=tuple((jax.ShapeDtypeStruct(shape, dtype...]
  transfers between devices with their start and end apart: 18 -> 18, of which waited for: 6 -> 5; matrix products, arithmetic and copies ran while one was open for 0% -> 0% of each run, Pallas kernels for 34% -> 35%
where the time goes in v4:
time: 46.6 us; the launch traced here: 46.4 us
  Pallas kernels  18.4 us (39%)
  starting transfers between devices  16.3 us (35%)
  waiting for transfers between devices  10.8 us (23%)
  between operations  0.83 us (2%)
    pallas_call x11, Pallas kernels, call(): pl.pallas_call(kernel, out_shape=tuple((jax.ShapeDtypeStruct(shape, dtype...  18.4 us
    ppermute x18, starting transfers between devices, across(): lax.ppermute(value, axis, [(source, source ^ mask) for source in range(si...  16.3 us
    ppermute x18, waiting for transfers between devices, across(): lax.ppermute(value, axis, [(source, source ^ mask) for source in range(si...  10.8 us
  transfers between devices with their start and end apart: 18, of which 5 were waited for; matrix products, arithmetic and copies ran while one was open for 0% of the time, Pallas kernels for 35%

profile of v4, /device:TPU:0, one launch (start us, length us, event | category | flops | bytes accessed | tf_op | source)
XLA Modules:
  0.0 46.4 jit_solution(10880295513098856050)
XLA Ops:
  0.7 0.5 %collective-permute-start = (bf16[256,384]{1,0:T(8,128)(2,1)}, bf16[256,384]{1,0:T(8,128)(2,1)S(1)}, u32[]{:S(2)}, u32[]{:S(2)}) collective-permute-start(bf16[256,384]{1,0:T(8,128)(2,1)} %k_ref.5), channel_id=1, source_target_pairs={{0,1},{1,0},{2,3},{3,2},{4,5},{5,4},{6,7},{7,6},{8,9},{9,8},{10,11... | collective-permute-start | bytes 589832 | tf_op jit(solution)/shard_map/ppermute | solution.py:536
  1.2 0.1 collective-permute-start.1
  1.3 3.0 %collective-permute-start.2 = (bf16[256,384]{1,0:T(8,128)(2,1)}, bf16[256,384]{1,0:T(8,128)(2,1)S(1)}, u32[]{:S(2)}, u32[]{:S(2)}) collective-permute-start(bf16[256,384]{1,0:T(8,128)(2,1)} %k_ref.5), channel_id=1, source_target_pairs={{0,2},{1,3},{2,0},{3,1},{4,6},{5,7},{6,4},{7,5},{8,10},{9,11},{10,... | collective-permute-start | bytes 589832 | tf_op jit(solution)/shard_map/ppermute | solution.py:536
  4.3 0.0 collective-permute-start.3
  4.3 2.3 %shard_map.77 = (bf16[64,384]{1,0:T(8,128)(2,1)}, bf16[64,384]{1,0:T(8,128)(2,1)}, bf16[64,384]{1,0:T(8,128)(2,1)}) custom-call(s32[6]{0:T(128)} %off_ref.9, bf16[256,384]{1,0:T(8,128)(2,1)} %q_ref.5, bf16[256,384]{1,0:T(8,128)(2,1)} %k_ref.5, bf16[256,384]{1,0:T(8,128)(2,1)} %v_ref.5, bf16[256,384]{1,0:T(8,128)(2,1)} %g_ref.5), custom_call_target="tpu_custom_call" | custom-call | flops 1495000064 | tf_op jit(solution)/shard_map/pallas_call | solution.py:521
  6.6 0.0 copy-start.4
  6.6 3.1 %collective-permute-start.4 = (bf16[64,384]{1,0:T(8,128)(2,1)}, bf16[64,384]{1,0:T(8,128)(2,1)S(1)}, u32[]{:S(2)}, u32[]{:S(2)}) collective-permute-start(bf16[64,384]{1,0:T(8,128)(2,1)} %get-tuple-element.14), channel_id=1, source_target_pairs={{0,4},{1,5},{2,6},{3,7},{4,0},{5,1},{6,2},{7,3},{8,12},{9,13},{10,... | collective-permute-start | bytes 147464 | tf_op jit(solution)/shard_map/ppermute | solution.py:536
  9.7 1.3 %collective-permute-start.5 = (bf16[64,384]{1,0:T(8,128)(2,1)}, bf16[64,384]{1,0:T(8,128)(2,1)S(1)}, u32[]{:S(2)}, u32[]{:S(2)}) collective-permute-start(bf16[64,384]{1,0:T(8,128)(2,1)} %get-tuple-element.14), channel_id=1, source_target_pairs={{0,6},{1,7},{2,4},{3,5},{4,2},{5,3},{6,0},{7,1},{8,14},{9,15},{10,... | collective-permute-start | bytes 147464 | tf_op jit(solution)/shard_map/ppermute | solution.py:536
  11.0 1.9 %shard_map.76.first_ref.known_ref = f32[24,256]{1,0:T(8,128)S(1)} custom-call(s32[6]{0:T(128)S(1)} %copy-done.4, bf16[256,384]{1,0:T(8,128)(2,1)S(1)} %copy-done, bf16[256,384]{1,0:T(8,128)(2,1)S(1)} %copy-done.1, bf16[256,384]{1,0:T(8,128)(2,1)S(1)} %copy-done.2, bf16[256,384]{1,0:T(8,128)(2,1)S(1)} %copy-done.3, ...), custom_call_target="tpu_custom_call" | custom-call | flops 2529999872 | tf_op jit(solution)/shard_map/pallas_call | solution.py:521
  12.9 1.9 %collective-permute-done.4.refs_2_ = bf16[64,384]{1,0:T(8,128)(2,1)S(1)} collective-permute-done((bf16[64,384]{1,0:T(8,128)(2,1)}, bf16[64,384]{1,0:T(8,128)(2,1)S(1)}, u32[]{:S(2)}, u32[]{:S(2)}) %collective-permute-start.4) | collective-permute-done | bytes 49184 | tf_op jit(solution)/shard_map/ppermute | solution.py:536
  14.8 3.4 %collective-permute-done.5.refs_3_ = bf16[64,384]{1,0:T(8,128)(2,1)S(1)} collective-permute-done((bf16[64,384]{1,0:T(8,128)(2,1)}, bf16[64,384]{1,0:T(8,128)(2,1)S(1)}, u32[]{:S(2)}, u32[]{:S(2)}) %collective-permute-start.5) | collective-permute-done | bytes 49184 | tf_op jit(solution)/shard_map/ppermute | solution.py:536
  18.2 0.0 copy-start.5
  18.2 0.0 copy-start.6
  18.2 0.1 collective-permute-start.6
  18.3 0.1 collective-permute-start.13
  18.5 1.7 %collective-permute-done.6.refs_1_.refs_5_ = bf16[640,384]{1,0:T(8,128)(2,1)S(1)} collective-permute-done((bf16[640,384]{1,0:T(8,128)(2,1)S(1)}, bf16[640,384]{1,0:T(8,128)(2,1)S(1)}, u32[]{:S(2)}, u32[]{:S(2)}) %collective-permute-start.6) | collective-permute-done | bytes 491552 | tf_op jit(solution)/shard_map/ppermute | solution.py:536
  20.1 2.6 %shard_map.80 = (f32[16,640]{1,0:T(8,128)S(1)}, bf16[96,384]{1,0:T(8,128)(2,1)S(1)}) custom-call(s32[6]{0:T(128)S(1)} %copy-done.4, bf16[256,384]{1,0:T(8,128)(2,1)S(1)} %copy-done, bf16[256,384]{1,0:T(8,128)(2,1)S(1)} %copy-done.1, f32[24,256]{1,0:T(8,128)S(1)} %shard_map.76.first_ref.known_ref, bf16[64,384]{1,0:T(8,128)(2,1)S(1)} %copy-done.5, ...), custom_call_target="tpu_custom_call" | custom-call | flops 2875000064 | tf_op jit(solution)/shard_map/pallas_call | solution.py:521
  22.8 0.5 %collective-permute-start.9 = (bf16[96,384]{1,0:T(8,128)(2,1)S(1)}, bf16[96,384]{1,0:T(8,128)(2,1)S(1)}, u32[]{:S(2)}, u32[]{:S(2)}) collective-permute-start(bf16[96,384]{1,0:T(8,128)(2,1)S(1)} %get-tuple-element.20), channel_id=1, source_target_pairs={{0,4},{1,5},{2,6},{3,7},{4,0},{5,1},{6,2},{7,3},{8,12},{9,13},{10,... | collective-permute-start | bytes 221192 | tf_op jit(solution)/shard_map/ppermute | solution.py:536
  23.2 2.3 %collective-permute-start.10 = (bf16[96,384]{1,0:T(8,128)(2,1)S(1)}, bf16[96,384]{1,0:T(8,128)(2,1)S(1)}, u32[]{:S(2)}, u32[]{:S(2)}) collective-permute-start(bf16[96,384]{1,0:T(8,128)(2,1)S(1)} %get-tuple-element.20), channel_id=1, source_target_pairs={{0,6},{1,7},{2,4},{3,5},{4,2},{5,3},{6,0},{7,1},{8,14},{9,15},{10,... | collective-permute-start | bytes 221192 | tf_op jit(solution)/shard_map/ppermute | solution.py:536
  25.5 0.8 %collective-permute-start.8 = (f32[16,640]{1,0:T(8,128)S(1)}, f32[16,640]{1,0:T(8,128)S(1)}, u32[]{:S(2)}, u32[]{:S(2)}) collective-permute-start(f32[16,640]{1,0:T(8,128)S(1)} %get-tuple-element.17.pay_ref.refs_0_), channel_id=1, source_target_pairs={{0,2},{1,3},{2,0},{3,1},{4,6},{5,7},{6,4},{7,5},{8,10},{9,11},{10,... | collective-permute-start | bytes 122888 | tf_op jit(solution)/shard_map/ppermute | solution.py:536
  26.3 4.6 %shard_map.81 = (f32[256,384]{1,0:T(8,128)S(1)}, f32[4,384]{1,0:T(4,128)S(1)}) custom-call(s32[6]{0:T(128)S(1)} %copy-done.4, bf16[512,384]{1,0:T(8,128)(2,1)S(1)} %shard_map.79.qg_ref.refs_0_, bf16[64,384]{1,0:T(8,128)(2,1)S(1)} %copy-done.5, f32[16,640]{1,0:T(8,128)S(1)} %get-tuple-element.17.pay_ref.refs_0_, bf16[256,384]{1,0:T(8,128)(2,1)S(1)} %copy-done.2, ...), custom_call_target="tpu_custom_call" | custom-call | flops 5750000128 | tf_op jit(solution)/shard_map/pallas_call | solution.py:521
  30.9 3.0 %collective-permute-done.8.refs_1_ = f32[16,640]{1,0:T(8,128)S(1)} collective-permute-done((f32[16,640]{1,0:T(8,128)S(1)}, f32[16,640]{1,0:T(8,128)S(1)}, u32[]{:S(2)}, u32[]{:S(2)}) %collective-permute-start.8) | collective-permute-done | bytes 40992 | tf_op jit(solution)/shard_map/ppermute | solution.py:536
  34.0 0.1 collective-permute-start.12
  34.1 0.5 %collective-permute-start.11 = (f32[32,640]{1,0:T(8,128)S(1)}, f32[32,640]{1,0:T(8,128)S(1)}, u32[]{:S(2)}, u32[]{:S(2)}) collective-permute-start(f32[32,640]{1,0:T(8,128)S(1)} %get-tuple-element.21.refs_0_.refs_4_), channel_id=1, source_target_pairs={{0,1},{1,0},{2,3},{3,2},{4,5},{5,4},{6,7},{7,6},{8,9},{9,8},{10,11... | collective-permute-start | bytes 245768 | tf_op jit(solution)/shard_map/ppermute | solution.py:536
  34.6 0.1 collective-permute-start.7
  34.6 0.9 %collective-permute-done.11.refs_1_.refs_5_ = f32[32,640]{1,0:T(8,128)S(1)} collective-permute-done((f32[32,640]{1,0:T(8,128)S(1)}, f32[32,640]{1,0:T(8,128)S(1)}, u32[]{:S(2)}, u32[]{:S(2)}) %collective-permute-start.11) | collective-permute-done | bytes 81952 | tf_op jit(solution)/shard_map/ppermute | solution.py:536
  35.6 0.4 collective-permute-start.14
  36.0 1.5 %collective-permute-start.15 = (bf16[80,384]{1,0:T(8,128)(2,1)S(1)}, bf16[80,384]{1,0:T(8,128)(2,1)S(1)}, u32[]{:S(2)}, u32[]{:S(2)}) collective-permute-start(bf16[80,384]{1,0:T(8,128)(2,1)S(1)} %shard_map.83._.refs_0_), channel_id=1, source_target_pairs={{0,8},{8,0},{16,24},{24,16},{1,9},{9,1},{17,25},{25,17},{2,10},{10... | collective-permute-start | bytes 184328 | tf_op jit(solution)/shard_map/ppermute | solution.py:536
  37.5 1.5 %collective-permute-start.16 = (bf16[80,384]{1,0:T(8,128)(2,1)S(1)}, bf16[80,384]{1,0:T(8,128)(2,1)S(1)}, u32[]{:S(2)}, u32[]{:S(2)}) collective-permute-start(bf16[80,384]{1,0:T(8,128)(2,1)S(1)} %shard_map.83._.refs_0_), channel_id=1, source_target_pairs={{0,16},{8,24},{16,0},{24,8},{1,17},{9,25},{17,1},{25,9},{2,18},{10... | collective-permute-start | bytes 184328 | tf_op jit(solution)/shard_map/ppermute | solution.py:536
  39.0 0.5 %collective-permute-start.17 = (bf16[80,384]{1,0:T(8,128)(2,1)S(1)}, bf16[80,384]{1,0:T(8,128)(2,1)S(1)}, u32[]{:S(2)}, u32[]{:S(2)}) collective-permute-start(bf16[80,384]{1,0:T(8,128)(2,1)S(1)} %shard_map.83._.refs_0_), channel_id=1, source_target_pairs={{0,24},{8,16},{16,8},{24,0},{1,25},{9,17},{17,9},{25,1},{2,26},{10... | collective-permute-start | bytes 184328 | tf_op jit(solution)/shard_map/ppermute | solution.py:536
  39.5 4.6 %shard_map.85 = (f32[256,384]{1,0:T(8,128)S(1)}, f32[256,384]{1,0:T(8,128)S(1)}) custom-call(s32[6]{0:T(128)S(1)} %copy-done.4, bf16[256,384]{1,0:T(8,128)(2,1)S(1)} %copy-done.2, bf16[256,384]{1,0:T(8,128)(2,1)S(1)} %copy-done.3, bf16[512,384]{1,0:T(8,128)(2,1)S(1)} %shard_map.79.qg_ref.refs_0_, bf16[512,384]{1,0:T(8,128)(2,1)S(1)} %collective-permute-done.7.refs_1_, ...), custom_call_target="tpu_custom_call" | custom-call | flops 5750000128 | tf_op jit(solution)/shard_map/pallas_call | solution.py:521
  44.1 2.3 %shard_map.86 = (bf16[256,384]{1,0:T(8,128)(2,1)}, bf16[256,384]{1,0:T(8,128)(2,1)}, bf16[256,384]{1,0:T(8,128)(2,1)}) custom-call(s32[6]{0:T(128)S(1)} %copy-done.4, bf16[256,384]{1,0:T(8,128)(2,1)S(1)} %copy-done.2, bf16[256,384]{1,0:T(8,128)(2,1)S(1)} %copy-done.3, f32[256,384]{1,0:T(8,128)S(1)} %get-tuple-element.18.dq_in, ...), custom_call_target="tpu_custom_call" | custom-call | flops 3449999872 | tf_op jit(solution)/shard_map/pallas_call | solution.py:521
  (29 shorter events, 0.2 us)
Async XLA Ops:
  0.6 10.4 %copy-start.2 = (bf16[256,384]{1,0:T(8,128)(2,1)S(1)}, bf16[256,384]{1,0:T(8,128)(2,1)}, u32[]{:S(2)}) copy-start(bf16[256,384]{1,0:T(8,128)(2,1)} %k_ref.5) | copy-start | bytes 589828
  0.6 10.4 %copy-start.3 = (bf16[256,384]{1,0:T(8,128)(2,1)S(1)}, bf16[256,384]{1,0:T(8,128)(2,1)}, u32[]{:S(2)}) copy-start(bf16[256,384]{1,0:T(8,128)(2,1)} %v_ref.5) | copy-start | bytes 589828
  0.7 10.4 %copy-start = (bf16[256,384]{1,0:T(8,128)(2,1)S(1)}, bf16[256,384]{1,0:T(8,128)(2,1)}, u32[]{:S(2)}) copy-start(bf16[256,384]{1,0:T(8,128)(2,1)} %q_ref.5) | copy-start | bytes 589828
  0.7 10.4 %copy-start.1 = (bf16[256,384]{1,0:T(8,128)(2,1)S(1)}, bf16[256,384]{1,0:T(8,128)(2,1)}, u32[]{:S(2)}) copy-start(bf16[256,384]{1,0:T(8,128)(2,1)} %g_ref.5) | copy-start | bytes 589828
  0.7 9.0 %collective-permute-start = (bf16[256,384]{1,0:T(8,128)(2,1)}, bf16[256,384]{1,0:T(8,128)(2,1)S(1)}, u32[]{:S(2)}, u32[]{:S(2)}) collective-permute-start(bf16[256,384]{1,0:T(8,128)(2,1)} %k_ref.5), channel_id=1, source_target_pairs={{0,1},{1,0},{2,3},{3,2},{4,5},{5,4},{6,7},{7,6},{8,9},{9,8},{10,11... | collective-permute-start | bytes 589832 | tf_op jit(solution)/shard_map/ppermute | solution.py:536
  1.2 9.8 %collective-permute-start.1 = (bf16[256,384]{1,0:T(8,128)(2,1)}, bf16[256,384]{1,0:T(8,128)(2,1)S(1)}, u32[]{:S(2)}, u32[]{:S(2)}) collective-permute-start(bf16[256,384]{1,0:T(8,128)(2,1)} %v_ref.5), channel_id=1, source_target_pairs={{0,1},{1,0},{2,3},{3,2},{4,5},{5,4},{6,7},{7,6},{8,9},{9,8},{10,11... | collective-permute-start | bytes 589832 | tf_op jit(solution)/shard_map/ppermute | solution.py:536
  1.3 16.9 %collective-permute-start.2 = (bf16[256,384]{1,0:T(8,128)(2,1)}, bf16[256,384]{1,0:T(8,128)(2,1)S(1)}, u32[]{:S(2)}, u32[]{:S(2)}) collective-permute-start(bf16[256,384]{1,0:T(8,128)(2,1)} %k_ref.5), channel_id=1, source_target_pairs={{0,2},{1,3},{2,0},{3,1},{4,6},{5,7},{6,4},{7,5},{8,10},{9,11},{10,... | collective-permute-start | bytes 589832 | tf_op jit(solution)/shard_map/ppermute | solution.py:536
  4.3 13.9 %collective-permute-start.3 = (bf16[256,384]{1,0:T(8,128)(2,1)}, bf16[256,384]{1,0:T(8,128)(2,1)S(1)}, u32[]{:S(2)}, u32[]{:S(2)}) collective-permute-start(bf16[256,384]{1,0:T(8,128)(2,1)} %v_ref.5), channel_id=1, source_target_pairs={{0,2},{1,3},{2,0},{3,1},{4,6},{5,7},{6,4},{7,5},{8,10},{9,11},{10,... | collective-permute-start | bytes 589832 | tf_op jit(solution)/shard_map/ppermute | solution.py:536
  6.6 4.5 %copy-start.4 = (s32[6]{0:T(128)S(1)}, s32[6]{0:T(128)}, u32[]{:S(2)}) copy-start(s32[6]{0:T(128)} %off_ref.9) | copy-start | bytes 76
  6.6 8.2 %collective-permute-start.4 = (bf16[64,384]{1,0:T(8,128)(2,1)}, bf16[64,384]{1,0:T(8,128)(2,1)S(1)}, u32[]{:S(2)}, u32[]{:S(2)}) collective-permute-start(bf16[64,384]{1,0:T(8,128)(2,1)} %get-tuple-element.14), channel_id=1, source_target_pairs={{0,4},{1,5},{2,6},{3,7},{4,0},{5,1},{6,2},{7,3},{8,12},{9,13},{10,... | collective-permute-start | bytes 147464 | tf_op jit(solution)/shard_map/ppermute | solution.py:536
  9.7 8.5 %collective-permute-start.5 = (bf16[64,384]{1,0:T(8,128)(2,1)}, bf16[64,384]{1,0:T(8,128)(2,1)S(1)}, u32[]{:S(2)}, u32[]{:S(2)}) collective-permute-start(bf16[64,384]{1,0:T(8,128)(2,1)} %get-tuple-element.14), channel_id=1, source_target_pairs={{0,6},{1,7},{2,4},{3,5},{4,2},{5,3},{6,0},{7,1},{8,14},{9,15},{10,... | collective-permute-start | bytes 147464 | tf_op jit(solution)/shard_map/ppermute | solution.py:536
  18.2 2.0 %copy-start.5 = (bf16[64,384]{1,0:T(8,128)(2,1)S(1)}, bf16[64,384]{1,0:T(8,128)(2,1)}, u32[]{:S(2)}) copy-start(bf16[64,384]{1,0:T(8,128)(2,1)} %get-tuple-element.15.spec_ref.spec_in) | copy-start | bytes 147460
  18.2 1.9 %copy-start.6 = (bf16[64,384]{1,0:T(8,128)(2,1)S(1)}, bf16[64,384]{1,0:T(8,128)(2,1)}, u32[]{:S(2)}) copy-start(bf16[64,384]{1,0:T(8,128)(2,1)} %get-tuple-element.16.own_near_ref) | copy-start | bytes 147460
  18.2 1.9 %collective-permute-start.6 = (bf16[640,384]{1,0:T(8,128)(2,1)S(1)}, bf16[640,384]{1,0:T(8,128)(2,1)S(1)}, u32[]{:S(2)}, u32[]{:S(2)}) collective-permute-start(bf16[640,384]{1,0:T(8,128)(2,1)S(1)} %shard_map.78._.refs_0_.refs_4_), channel_id=1, source_target_pairs={{0,1},{1,0},{2,3},{3,2},{4,5},{5,4},{6,7},{7,6},{8,9},{9,8},{10,11... | collective-permute-start | bytes 1474568 | tf_op jit(solution)/shard_map/ppermute | solution.py:536
  18.3 17.2 %collective-permute-start.13 = (bf16[512,384]{1,0:T(8,128)(2,1)S(1)}, bf16[512,384]{1,0:T(8,128)(2,1)S(1)}, u32[]{:S(2)}, u32[]{:S(2)}) collective-permute-start(bf16[512,384]{1,0:T(8,128)(2,1)S(1)} %shard_map.79.qg_ref.refs_0_), channel_id=1, source_target_pairs={{0,2},{1,3},{2,0},{3,1},{4,6},{5,7},{6,4},{7,5},{8,10},{9,11},{10,... | collective-permute-start | bytes 1179656 | tf_op jit(solution)/shard_map/ppermute | solution.py:536
  22.8 11.2 %collective-permute-start.9 = (bf16[96,384]{1,0:T(8,128)(2,1)S(1)}, bf16[96,384]{1,0:T(8,128)(2,1)S(1)}, u32[]{:S(2)}, u32[]{:S(2)}) collective-permute-start(bf16[96,384]{1,0:T(8,128)(2,1)S(1)} %get-tuple-element.20), channel_id=1, source_target_pairs={{0,4},{1,5},{2,6},{3,7},{4,0},{5,1},{6,2},{7,3},{8,12},{9,13},{10,... | collective-permute-start | bytes 221192 | tf_op jit(solution)/shard_map/ppermute | solution.py:536
  23.2 10.7 %collective-permute-start.10 = (bf16[96,384]{1,0:T(8,128)(2,1)S(1)}, bf16[96,384]{1,0:T(8,128)(2,1)S(1)}, u32[]{:S(2)}, u32[]{:S(2)}) collective-permute-start(bf16[96,384]{1,0:T(8,128)(2,1)S(1)} %get-tuple-element.20), channel_id=1, source_target_pairs={{0,6},{1,7},{2,4},{3,5},{4,2},{5,3},{6,0},{7,1},{8,14},{9,15},{10,... | collective-permute-start | bytes 221192 | tf_op jit(solution)/shard_map/ppermute | solution.py:536
  25.5 8.5 %collective-permute-start.8 = (f32[16,640]{1,0:T(8,128)S(1)}, f32[16,640]{1,0:T(8,128)S(1)}, u32[]{:S(2)}, u32[]{:S(2)}) collective-permute-start(f32[16,640]{1,0:T(8,128)S(1)} %get-tuple-element.17.pay_ref.refs_0_), channel_id=1, source_target_pairs={{0,2},{1,3},{2,0},{3,1},{4,6},{5,7},{6,4},{7,5},{8,10},{9,11},{10,... | collective-permute-start | bytes 122888 | tf_op jit(solution)/shard_map/ppermute | solution.py:536
  34.0 1.6 %collective-permute-start.12 = (bf16[192,384]{1,0:T(8,128)(2,1)S(1)}, bf16[192,384]{1,0:T(8,128)(2,1)S(1)}, u32[]{:S(2)}, u32[]{:S(2)}) collective-permute-start(bf16[192,384]{1,0:T(8,128)(2,1)S(1)} %get-tuple-element.22.refs_2_.refs_6_), channel_id=1, source_target_pairs={{0,1},{1,0},{2,3},{3,2},{4,5},{5,4},{6,7},{7,6},{8,9},{9,8},{10,11... | collective-permute-start | bytes 442376 | tf_op jit(solution)/shard_map/ppermute | solution.py:536
  34.1 1.5 %collective-permute-start.11 = (f32[32,640]{1,0:T(8,128)S(1)}, f32[32,640]{1,0:T(8,128)S(1)}, u32[]{:S(2)}, u32[]{:S(2)}) collective-permute-start(f32[32,640]{1,0:T(8,128)S(1)} %get-tuple-element.21.refs_0_.refs_4_), channel_id=1, source_target_pairs={{0,1},{1,0},{2,3},{3,2},{4,5},{5,4},{6,7},{7,6},{8,9},{9,8},{10,11... | collective-permute-start | bytes 245768 | tf_op jit(solution)/shard_map/ppermute | solution.py:536
  34.6 4.9 %collective-permute-start.7 = (bf16[512,384]{1,0:T(8,128)(2,1)S(1)}, bf16[512,384]{1,0:T(8,128)(2,1)S(1)}, u32[]{:S(2)}, u32[]{:S(2)}) collective-permute-start(bf16[512,384]{1,0:T(8,128)(2,1)S(1)} %shard_map.79.qg_ref.refs_0_), channel_id=1, source_target_pairs={{0,1},{1,0},{2,3},{3,2},{4,5},{5,4},{6,7},{7,6},{8,9},{9,8},{10,11... | collective-permute-start | bytes 1179656 | tf_op jit(solution)/shard_map/ppermute | solution.py:536
  35.6 3.9 %collective-permute-start.14 = (bf16[512,384]{1,0:T(8,128)(2,1)S(1)}, bf16[512,384]{1,0:T(8,128)(2,1)S(1)}, u32[]{:S(2)}, u32[]{:S(2)}) collective-permute-start(bf16[512,384]{1,0:T(8,128)(2,1)S(1)} %shard_map.84.refs_2_), channel_id=1, source_target_pairs={{0,1},{1,0},{2,3},{3,2},{4,5},{5,4},{6,7},{7,6},{8,9},{9,8},{10,11... | collective-permute-start | bytes 1179656 | tf_op jit(solution)/shard_map/ppermute | solution.py:536
  36.0 8.1 %collective-permute-start.15 = (bf16[80,384]{1,0:T(8,128)(2,1)S(1)}, bf16[80,384]{1,0:T(8,128)(2,1)S(1)}, u32[]{:S(2)}, u32[]{:S(2)}) collective-permute-start(bf16[80,384]{1,0:T(8,128)(2,1)S(1)} %shard_map.83._.refs_0_), channel_id=1, source_target_pairs={{0,8},{8,0},{16,24},{24,16},{1,9},{9,1},{17,25},{25,17},{2,10},{10... | collective-permute-start | bytes 184328 | tf_op jit(solution)/shard_map/ppermute | solution.py:536
  37.5 6.6 %collective-permute-start.16 = (bf16[80,384]{1,0:T(8,128)(2,1)S(1)}, bf16[80,384]{1,0:T(8,128)(2,1)S(1)}, u32[]{:S(2)}, u32[]{:S(2)}) collective-permute-start(bf16[80,384]{1,0:T(8,128)(2,1)S(1)} %shard_map.83._.refs_0_), channel_id=1, source_target_pairs={{0,16},{8,24},{16,0},{24,8},{1,17},{9,25},{17,1},{25,9},{2,18},{10... | collective-permute-start | bytes 184328 | tf_op jit(solution)/shard_map/ppermute | solution.py:536
  39.0 5.1 %collective-permute-start.17 = (bf16[80,384]{1,0:T(8,128)(2,1)S(1)}, bf16[80,384]{1,0:T(8,128)(2,1)S(1)}, u32[]{:S(2)}, u32[]{:S(2)}) collective-permute-start(bf16[80,384]{1,0:T(8,128)(2,1)S(1)} %shard_map.83._.refs_0_), channel_id=1, source_target_pairs={{0,24},{8,16},{16,8},{24,0},{1,25},{9,17},{17,9},{25,1},{2,26},{10... | collective-permute-start | bytes 184328 | tf_op jit(solution)/shard_map/ppermute | solution.py:536

commit v5 on v4

--- a/solution.py
+++ b/solution.py
@@ -172,7 +172,7 @@
         if weight is not None:
             probs = weighted(probs, weight)
         part_total = jnp.sum(probs, axis=0, keepdims=True)
-        part_product = jnp.sum(probs * inner(), axis=0, keepdims=True)
+        part_product = jnp.sum(probs * inner, axis=0, keepdims=True)
         total = part_total if total is None else total + part_total
         product = part_product if product is None else product + part_product
     return new_top, total, product
@@ -182,13 +182,18 @@
     kv_refs, out_ref = refs[:-1], refs[-1]
     rows, width = q_ref.shape
     heads = width // HD
-    for head in range(heads):
+
+    def products(head):
         lanes = pair_slice(head)
-        weight = pair_weights(rows, off_ref[head] % MIDDLE)
         query = one_head(q_ref[:, lanes], head, SCALE)
         grad = one_head(g_ref[:, lanes], head)
         scores = [dot_nt(r[:, lanes], query) for r in kv_refs[::2]]
-        inners = [partial(lambda r: dot_nt(r[:, lanes], grad), r) for r in kv_refs[1::2]]
+        return scores, [dot_nt(r[:, lanes], grad) for r in kv_refs[1::2]]
+
+    ahead = products(0)
+    for head in range(heads):
+        (scores, inners), ahead = ahead, products(head + 1) if head + 1 < heads else None
+        weight = pair_weights(rows, off_ref[head] % MIDDLE)
         terms = softmax_terms(scores, inners, [weight] * len(scores), None, None, None)
         for index, term in enumerate(terms):
             row = index * heads + head
@@ -201,20 +206,25 @@
     rows, width = q_ref.shape
     heads = width // HD
     log_sums, dots = [], []
-    for head in range(heads):
+
+    def products(head):
         lanes = pair_slice(head)
-        middle_offset = off_ref[head] % MIDDLE
-        chosen = iota((1, rows), 1) % MIDDLE == middle_offset
-        weight = pair_weights(rows, middle_offset)
         query = one_head(q_ref[:, lanes], head, SCALE)
         grad = one_head(g_ref[:, lanes], head)
-        scores = [dot_nt(r[:, lanes], query) for r in k_refs]
-        inners = [partial(lambda r: dot_nt(r[:, lanes], grad), r) for r in v_refs]
-        weights = [weight] * len(scores)
+        keys, values = [r[:, lanes] for r in k_refs], [r[:, lanes] for r in v_refs]
         if near_count:
-            far_scores = dot_nt(near_part(near_refs, 0, lanes), query)
-            scores.append(jnp.where(chosen, far_scores, LOW))
-            inners.append(lambda: dot_nt(near_part(near_refs, 1, lanes), grad))
+            keys.append(near_part(near_refs, 0, lanes))
+            values.append(near_part(near_refs, 1, lanes))
+        return [dot_nt(key, query) for key in keys], [dot_nt(value, grad) for value in values]
+
+    ahead = products(0)
+    for head in range(heads):
+        (scores, inners), ahead = ahead, products(head + 1) if head + 1 < heads else None
+        middle_offset = off_ref[head] % MIDDLE
+        weights = [pair_weights(rows, middle_offset)] * len(k_refs)
+        if near_count:
+            chosen = iota((1, rows), 1) % MIDDLE == middle_offset
+            scores[-1] = jnp.where(chosen, scores[-1], LOW)
             weights.append(None)
         known = [known_ref[i * heads + head : i * heads + head + 1, :] for i in range(3)]
         top, total, product = softmax_terms(scores, inners, weights, *known)
@@ -341,7 +351,7 @@
     return chunks(refs, 2 * (tok_rows // MIDDLE) + 2 * STAT_ROWS) if refs else []
 
 
-def relay_kernel(first_ref, *refs):
+def relay_kernel(first_ref, second_ref, *refs):
     pay_refs, far_refs = refs[:2], refs[2:-2]
     for parts, out in zip((pay_refs, far_refs), refs[-2:]):
         for index, ref in enumerate(parts):
@@ -354,13 +364,17 @@
 
 
 def key_kernel(near_count, off_ref, k_ref, v_ref, *refs):
-    qg_refs = refs[:GROUP]
-    pay_refs = chunks(refs[GROUP : GROUP + 2], STAT_ROWS)
-    far_refs = far_chunks(k_ref.shape[0], refs[GROUP + 2 : -2])
     dk_ref, dv_ref = refs[-2:]
     rows, width = k_ref.shape
     heads = width // HD
     near_rows = rows // MIDDLE
+    if len(refs) == 4:
+        qg_refs, pay_refs, known_refs = refs[:1], refs[1:2], None
+    else:
+        qg_refs = refs[: GROUP - 1]
+        pay_refs = chunks(refs[GROUP - 1 : GROUP + 1], STAT_ROWS)[1:]
+        far_refs = far_chunks(k_ref.shape[0], refs[GROUP + 1 : -4])
+        known_refs = refs[-4:-2]
     if near_count:
         first = 2 * near_rows + STAT_ROWS
         far_stats = []
@@ -411,8 +425,13 @@
             key_grads.append(dot_nn(jnp.concatenate(score_parts, axis=1), every_query))
             value_grads.append(dot_nn(jnp.concatenate(prob_parts, axis=1), every_grad))
         low = half_mask(0)
-        dk_ref[:, lanes] = jnp.where(low, key_grads[0], key_grads[1]) * SCALE
-        dv_ref[:, lanes] = jnp.where(low, value_grads[0], value_grads[1])
+        grad_k = jnp.where(low, key_grads[0], key_grads[1]) * SCALE
+        grad_v = jnp.where(low, value_grads[0], value_grads[1])
+        if known_refs:
+            grad_k = grad_k + known_refs[0][:, lanes]
+            grad_v = grad_v + known_refs[1][:, lanes]
+        dk_ref[:, lanes] = grad_k
+        dv_ref[:, lanes] = grad_v
 
 
 def collect_kernel(tok_rows, *refs):
@@ -560,7 +579,7 @@
             pltpu.SemaphoreType.DMA,
         ],
     )
-    near_came = [across(near_kv, "ctxb", mask) for mask in range(GROUP, slots, 2)]
+    near_came = [across(near_kv, "ctxb", mask) for mask in reversed(range(GROUP, slots, 2))]
     both = [((2 * rows, width), BF16)]
     own_kv = [key_matrix, value_matrix, core_k, core_v]
     term_rows = -(-3 * (width // HD) // 8) * 8
@@ -591,14 +610,18 @@
         offsets, qg, spec, pay, *kv_parts, us=5.0,
     )
     pays_far = [pay, across(pay, "ctxb", 2)]
-    far_came = [across(far, "ctxb", mask) for mask in range(GROUP, slots, 2)]
+    far_came = [across(far, "ctxb", mask) for mask in reversed(range(GROUP, slots, 2))]
+    grads = [((rows, width), F32)] * 2
+    own_dk, own_dv = call(
+        partial(key_kernel, 0), grads, offsets, key_matrix, value_matrix, qg, pay, us=1.3,
+    )
     held = call(
         relay_kernel,
         [
             ((2 * STAT_ROWS, rows + width), F32),
             ((far.shape[0] * len(far_came), width), BF16),
         ],
-        dq_spec, *pays_far, *far_came, us=0.3,
+        dq_spec, own_dk, *pays_far, *far_came, us=0.3,
     )
     pays, fars = [(part, across(part, "ctxb", 1)) for part in held]
     (block,) = call(
@@ -607,11 +630,11 @@
     )
     (next_qg,) = call(copy_kernel, [((2 * rows, width), BF16)], block, next_qg, us=0.2)
     qg_parts = [qg, core_qg, next_qg, across(next_qg, "ctxb", 1)]
-    blocks = [block] + [across(block, "ctxa", mask) for mask in range(1, outer)]
+    blocks = [block] + [across(block, "ctxa", mask) for mask in reversed(range(1, outer))]
     dk, dv = call(
         partial(key_kernel, near_count),
-        [((rows, width), F32), ((rows, width), F32)],
-        offsets, key_matrix, value_matrix, *qg_parts, *pays, *fars, us=5.0,
+        grads,
+        offsets, key_matrix, value_matrix, *qg_parts[1:], *pays, *fars, own_dk, own_dv, us=4.0,
     )
     return call(
         partial(special_kernel, slots),

time: 46.6 us -> 45.3 us (0.972)
  waiting for transfers between devices: 10.8 us -> 6.69 us
  starting transfers between devices: 16.3 us -> 17.9 us
  Pallas kernels: 18.4 us -> 19.6 us
    ppermute x18, waiting for transfers between devices: 10.8 us -> 6.69 us  [across(): lax.ppermute(value, axis, [(source, source ^ mask) for source in range(si...]
    ppermute x18, starting transfers between devices: 16.3 us -> 17.9 us  [across(): lax.ppermute(value, axis, [(source, source ^ mask) for source in range(si...]
    pallas_call x11 -> x12, Pallas kernels: 18.4 us -> 19.6 us  [call(): pl.pallas_call(kernel, out_shape=tuple((jax.ShapeDtypeStruct(shape, dtype...]
  transfers between devices with their start and end apart: 18 -> 18, of which waited for: 5 -> 4; matrix products, arithmetic and copies ran while one was open for 0% -> 0% of each run, Pallas kernels for 35% -> 38%
where the time goes in v5:
time: 45.3 us; the launch traced here: 45.1 us
  Pallas kernels  19.6 us (43%)
  starting transfers between devices  17.9 us (40%)
  waiting for transfers between devices  6.69 us (15%)
  between operations  0.86 us (2%)
    pallas_call x12, Pallas kernels, call(): pl.pallas_call(kernel, out_shape=tuple((jax.ShapeDtypeStruct(shape, dtype...  19.6 us
    ppermute x18, starting transfers between devices, across(): lax.ppermute(value, axis, [(source, source ^ mask) for source in range(si...  17.9 us
    ppermute x18, waiting for transfers between devices, across(): lax.ppermute(value, axis, [(source, source ^ mask) for source in range(si...  6.69 us
  transfers between devices with their start and end apart: 18, of which 4 were waited for; matrix products, arithmetic and copies ran while one was open for 0% of the time, Pallas kernels for 38%

profile of v5, /device:TPU:0, one launch (start us, length us, event | category | flops | bytes accessed | tf_op | source)
XLA Modules:
  0.0 45.1 jit_solution(10941444385178468743)
XLA Ops:
  0.7 0.5 %collective-permute-start = (bf16[256,384]{1,0:T(8,128)(2,1)}, bf16[256,384]{1,0:T(8,128)(2,1)S(1)}, u32[]{:S(2)}, u32[]{:S(2)}) collective-permute-start(bf16[256,384]{1,0:T(8,128)(2,1)} %k_ref.7), channel_id=1, source_target_pairs={{0,1},{1,0},{2,3},{3,2},{4,5},{5,4},{6,7},{7,6},{8,9},{9,8},{10,11... | collective-permute-start | bytes 589832 | tf_op jit(solution)/shard_map/ppermute | solution.py:555
  1.2 0.1 collective-permute-start.1
  1.3 3.0 %collective-permute-start.2 = (bf16[256,384]{1,0:T(8,128)(2,1)}, bf16[256,384]{1,0:T(8,128)(2,1)S(1)}, u32[]{:S(2)}, u32[]{:S(2)}) collective-permute-start(bf16[256,384]{1,0:T(8,128)(2,1)} %k_ref.7), channel_id=1, source_target_pairs={{0,2},{1,3},{2,0},{3,1},{4,6},{5,7},{6,4},{7,5},{8,10},{9,11},{10,... | collective-permute-start | bytes 589832 | tf_op jit(solution)/shard_map/ppermute | solution.py:555
  4.3 0.0 collective-permute-start.3
  4.3 2.3 %shard_map.77 = (bf16[64,384]{1,0:T(8,128)(2,1)}, bf16[64,384]{1,0:T(8,128)(2,1)}, bf16[64,384]{1,0:T(8,128)(2,1)}) custom-call(s32[6]{0:T(128)} %off_ref.11, bf16[256,384]{1,0:T(8,128)(2,1)} %q_ref.5, bf16[256,384]{1,0:T(8,128)(2,1)} %k_ref.7, bf16[256,384]{1,0:T(8,128)(2,1)} %v_ref.7, bf16[256,384]{1,0:T(8,128)(2,1)} %g_ref.5), custom_call_target="tpu_custom_call" | custom-call | flops 1495000064 | tf_op jit(solution)/shard_map/pallas_call | solution.py:540
  6.6 0.0 copy-start.4
  6.6 4.1 %collective-permute-start.4 = (bf16[64,384]{1,0:T(8,128)(2,1)}, bf16[64,384]{1,0:T(8,128)(2,1)S(1)}, u32[]{:S(2)}, u32[]{:S(2)}) collective-permute-start(bf16[64,384]{1,0:T(8,128)(2,1)} %get-tuple-element.16), channel_id=1, source_target_pairs={{0,6},{1,7},{2,4},{3,5},{4,2},{5,3},{6,0},{7,1},{8,14},{9,15},{10,... | collective-permute-start | bytes 147464 | tf_op jit(solution)/shard_map/ppermute | solution.py:555
  10.7 0.0 collective-permute-done.refs_2_
  10.7 1.9 %shard_map.76.first_ref.known_ref = f32[24,256]{1,0:T(8,128)S(1)} custom-call(s32[6]{0:T(128)S(1)} %copy-done.4, bf16[256,384]{1,0:T(8,128)(2,1)S(1)} %copy-done, bf16[256,384]{1,0:T(8,128)(2,1)S(1)} %copy-done.1, bf16[256,384]{1,0:T(8,128)(2,1)S(1)} %copy-done.2, bf16[256,384]{1,0:T(8,128)(2,1)S(1)} %copy-done.3, ...), custom_call_target="tpu_custom_call" | custom-call | flops 2529999872 | tf_op jit(solution)/shard_map/pallas_call | solution.py:540
  12.6 5.0 %collective-permute-done.4.refs_2_ = bf16[64,384]{1,0:T(8,128)(2,1)S(1)} collective-permute-done((bf16[64,384]{1,0:T(8,128)(2,1)}, bf16[64,384]{1,0:T(8,128)(2,1)S(1)}, u32[]{:S(2)}, u32[]{:S(2)}) %collective-permute-start.4) | collective-permute-done | bytes 49184 | tf_op jit(solution)/shard_map/ppermute | solution.py:555
  17.7 0.0 copy-start.5
  17.7 0.0 copy-start.6
  17.7 0.1 collective-permute-start.6
  17.8 1.1 %collective-permute-start.13 = (bf16[512,384]{1,0:T(8,128)(2,1)S(1)}, bf16[512,384]{1,0:T(8,128)(2,1)S(1)}, u32[]{:S(2)}, u32[]{:S(2)}) collective-permute-start(bf16[512,384]{1,0:T(8,128)(2,1)S(1)} %shard_map.79.qg_ref.refs_0_), channel_id=1, source_target_pairs={{0,2},{1,3},{2,0},{3,1},{4,6},{5,7},{6,4},{7,5},{8,10},{9,11},{10,... | collective-permute-start | bytes 1179656 | tf_op jit(solution)/shard_map/ppermute | solution.py:555
  19.0 0.7 %collective-permute-done.6.refs_1_.refs_5_ = bf16[640,384]{1,0:T(8,128)(2,1)S(1)} collective-permute-done((bf16[640,384]{1,0:T(8,128)(2,1)S(1)}, bf16[640,384]{1,0:T(8,128)(2,1)S(1)}, u32[]{:S(2)}, u32[]{:S(2)}) %collective-permute-start.6) | collective-permute-done | bytes 491552 | tf_op jit(solution)/shard_map/ppermute | solution.py:555
  19.6 2.6 %shard_map.80 = (f32[16,640]{1,0:T(8,128)S(1)}, bf16[96,384]{1,0:T(8,128)(2,1)S(1)}) custom-call(s32[6]{0:T(128)S(1)} %copy-done.4, bf16[256,384]{1,0:T(8,128)(2,1)S(1)} %copy-done, bf16[256,384]{1,0:T(8,128)(2,1)S(1)} %copy-done.1, f32[24,256]{1,0:T(8,128)S(1)} %shard_map.76.first_ref.known_ref, bf16[64,384]{1,0:T(8,128)(2,1)S(1)} %copy-done.5, ...), custom_call_target="tpu_custom_call" | custom-call | flops 2875000064 | tf_op jit(solution)/shard_map/pallas_call | solution.py:540
  22.2 2.1 %collective-permute-start.9 = (bf16[96,384]{1,0:T(8,128)(2,1)S(1)}, bf16[96,384]{1,0:T(8,128)(2,1)S(1)}, u32[]{:S(2)}, u32[]{:S(2)}) collective-permute-start(bf16[96,384]{1,0:T(8,128)(2,1)S(1)} %get-tuple-element.23), channel_id=1, source_target_pairs={{0,6},{1,7},{2,4},{3,5},{4,2},{5,3},{6,0},{7,1},{8,14},{9,15},{10,... | collective-permute-start | bytes 221192 | tf_op jit(solution)/shard_map/ppermute | solution.py:555
  24.4 0.5 %collective-permute-start.10 = (bf16[96,384]{1,0:T(8,128)(2,1)S(1)}, bf16[96,384]{1,0:T(8,128)(2,1)S(1)}, u32[]{:S(2)}, u32[]{:S(2)}) collective-permute-start(bf16[96,384]{1,0:T(8,128)(2,1)S(1)} %get-tuple-element.23), channel_id=1, source_target_pairs={{0,4},{1,5},{2,6},{3,7},{4,0},{5,1},{6,2},{7,3},{8,12},{9,13},{10,... | collective-permute-start | bytes 221192 | tf_op jit(solution)/shard_map/ppermute | solution.py:555
  24.8 1.8 %collective-permute-start.8 = (f32[16,640]{1,0:T(8,128)S(1)}, f32[16,640]{1,0:T(8,128)S(1)}, u32[]{:S(2)}, u32[]{:S(2)}) collective-permute-start(f32[16,640]{1,0:T(8,128)S(1)} %get-tuple-element.19.pay_ref.refs_1_.refs_0_), channel_id=1, source_target_pairs={{0,2},{1,3},{2,0},{3,1},{4,6},{5,7},{6,4},{7,5},{8,10},{9,11},{10,... | collective-permute-start | bytes 122888 | tf_op jit(solution)/shard_map/ppermute | solution.py:555
  26.7 4.6 %shard_map.81 = (f32[256,384]{1,0:T(8,128)S(1)}, f32[4,384]{1,0:T(4,128)S(1)}) custom-call(s32[6]{0:T(128)S(1)} %copy-done.4, bf16[512,384]{1,0:T(8,128)(2,1)S(1)} %shard_map.79.qg_ref.refs_0_, bf16[64,384]{1,0:T(8,128)(2,1)S(1)} %copy-done.5, f32[16,640]{1,0:T(8,128)S(1)} %get-tuple-element.19.pay_ref.refs_1_.refs_0_, bf16[256,384]{1,0:T(8,128)(2,1)S(1)} %copy-done.2, ...), custom_call_target="tpu_custom_call" | custom-call | flops 5750000128 | tf_op jit(solution)/shard_map/pallas_call | solution.py:540
  31.3 2.0 %shard_map.82 = (f32[256,384]{1,0:T(8,128)S(1)}, f32[256,384]{1,0:T(8,128)S(1)}) custom-call(s32[6]{0:T(128)S(1)} %copy-done.4, bf16[256,384]{1,0:T(8,128)(2,1)S(1)} %copy-done.2, bf16[256,384]{1,0:T(8,128)(2,1)S(1)} %copy-done.3, bf16[512,384]{1,0:T(8,128)(2,1)S(1)} %shard_map.79.qg_ref.refs_0_, f32[16,640]{1,0:T(8,128)S(1)} %get-tuple-element.19.pay_ref.refs_1_.refs_0_), custom_call_target="tpu_custom_call" | custom-call | flops 1495000064 | tf_op jit(solution)/shard_map/pallas_call | solution.py:540
  33.3 0.1 collective-permute-done.8.refs_1_
  33.5 0.1 collective-permute-start.12
  33.5 0.5 %collective-permute-start.11 = (f32[32,640]{1,0:T(8,128)S(1)}, f32[32,640]{1,0:T(8,128)S(1)}, u32[]{:S(2)}, u32[]{:S(2)}) collective-permute-start(f32[32,640]{1,0:T(8,128)S(1)} %get-tuple-element.24.refs_0_.refs_3_), channel_id=1, source_target_pairs={{0,1},{1,0},{2,3},{3,2},{4,5},{5,4},{6,7},{7,6},{8,9},{9,8},{10,11... | collective-permute-start | bytes 245768 | tf_op jit(solution)/shard_map/ppermute | solution.py:555
  34.0 0.1 collective-permute-start.7
  34.1 0.9 %collective-permute-done.11.refs_1_.refs_4_ = f32[32,640]{1,0:T(8,128)S(1)} collective-permute-done((f32[32,640]{1,0:T(8,128)S(1)}, f32[32,640]{1,0:T(8,128)S(1)}, u32[]{:S(2)}, u32[]{:S(2)}) %collective-permute-start.11) | collective-permute-done | bytes 81952 | tf_op jit(solution)/shard_map/ppermute | solution.py:555
  35.1 0.4 collective-permute-start.14
  35.5 2.4 %collective-permute-start.15 = (bf16[80,384]{1,0:T(8,128)(2,1)S(1)}, bf16[80,384]{1,0:T(8,128)(2,1)S(1)}, u32[]{:S(2)}, u32[]{:S(2)}) collective-permute-start(bf16[80,384]{1,0:T(8,128)(2,1)S(1)} %shard_map.84._.refs_0_), channel_id=1, source_target_pairs={{0,24},{8,16},{16,8},{24,0},{1,25},{9,17},{17,9},{25,1},{2,26},{10... | collective-permute-start | bytes 184328 | tf_op jit(solution)/shard_map/ppermute | solution.py:555
  37.9 0.5 %collective-permute-start.16 = (bf16[80,384]{1,0:T(8,128)(2,1)S(1)}, bf16[80,384]{1,0:T(8,128)(2,1)S(1)}, u32[]{:S(2)}, u32[]{:S(2)}) collective-permute-start(bf16[80,384]{1,0:T(8,128)(2,1)S(1)} %shard_map.84._.refs_0_), channel_id=1, source_target_pairs={{0,16},{8,24},{16,0},{24,8},{1,17},{9,25},{17,1},{25,9},{2,18},{10... | collective-permute-start | bytes 184328 | tf_op jit(solution)/shard_map/ppermute | solution.py:555
  38.4 0.5 %collective-permute-start.17 = (bf16[80,384]{1,0:T(8,128)(2,1)S(1)}, bf16[80,384]{1,0:T(8,128)(2,1)S(1)}, u32[]{:S(2)}, u32[]{:S(2)}) collective-permute-start(bf16[80,384]{1,0:T(8,128)(2,1)S(1)} %shard_map.84._.refs_0_), channel_id=1, source_target_pairs={{0,8},{8,0},{16,24},{24,16},{1,9},{9,1},{17,25},{25,17},{2,10},{10... | collective-permute-start | bytes 184328 | tf_op jit(solution)/shard_map/ppermute | solution.py:555
  39.0 3.8 %shard_map.86 = (f32[256,384]{1,0:T(8,128)S(1)}, f32[256,384]{1,0:T(8,128)S(1)}) custom-call(s32[6]{0:T(128)S(1)} %copy-done.4, bf16[256,384]{1,0:T(8,128)(2,1)S(1)} %copy-done.2, bf16[256,384]{1,0:T(8,128)(2,1)S(1)} %copy-done.3, bf16[512,384]{1,0:T(8,128)(2,1)S(1)} %collective-permute-done.7.refs_0_, bf16[512,384]{1,0:T(8,128)(2,1)S(1)} %shard_map.85.refs_1_, ...), custom_call_target="tpu_custom_call" | custom-call | flops 4600000000 | tf_op jit(solution)/shard_map/pallas_call | solution.py:540
  42.9 2.3 %shard_map.87 = (bf16[256,384]{1,0:T(8,128)(2,1)}, bf16[256,384]{1,0:T(8,128)(2,1)}, bf16[256,384]{1,0:T(8,128)(2,1)}) custom-call(s32[6]{0:T(128)S(1)} %copy-done.4, bf16[256,384]{1,0:T(8,128)(2,1)S(1)} %copy-done.2, bf16[256,384]{1,0:T(8,128)(2,1)S(1)} %copy-done.3, f32[256,384]{1,0:T(8,128)S(1)} %get-tuple-element.20.dq_in, ...), custom_call_target="tpu_custom_call" | custom-call | flops 3449999872 | tf_op jit(solution)/shard_map/pallas_call | solution.py:540
  (30 shorter events, 0.2 us)
Async XLA Ops:
  0.6 10.0 %copy-start.2 = (bf16[256,384]{1,0:T(8,128)(2,1)S(1)}, bf16[256,384]{1,0:T(8,128)(2,1)}, u32[]{:S(2)}) copy-start(bf16[256,384]{1,0:T(8,128)(2,1)} %k_ref.7) | copy-start | bytes 589828
  0.6 10.0 %copy-start.3 = (bf16[256,384]{1,0:T(8,128)(2,1)S(1)}, bf16[256,384]{1,0:T(8,128)(2,1)}, u32[]{:S(2)}) copy-start(bf16[256,384]{1,0:T(8,128)(2,1)} %v_ref.7) | copy-start | bytes 589828
  0.7 10.0 %copy-start = (bf16[256,384]{1,0:T(8,128)(2,1)S(1)}, bf16[256,384]{1,0:T(8,128)(2,1)}, u32[]{:S(2)}) copy-start(bf16[256,384]{1,0:T(8,128)(2,1)} %q_ref.5) | copy-start | bytes 589828
  0.7 10.0 %copy-start.1 = (bf16[256,384]{1,0:T(8,128)(2,1)S(1)}, bf16[256,384]{1,0:T(8,128)(2,1)}, u32[]{:S(2)}) copy-start(bf16[256,384]{1,0:T(8,128)(2,1)} %g_ref.5) | copy-start | bytes 589828
  0.7 10.0 %collective-permute-start = (bf16[256,384]{1,0:T(8,128)(2,1)}, bf16[256,384]{1,0:T(8,128)(2,1)S(1)}, u32[]{:S(2)}, u32[]{:S(2)}) collective-permute-start(bf16[256,384]{1,0:T(8,128)(2,1)} %k_ref.7), channel_id=1, source_target_pairs={{0,1},{1,0},{2,3},{3,2},{4,5},{5,4},{6,7},{7,6},{8,9},{9,8},{10,11... | collective-permute-start | bytes 589832 | tf_op jit(solution)/shard_map/ppermute | solution.py:555
  1.2 9.5 %collective-permute-start.1 = (bf16[256,384]{1,0:T(8,128)(2,1)}, bf16[256,384]{1,0:T(8,128)(2,1)S(1)}, u32[]{:S(2)}, u32[]{:S(2)}) collective-permute-start(bf16[256,384]{1,0:T(8,128)(2,1)} %v_ref.7), channel_id=1, source_target_pairs={{0,1},{1,0},{2,3},{3,2},{4,5},{5,4},{6,7},{7,6},{8,9},{9,8},{10,11... | collective-permute-start | bytes 589832 | tf_op jit(solution)/shard_map/ppermute | solution.py:555
  1.3 16.3 %collective-permute-start.2 = (bf16[256,384]{1,0:T(8,128)(2,1)}, bf16[256,384]{1,0:T(8,128)(2,1)S(1)}, u32[]{:S(2)}, u32[]{:S(2)}) collective-permute-start(bf16[256,384]{1,0:T(8,128)(2,1)} %k_ref.7), channel_id=1, source_target_pairs={{0,2},{1,3},{2,0},{3,1},{4,6},{5,7},{6,4},{7,5},{8,10},{9,11},{10,... | collective-permute-start | bytes 589832 | tf_op jit(solution)/shard_map/ppermute | solution.py:555
  4.3 13.3 %collective-permute-start.3 = (bf16[256,384]{1,0:T(8,128)(2,1)}, bf16[256,384]{1,0:T(8,128)(2,1)S(1)}, u32[]{:S(2)}, u32[]{:S(2)}) collective-permute-start(bf16[256,384]{1,0:T(8,128)(2,1)} %v_ref.7), channel_id=1, source_target_pairs={{0,2},{1,3},{2,0},{3,1},{4,6},{5,7},{6,4},{7,5},{8,10},{9,11},{10,... | collective-permute-start | bytes 589832 | tf_op jit(solution)/shard_map/ppermute | solution.py:555
  6.6 4.2 %copy-start.4 = (s32[6]{0:T(128)S(1)}, s32[6]{0:T(128)}, u32[]{:S(2)}) copy-start(s32[6]{0:T(128)} %off_ref.11) | copy-start | bytes 76
  6.6 11.0 %collective-permute-start.4 = (bf16[64,384]{1,0:T(8,128)(2,1)}, bf16[64,384]{1,0:T(8,128)(2,1)S(1)}, u32[]{:S(2)}, u32[]{:S(2)}) collective-permute-start(bf16[64,384]{1,0:T(8,128)(2,1)} %get-tuple-element.16), channel_id=1, source_target_pairs={{0,6},{1,7},{2,4},{3,5},{4,2},{5,3},{6,0},{7,1},{8,14},{9,15},{10,... | collective-permute-start | bytes 147464 | tf_op jit(solution)/shard_map/ppermute | solution.py:555
  10.7 6.9 %collective-permute-start.5 = (bf16[64,384]{1,0:T(8,128)(2,1)}, bf16[64,384]{1,0:T(8,128)(2,1)S(1)}, u32[]{:S(2)}, u32[]{:S(2)}) collective-permute-start(bf16[64,384]{1,0:T(8,128)(2,1)} %get-tuple-element.16), channel_id=1, source_target_pairs={{0,4},{1,5},{2,6},{3,7},{4,0},{5,1},{6,2},{7,3},{8,12},{9,13},{10,... | collective-permute-start | bytes 147464 | tf_op jit(solution)/shard_map/ppermute | solution.py:555
  17.7 2.0 %copy-start.5 = (bf16[64,384]{1,0:T(8,128)(2,1)S(1)}, bf16[64,384]{1,0:T(8,128)(2,1)}, u32[]{:S(2)}) copy-start(bf16[64,384]{1,0:T(8,128)(2,1)} %get-tuple-element.17.spec_ref.spec_in) | copy-start | bytes 147460
  17.7 1.9 %copy-start.6 = (bf16[64,384]{1,0:T(8,128)(2,1)S(1)}, bf16[64,384]{1,0:T(8,128)(2,1)}, u32[]{:S(2)}) copy-start(bf16[64,384]{1,0:T(8,128)(2,1)} %get-tuple-element.18.own_near_ref) | copy-start | bytes 147460
  17.7 1.9 %collective-permute-start.6 = (bf16[640,384]{1,0:T(8,128)(2,1)S(1)}, bf16[640,384]{1,0:T(8,128)(2,1)S(1)}, u32[]{:S(2)}, u32[]{:S(2)}) collective-permute-start(bf16[640,384]{1,0:T(8,128)(2,1)S(1)} %shard_map.78._.refs_0_.refs_4_), channel_id=1, source_target_pairs={{0,1},{1,0},{2,3},{3,2},{4,5},{5,4},{6,7},{7,6},{8,9},{9,8},{10,11... | collective-permute-start | bytes 1474568 | tf_op jit(solution)/shard_map/ppermute | solution.py:555
  17.8 17.2 %collective-permute-start.13 = (bf16[512,384]{1,0:T(8,128)(2,1)S(1)}, bf16[512,384]{1,0:T(8,128)(2,1)S(1)}, u32[]{:S(2)}, u32[]{:S(2)}) collective-permute-start(bf16[512,384]{1,0:T(8,128)(2,1)S(1)} %shard_map.79.qg_ref.refs_0_), channel_id=1, source_target_pairs={{0,2},{1,3},{2,0},{3,1},{4,6},{5,7},{6,4},{7,5},{8,10},{9,11},{10,... | collective-permute-start | bytes 1179656 | tf_op jit(solution)/shard_map/ppermute | solution.py:555
  22.2 11.2 %collective-permute-start.9 = (bf16[96,384]{1,0:T(8,128)(2,1)S(1)}, bf16[96,384]{1,0:T(8,128)(2,1)S(1)}, u32[]{:S(2)}, u32[]{:S(2)}) collective-permute-start(bf16[96,384]{1,0:T(8,128)(2,1)S(1)} %get-tuple-element.23), channel_id=1, source_target_pairs={{0,6},{1,7},{2,4},{3,5},{4,2},{5,3},{6,0},{7,1},{8,14},{9,15},{10,... | collective-permute-start | bytes 221192 | tf_op jit(solution)/shard_map/ppermute | solution.py:555
  24.4 9.1 %collective-permute-start.10 = (bf16[96,384]{1,0:T(8,128)(2,1)S(1)}, bf16[96,384]{1,0:T(8,128)(2,1)S(1)}, u32[]{:S(2)}, u32[]{:S(2)}) collective-permute-start(bf16[96,384]{1,0:T(8,128)(2,1)S(1)} %get-tuple-element.23), channel_id=1, source_target_pairs={{0,4},{1,5},{2,6},{3,7},{4,0},{5,1},{6,2},{7,3},{8,12},{9,13},{10,... | collective-permute-start | bytes 221192 | tf_op jit(solution)/shard_map/ppermute | solution.py:555
  24.8 8.6 %collective-permute-start.8 = (f32[16,640]{1,0:T(8,128)S(1)}, f32[16,640]{1,0:T(8,128)S(1)}, u32[]{:S(2)}, u32[]{:S(2)}) collective-permute-start(f32[16,640]{1,0:T(8,128)S(1)} %get-tuple-element.19.pay_ref.refs_1_.refs_0_), channel_id=1, source_target_pairs={{0,2},{1,3},{2,0},{3,1},{4,6},{5,7},{6,4},{7,5},{8,10},{9,11},{10,... | collective-permute-start | bytes 122888 | tf_op jit(solution)/shard_map/ppermute | solution.py:555
  33.5 1.6 %collective-permute-start.12 = (bf16[192,384]{1,0:T(8,128)(2,1)S(1)}, bf16[192,384]{1,0:T(8,128)(2,1)S(1)}, u32[]{:S(2)}, u32[]{:S(2)}) collective-permute-start(bf16[192,384]{1,0:T(8,128)(2,1)S(1)} %get-tuple-element.25.refs_2_.refs_5_), channel_id=1, source_target_pairs={{0,1},{1,0},{2,3},{3,2},{4,5},{5,4},{6,7},{7,6},{8,9},{9,8},{10,11... | collective-permute-start | bytes 442376 | tf_op jit(solution)/shard_map/ppermute | solution.py:555
  33.5 1.5 %collective-permute-start.11 = (f32[32,640]{1,0:T(8,128)S(1)}, f32[32,640]{1,0:T(8,128)S(1)}, u32[]{:S(2)}, u32[]{:S(2)}) collective-permute-start(f32[32,640]{1,0:T(8,128)S(1)} %get-tuple-element.24.refs_0_.refs_3_), channel_id=1, source_target_pairs={{0,1},{1,0},{2,3},{3,2},{4,5},{5,4},{6,7},{7,6},{8,9},{9,8},{10,11... | collective-permute-start | bytes 245768 | tf_op jit(solution)/shard_map/ppermute | solution.py:555
  34.0 4.9 %collective-permute-start.7 = (bf16[512,384]{1,0:T(8,128)(2,1)S(1)}, bf16[512,384]{1,0:T(8,128)(2,1)S(1)}, u32[]{:S(2)}, u32[]{:S(2)}) collective-permute-start(bf16[512,384]{1,0:T(8,128)(2,1)S(1)} %shard_map.79.qg_ref.refs_0_), channel_id=1, source_target_pairs={{0,1},{1,0},{2,3},{3,2},{4,5},{5,4},{6,7},{7,6},{8,9},{9,8},{10,11... | collective-permute-start | bytes 1179656 | tf_op jit(solution)/shard_map/ppermute | solution.py:555
  35.1 3.9 %collective-permute-start.14 = (bf16[512,384]{1,0:T(8,128)(2,1)S(1)}, bf16[512,384]{1,0:T(8,128)(2,1)S(1)}, u32[]{:S(2)}, u32[]{:S(2)}) collective-permute-start(bf16[512,384]{1,0:T(8,128)(2,1)S(1)} %shard_map.85.refs_1_), channel_id=1, source_target_pairs={{0,1},{1,0},{2,3},{3,2},{4,5},{5,4},{6,7},{7,6},{8,9},{9,8},{10,11... | collective-permute-start | bytes 1179656 | tf_op jit(solution)/shard_map/ppermute | solution.py:555
  35.5 7.4 %collective-permute-start.15 = (bf16[80,384]{1,0:T(8,128)(2,1)S(1)}, bf16[80,384]{1,0:T(8,128)(2,1)S(1)}, u32[]{:S(2)}, u32[]{:S(2)}) collective-permute-start(bf16[80,384]{1,0:T(8,128)(2,1)S(1)} %shard_map.84._.refs_0_), channel_id=1, source_target_pairs={{0,24},{8,16},{16,8},{24,0},{1,25},{9,17},{17,9},{25,1},{2,26},{10... | collective-permute-start | bytes 184328 | tf_op jit(solution)/shard_map/ppermute | solution.py:555
  37.9 4.9 %collective-permute-start.16 = (bf16[80,384]{1,0:T(8,128)(2,1)S(1)}, bf16[80,384]{1,0:T(8,128)(2,1)S(1)}, u32[]{:S(2)}, u32[]{:S(2)}) collective-permute-start(bf16[80,384]{1,0:T(8,128)(2,1)S(1)} %shard_map.84._.refs_0_), channel_id=1, source_target_pairs={{0,16},{8,24},{16,0},{24,8},{1,17},{9,25},{17,1},{25,9},{2,18},{10... | collective-permute-start | bytes 184328 | tf_op jit(solution)/shard_map/ppermute | solution.py:555
  38.4 4.4 %collective-permute-start.17 = (bf16[80,384]{1,0:T(8,128)(2,1)S(1)}, bf16[80,384]{1,0:T(8,128)(2,1)S(1)}, u32[]{:S(2)}, u32[]{:S(2)}) collective-permute-start(bf16[80,384]{1,0:T(8,128)(2,1)S(1)} %shard_map.84._.refs_0_), channel_id=1, source_target_pairs={{0,8},{8,0},{16,24},{24,16},{1,9},{9,1},{17,25},{25,17},{2,10},{10... | collective-permute-start | bytes 184328 | tf_op jit(solution)/shard_map/ppermute | solution.py:555

commit v6 on v5

--- a/solution.py
+++ b/solution.py
@@ -205,7 +205,7 @@
     out_ref, far_ref = refs[-2:]
     rows, width = q_ref.shape
     heads = width // HD
-    log_sums, dots = [], []
+    terms = []
 
     def products(head):
         lanes = pair_slice(head)
@@ -227,11 +227,10 @@
             scores[-1] = jnp.where(chosen, scores[-1], LOW)
             weights.append(None)
         known = [known_ref[i * heads + head : i * heads + head + 1, :] for i in range(3)]
-        top, total, product = softmax_terms(scores, inners, weights, *known)
-        log_sums.append(top + jnp.log(total))
-        dots.append(product / total)
+        terms.append(softmax_terms(scores, inners, weights, *known))
+    top, total, product = [jnp.concatenate(lines, axis=0) for lines in zip(*terms)]
     pad = jnp.zeros((STAT_ROWS - 2 * heads, rows), F32)
-    stats = jnp.concatenate(log_sums + dots + [pad], axis=0)
+    stats = jnp.concatenate([top + jnp.log(total), product / total, pad], axis=0)
     out_ref[:, :rows] = stats
     offsets = row_offsets(off_ref, heads)
     token = iota((STAT_ROWS, rows), 1)
@@ -476,15 +475,18 @@
     place = iota((8, PAIR), 1) % HD
     first_term = jnp.where(iota((8, PAIR), 0) == 0, 0, 3)
     picks = jnp.where((place >= first_term) & (place < first_term + 3), 1.0, 0.0).astype(BF16)
-    states = []
+    every_product = []
     for pair in range(heads // 2):
         lanes = slice(pair * PAIR, (pair + 1) * PAIR)
         all_q, all_k, all_v, all_g, all_s = [kind(index, lanes) for index in range(5)]
         query, grad = two(all_q, SCALE), two(all_g)
         known = dot_nt(picks, two(all_s))
+        scores, inner = dot_nt(all_k, query), dot_nt(all_v, grad)
+        own = dot_nt(k_ref[:, lanes], query), dot_nt(v_ref[:, lanes], grad)
+        every_product.append((lanes, query, grad, all_k, known, scores, inner, own))
+    states = []
+    for lanes, query, grad, all_k, known, scores, inner, own in every_product:
         known_sum, known_dot = known[0:1], known[1:2]
-        scores = dot_nt(all_k, query)
-        inner = dot_nt(all_v, grad)
         top = jnp.max(scores, axis=0, keepdims=True)
         weights = jnp.exp(scores - top)
         total = jnp.sum(weights, axis=0, keepdims=True)
@@ -494,21 +496,22 @@
         joint = most + jnp.log(jnp.exp(known_sum - most) + jnp.exp(log_sum - most))
         share = jnp.exp(known_sum - joint)
         dot = known_dot * share + product * jnp.exp(log_sum - joint)
-        states.append((lanes, query, grad, all_k, scores, inner, joint, share, dot, known_dot - dot))
+        change = known_dot - dot
+        states.append((lanes, query, grad, all_k, scores, inner, own, joint, share, dot, change))
     for pair, state in enumerate(states):
-        lanes, query, grad, _, _, _, joint, _, dot, _ = state
+        lanes, query, grad, _, _, _, own, joint, _, dot, _ = state
         offset = jnp.where(second, off_ref[2 * pair + 1], off_ref[2 * pair])
         middle = row % MIDDLE == offset % MIDDLE
         upper = row % UPPER == offset
         weight = same_group + jnp.where(middle, same_segment, 0.0) + jnp.where(upper, 1.0, 0.0)
-        scores = jnp.where(weight > 0.0, dot_nt(k_ref[:, lanes], query), LOW)
+        scores = jnp.where(weight > 0.0, own[0], LOW)
         probs = jnp.exp(scores - joint) * weight
-        inner = dot_nt(v_ref[:, lanes], grad) - dot
+        inner = own[1] - dot
         dk_ref[:, lanes] = (
             dk_in[:, lanes] + dot_nn((probs * inner).astype(BF16), query)
         ).astype(BF16)
         dv_ref[:, lanes] = (dv_in[:, lanes] + dot_nn(probs.astype(BF16), grad)).astype(BF16)
-    for lanes, _, _, all_k, scores, inner, joint, share, dot, change in states:
+    for lanes, _, _, all_k, scores, inner, _, joint, share, dot, change in states:
         probs = jnp.exp(scores - joint)
         grad_q = SCALE * lax.dot_general(
             (probs * (inner - dot)).astype(BF16),

time: 45.3 us -> 45 us (level)
  transfers between devices with their start and end apart: 18 -> 18, of which waited for: 4 -> 4; matrix products, arithmetic and copies ran while one was open for 0% -> 0% of each run, Pallas kernels for 38% -> 39%
where the time goes in v6:
time: 45 us; the launch traced here: 44.9 us
  Pallas kernels  19.4 us (43%)
  starting transfers between devices  17.9 us (40%)
  waiting for transfers between devices  6.68 us (15%)
  between operations  0.86 us (2%)
    pallas_call x12, Pallas kernels, call(): pl.pallas_call(kernel, out_shape=tuple((jax.ShapeDtypeStruct(shape, dtype...  19.4 us
    ppermute x18, starting transfers between devices, across(): lax.ppermute(value, axis, [(source, source ^ mask) for source in range(si...  17.9 us
    ppermute x18, waiting for transfers between devices, across(): lax.ppermute(value, axis, [(source, source ^ mask) for source in range(si...  6.68 us
  transfers between devices with their start and end apart: 18, of which 4 were waited for; matrix products, arithmetic and copies ran while one was open for 0% of the time, Pallas kernels for 39%

profile of v6, /device:TPU:0, one launch (start us, length us, event | category | flops | bytes accessed | tf_op | source)
XLA Modules:
  0.0 44.9 jit_solution(1075819813926033543)
XLA Ops:
  0.7 0.5 %collective-permute-start = (bf16[256,384]{1,0:T(8,128)(2,1)}, bf16[256,384]{1,0:T(8,128)(2,1)S(1)}, u32[]{:S(2)}, u32[]{:S(2)}) collective-permute-start(bf16[256,384]{1,0:T(8,128)(2,1)} %k_ref.7), channel_id=1, source_target_pairs={{0,1},{1,0},{2,3},{3,2},{4,5},{5,4},{6,7},{7,6},{8,9},{9,8},{10,11... | collective-permute-start | bytes 589832 | tf_op jit(solution)/shard_map/ppermute | solution.py:558
  1.2 0.1 collective-permute-start.1
  1.3 3.0 %collective-permute-start.2 = (bf16[256,384]{1,0:T(8,128)(2,1)}, bf16[256,384]{1,0:T(8,128)(2,1)S(1)}, u32[]{:S(2)}, u32[]{:S(2)}) collective-permute-start(bf16[256,384]{1,0:T(8,128)(2,1)} %k_ref.7), channel_id=1, source_target_pairs={{0,2},{1,3},{2,0},{3,1},{4,6},{5,7},{6,4},{7,5},{8,10},{9,11},{10,... | collective-permute-start | bytes 589832 | tf_op jit(solution)/shard_map/ppermute | solution.py:558
  4.3 0.0 collective-permute-start.3
  4.3 2.3 %shard_map.77 = (bf16[64,384]{1,0:T(8,128)(2,1)}, bf16[64,384]{1,0:T(8,128)(2,1)}, bf16[64,384]{1,0:T(8,128)(2,1)}) custom-call(s32[6]{0:T(128)} %off_ref.11, bf16[256,384]{1,0:T(8,128)(2,1)} %q_ref.5, bf16[256,384]{1,0:T(8,128)(2,1)} %k_ref.7, bf16[256,384]{1,0:T(8,128)(2,1)} %v_ref.7, bf16[256,384]{1,0:T(8,128)(2,1)} %g_ref.5), custom_call_target="tpu_custom_call" | custom-call | flops 1495000064 | tf_op jit(solution)/shard_map/pallas_call | solution.py:543
  6.6 0.0 copy-start.4
  6.6 4.1 %collective-permute-start.4 = (bf16[64,384]{1,0:T(8,128)(2,1)}, bf16[64,384]{1,0:T(8,128)(2,1)S(1)}, u32[]{:S(2)}, u32[]{:S(2)}) collective-permute-start(bf16[64,384]{1,0:T(8,128)(2,1)} %get-tuple-element.16), channel_id=1, source_target_pairs={{0,6},{1,7},{2,4},{3,5},{4,2},{5,3},{6,0},{7,1},{8,14},{9,15},{10,... | collective-permute-start | bytes 147464 | tf_op jit(solution)/shard_map/ppermute | solution.py:558
  10.7 1.9 %shard_map.76.first_ref.known_ref = f32[24,256]{1,0:T(8,128)S(1)} custom-call(s32[6]{0:T(128)S(1)} %copy-done.4, bf16[256,384]{1,0:T(8,128)(2,1)S(1)} %copy-done, bf16[256,384]{1,0:T(8,128)(2,1)S(1)} %copy-done.1, bf16[256,384]{1,0:T(8,128)(2,1)S(1)} %copy-done.2, bf16[256,384]{1,0:T(8,128)(2,1)S(1)} %copy-done.3, ...), custom_call_target="tpu_custom_call" | custom-call | flops 2529999872 | tf_op jit(solution)/shard_map/pallas_call | solution.py:543
  12.6 5.0 %collective-permute-done.4.refs_2_ = bf16[64,384]{1,0:T(8,128)(2,1)S(1)} collective-permute-done((bf16[64,384]{1,0:T(8,128)(2,1)}, bf16[64,384]{1,0:T(8,128)(2,1)S(1)}, u32[]{:S(2)}, u32[]{:S(2)}) %collective-permute-start.4) | collective-permute-done | bytes 49184 | tf_op jit(solution)/shard_map/ppermute | solution.py:558
  17.6 0.0 collective-permute-done.5.refs_3_
  17.7 0.0 copy-start.5
  17.7 0.0 copy-start.6
  17.7 0.1 collective-permute-start.6
  17.8 1.1 %collective-permute-start.13 = (bf16[512,384]{1,0:T(8,128)(2,1)S(1)}, bf16[512,384]{1,0:T(8,128)(2,1)S(1)}, u32[]{:S(2)}, u32[]{:S(2)}) collective-permute-start(bf16[512,384]{1,0:T(8,128)(2,1)S(1)} %shard_map.79.qg_ref.refs_0_), channel_id=1, source_target_pairs={{0,2},{1,3},{2,0},{3,1},{4,6},{5,7},{6,4},{7,5},{8,10},{9,11},{10,... | collective-permute-start | bytes 1179656 | tf_op jit(solution)/shard_map/ppermute | solution.py:558
  19.0 0.7 %collective-permute-done.6.refs_1_.refs_5_ = bf16[640,384]{1,0:T(8,128)(2,1)S(1)} collective-permute-done((bf16[640,384]{1,0:T(8,128)(2,1)S(1)}, bf16[640,384]{1,0:T(8,128)(2,1)S(1)}, u32[]{:S(2)}, u32[]{:S(2)}) %collective-permute-start.6) | collective-permute-done | bytes 491552 | tf_op jit(solution)/shard_map/ppermute | solution.py:558
  19.6 2.6 %shard_map.80 = (f32[16,640]{1,0:T(8,128)S(1)}, bf16[96,384]{1,0:T(8,128)(2,1)S(1)}) custom-call(s32[6]{0:T(128)S(1)} %copy-done.4, bf16[256,384]{1,0:T(8,128)(2,1)S(1)} %copy-done, bf16[256,384]{1,0:T(8,128)(2,1)S(1)} %copy-done.1, f32[24,256]{1,0:T(8,128)S(1)} %shard_map.76.first_ref.known_ref, bf16[64,384]{1,0:T(8,128)(2,1)S(1)} %copy-done.5, ...), custom_call_target="tpu_custom_call" | custom-call | flops 2875000064 | tf_op jit(solution)/shard_map/pallas_call | solution.py:543
  22.2 2.1 %collective-permute-start.9 = (bf16[96,384]{1,0:T(8,128)(2,1)S(1)}, bf16[96,384]{1,0:T(8,128)(2,1)S(1)}, u32[]{:S(2)}, u32[]{:S(2)}) collective-permute-start(bf16[96,384]{1,0:T(8,128)(2,1)S(1)} %get-tuple-element.23), channel_id=1, source_target_pairs={{0,6},{1,7},{2,4},{3,5},{4,2},{5,3},{6,0},{7,1},{8,14},{9,15},{10,... | collective-permute-start | bytes 221192 | tf_op jit(solution)/shard_map/ppermute | solution.py:558
  24.4 0.5 %collective-permute-start.10 = (bf16[96,384]{1,0:T(8,128)(2,1)S(1)}, bf16[96,384]{1,0:T(8,128)(2,1)S(1)}, u32[]{:S(2)}, u32[]{:S(2)}) collective-permute-start(bf16[96,384]{1,0:T(8,128)(2,1)S(1)} %get-tuple-element.23), channel_id=1, source_target_pairs={{0,4},{1,5},{2,6},{3,7},{4,0},{5,1},{6,2},{7,3},{8,12},{9,13},{10,... | collective-permute-start | bytes 221192 | tf_op jit(solution)/shard_map/ppermute | solution.py:558
  24.9 1.8 %collective-permute-start.8 = (f32[16,640]{1,0:T(8,128)S(1)}, f32[16,640]{1,0:T(8,128)S(1)}, u32[]{:S(2)}, u32[]{:S(2)}) collective-permute-start(f32[16,640]{1,0:T(8,128)S(1)} %get-tuple-element.19.pay_ref.refs_1_.refs_0_), channel_id=1, source_target_pairs={{0,2},{1,3},{2,0},{3,1},{4,6},{5,7},{6,4},{7,5},{8,10},{9,11},{10,... | collective-permute-start | bytes 122888 | tf_op jit(solution)/shard_map/ppermute | solution.py:558
  26.7 4.6 %shard_map.81 = (f32[256,384]{1,0:T(8,128)S(1)}, f32[4,384]{1,0:T(4,128)S(1)}) custom-call(s32[6]{0:T(128)S(1)} %copy-done.4, bf16[512,384]{1,0:T(8,128)(2,1)S(1)} %shard_map.79.qg_ref.refs_0_, bf16[64,384]{1,0:T(8,128)(2,1)S(1)} %copy-done.5, f32[16,640]{1,0:T(8,128)S(1)} %get-tuple-element.19.pay_ref.refs_1_.refs_0_, bf16[256,384]{1,0:T(8,128)(2,1)S(1)} %copy-done.2, ...), custom_call_target="tpu_custom_call" | custom-call | flops 5750000128 | tf_op jit(solution)/shard_map/pallas_call | solution.py:543
  31.3 2.0 %shard_map.82 = (f32[256,384]{1,0:T(8,128)S(1)}, f32[256,384]{1,0:T(8,128)S(1)}) custom-call(s32[6]{0:T(128)S(1)} %copy-done.4, bf16[256,384]{1,0:T(8,128)(2,1)S(1)} %copy-done.2, bf16[256,384]{1,0:T(8,128)(2,1)S(1)} %copy-done.3, bf16[512,384]{1,0:T(8,128)(2,1)S(1)} %shard_map.79.qg_ref.refs_0_, f32[16,640]{1,0:T(8,128)S(1)} %get-tuple-element.19.pay_ref.refs_1_.refs_0_), custom_call_target="tpu_custom_call" | custom-call | flops 1495000064 | tf_op jit(solution)/shard_map/pallas_call | solution.py:543
  33.3 0.1 collective-permute-done.8.refs_1_
  33.5 0.1 collective-permute-start.12
  33.5 0.5 %collective-permute-start.11 = (f32[32,640]{1,0:T(8,128)S(1)}, f32[32,640]{1,0:T(8,128)S(1)}, u32[]{:S(2)}, u32[]{:S(2)}) collective-permute-start(f32[32,640]{1,0:T(8,128)S(1)} %get-tuple-element.24.refs_0_.refs_3_), channel_id=1, source_target_pairs={{0,1},{1,0},{2,3},{3,2},{4,5},{5,4},{6,7},{7,6},{8,9},{9,8},{10,11... | collective-permute-start | bytes 245768 | tf_op jit(solution)/shard_map/ppermute | solution.py:558
  34.0 0.1 collective-permute-start.7
  34.1 0.9 %collective-permute-done.11.refs_1_.refs_4_ = f32[32,640]{1,0:T(8,128)S(1)} collective-permute-done((f32[32,640]{1,0:T(8,128)S(1)}, f32[32,640]{1,0:T(8,128)S(1)}, u32[]{:S(2)}, u32[]{:S(2)}) %collective-permute-start.11) | collective-permute-done | bytes 81952 | tf_op jit(solution)/shard_map/ppermute | solution.py:558
  35.1 0.4 collective-permute-start.14
  35.5 2.4 %collective-permute-start.15 = (bf16[80,384]{1,0:T(8,128)(2,1)S(1)}, bf16[80,384]{1,0:T(8,128)(2,1)S(1)}, u32[]{:S(2)}, u32[]{:S(2)}) collective-permute-start(bf16[80,384]{1,0:T(8,128)(2,1)S(1)} %shard_map.84._.refs_0_), channel_id=1, source_target_pairs={{0,24},{8,16},{16,8},{24,0},{1,25},{9,17},{17,9},{25,1},{2,26},{10... | collective-permute-start | bytes 184328 | tf_op jit(solution)/shard_map/ppermute | solution.py:558
  37.9 0.5 %collective-permute-start.16 = (bf16[80,384]{1,0:T(8,128)(2,1)S(1)}, bf16[80,384]{1,0:T(8,128)(2,1)S(1)}, u32[]{:S(2)}, u32[]{:S(2)}) collective-permute-start(bf16[80,384]{1,0:T(8,128)(2,1)S(1)} %shard_map.84._.refs_0_), channel_id=1, source_target_pairs={{0,16},{8,24},{16,0},{24,8},{1,17},{9,25},{17,1},{25,9},{2,18},{10... | collective-permute-start | bytes 184328 | tf_op jit(solution)/shard_map/ppermute | solution.py:558
  38.4 0.5 %collective-permute-start.17 = (bf16[80,384]{1,0:T(8,128)(2,1)S(1)}, bf16[80,384]{1,0:T(8,128)(2,1)S(1)}, u32[]{:S(2)}, u32[]{:S(2)}) collective-permute-start(bf16[80,384]{1,0:T(8,128)(2,1)S(1)} %shard_map.84._.refs_0_), channel_id=1, source_target_pairs={{0,8},{8,0},{16,24},{24,16},{1,9},{9,1},{17,25},{25,17},{2,10},{10... | collective-permute-start | bytes 184328 | tf_op jit(solution)/shard_map/ppermute | solution.py:558
  39.0 3.8 %shard_map.86 = (f32[256,384]{1,0:T(8,128)S(1)}, f32[256,384]{1,0:T(8,128)S(1)}) custom-call(s32[6]{0:T(128)S(1)} %copy-done.4, bf16[256,384]{1,0:T(8,128)(2,1)S(1)} %copy-done.2, bf16[256,384]{1,0:T(8,128)(2,1)S(1)} %copy-done.3, bf16[512,384]{1,0:T(8,128)(2,1)S(1)} %collective-permute-done.7.refs_0_, bf16[512,384]{1,0:T(8,128)(2,1)S(1)} %shard_map.85.refs_1_, ...), custom_call_target="tpu_custom_call" | custom-call | flops 4600000000 | tf_op jit(solution)/shard_map/pallas_call | solution.py:543
  42.9 2.0 %shard_map.87 = (bf16[256,384]{1,0:T(8,128)(2,1)}, bf16[256,384]{1,0:T(8,128)(2,1)}, bf16[256,384]{1,0:T(8,128)(2,1)}) custom-call(s32[6]{0:T(128)S(1)} %copy-done.4, bf16[256,384]{1,0:T(8,128)(2,1)S(1)} %copy-done.2, bf16[256,384]{1,0:T(8,128)(2,1)S(1)} %copy-done.3, f32[256,384]{1,0:T(8,128)S(1)} %get-tuple-element.20.dq_in, ...), custom_call_target="tpu_custom_call" | custom-call | flops 3449999872 | tf_op jit(solution)/shard_map/pallas_call | solution.py:543
  (30 shorter events, 0.2 us)
Async XLA Ops:
  0.6 10.0 %copy-start.2 = (bf16[256,384]{1,0:T(8,128)(2,1)S(1)}, bf16[256,384]{1,0:T(8,128)(2,1)}, u32[]{:S(2)}) copy-start(bf16[256,384]{1,0:T(8,128)(2,1)} %k_ref.7) | copy-start | bytes 589828
  0.6 10.0 %copy-start.3 = (bf16[256,384]{1,0:T(8,128)(2,1)S(1)}, bf16[256,384]{1,0:T(8,128)(2,1)}, u32[]{:S(2)}) copy-start(bf16[256,384]{1,0:T(8,128)(2,1)} %v_ref.7) | copy-start | bytes 589828
  0.7 10.0 %copy-start = (bf16[256,384]{1,0:T(8,128)(2,1)S(1)}, bf16[256,384]{1,0:T(8,128)(2,1)}, u32[]{:S(2)}) copy-start(bf16[256,384]{1,0:T(8,128)(2,1)} %q_ref.5) | copy-start | bytes 589828
  0.7 10.0 %copy-start.1 = (bf16[256,384]{1,0:T(8,128)(2,1)S(1)}, bf16[256,384]{1,0:T(8,128)(2,1)}, u32[]{:S(2)}) copy-start(bf16[256,384]{1,0:T(8,128)(2,1)} %g_ref.5) | copy-start | bytes 589828
  0.7 10.0 %collective-permute-start = (bf16[256,384]{1,0:T(8,128)(2,1)}, bf16[256,384]{1,0:T(8,128)(2,1)S(1)}, u32[]{:S(2)}, u32[]{:S(2)}) collective-permute-start(bf16[256,384]{1,0:T(8,128)(2,1)} %k_ref.7), channel_id=1, source_target_pairs={{0,1},{1,0},{2,3},{3,2},{4,5},{5,4},{6,7},{7,6},{8,9},{9,8},{10,11... | collective-permute-start | bytes 589832 | tf_op jit(solution)/shard_map/ppermute | solution.py:558
  1.2 9.5 %collective-permute-start.1 = (bf16[256,384]{1,0:T(8,128)(2,1)}, bf16[256,384]{1,0:T(8,128)(2,1)S(1)}, u32[]{:S(2)}, u32[]{:S(2)}) collective-permute-start(bf16[256,384]{1,0:T(8,128)(2,1)} %v_ref.7), channel_id=1, source_target_pairs={{0,1},{1,0},{2,3},{3,2},{4,5},{5,4},{6,7},{7,6},{8,9},{9,8},{10,11... | collective-permute-start | bytes 589832 | tf_op jit(solution)/shard_map/ppermute | solution.py:558
  1.3 16.3 %collective-permute-start.2 = (bf16[256,384]{1,0:T(8,128)(2,1)}, bf16[256,384]{1,0:T(8,128)(2,1)S(1)}, u32[]{:S(2)}, u32[]{:S(2)}) collective-permute-start(bf16[256,384]{1,0:T(8,128)(2,1)} %k_ref.7), channel_id=1, source_target_pairs={{0,2},{1,3},{2,0},{3,1},{4,6},{5,7},{6,4},{7,5},{8,10},{9,11},{10,... | collective-permute-start | bytes 589832 | tf_op jit(solution)/shard_map/ppermute | solution.py:558
  4.3 13.3 %collective-permute-start.3 = (bf16[256,384]{1,0:T(8,128)(2,1)}, bf16[256,384]{1,0:T(8,128)(2,1)S(1)}, u32[]{:S(2)}, u32[]{:S(2)}) collective-permute-start(bf16[256,384]{1,0:T(8,128)(2,1)} %v_ref.7), channel_id=1, source_target_pairs={{0,2},{1,3},{2,0},{3,1},{4,6},{5,7},{6,4},{7,5},{8,10},{9,11},{10,... | collective-permute-start | bytes 589832 | tf_op jit(solution)/shard_map/ppermute | solution.py:558
  6.6 4.2 %copy-start.4 = (s32[6]{0:T(128)S(1)}, s32[6]{0:T(128)}, u32[]{:S(2)}) copy-start(s32[6]{0:T(128)} %off_ref.11) | copy-start | bytes 76
  6.6 11.0 %collective-permute-start.4 = (bf16[64,384]{1,0:T(8,128)(2,1)}, bf16[64,384]{1,0:T(8,128)(2,1)S(1)}, u32[]{:S(2)}, u32[]{:S(2)}) collective-permute-start(bf16[64,384]{1,0:T(8,128)(2,1)} %get-tuple-element.16), channel_id=1, source_target_pairs={{0,6},{1,7},{2,4},{3,5},{4,2},{5,3},{6,0},{7,1},{8,14},{9,15},{10,... | collective-permute-start | bytes 147464 | tf_op jit(solution)/shard_map/ppermute | solution.py:558
  10.7 6.9 %collective-permute-start.5 = (bf16[64,384]{1,0:T(8,128)(2,1)}, bf16[64,384]{1,0:T(8,128)(2,1)S(1)}, u32[]{:S(2)}, u32[]{:S(2)}) collective-permute-start(bf16[64,384]{1,0:T(8,128)(2,1)} %get-tuple-element.16), channel_id=1, source_target_pairs={{0,4},{1,5},{2,6},{3,7},{4,0},{5,1},{6,2},{7,3},{8,12},{9,13},{10,... | collective-permute-start | bytes 147464 | tf_op jit(solution)/shard_map/ppermute | solution.py:558
  17.7 2.0 %copy-start.5 = (bf16[64,384]{1,0:T(8,128)(2,1)S(1)}, bf16[64,384]{1,0:T(8,128)(2,1)}, u32[]{:S(2)}) copy-start(bf16[64,384]{1,0:T(8,128)(2,1)} %get-tuple-element.17.spec_ref.spec_in) | copy-start | bytes 147460
  17.7 1.9 %copy-start.6 = (bf16[64,384]{1,0:T(8,128)(2,1)S(1)}, bf16[64,384]{1,0:T(8,128)(2,1)}, u32[]{:S(2)}) copy-start(bf16[64,384]{1,0:T(8,128)(2,1)} %get-tuple-element.18.own_near_ref) | copy-start | bytes 147460
  17.7 1.9 %collective-permute-start.6 = (bf16[640,384]{1,0:T(8,128)(2,1)S(1)}, bf16[640,384]{1,0:T(8,128)(2,1)S(1)}, u32[]{:S(2)}, u32[]{:S(2)}) collective-permute-start(bf16[640,384]{1,0:T(8,128)(2,1)S(1)} %shard_map.78._.refs_0_.refs_4_), channel_id=1, source_target_pairs={{0,1},{1,0},{2,3},{3,2},{4,5},{5,4},{6,7},{7,6},{8,9},{9,8},{10,11... | collective-permute-start | bytes 1474568 | tf_op jit(solution)/shard_map/ppermute | solution.py:558
  17.8 17.2 %collective-permute-start.13 = (bf16[512,384]{1,0:T(8,128)(2,1)S(1)}, bf16[512,384]{1,0:T(8,128)(2,1)S(1)}, u32[]{:S(2)}, u32[]{:S(2)}) collective-permute-start(bf16[512,384]{1,0:T(8,128)(2,1)S(1)} %shard_map.79.qg_ref.refs_0_), channel_id=1, source_target_pairs={{0,2},{1,3},{2,0},{3,1},{4,6},{5,7},{6,4},{7,5},{8,10},{9,11},{10,... | collective-permute-start | bytes 1179656 | tf_op jit(solution)/shard_map/ppermute | solution.py:558
  22.2 11.2 %collective-permute-start.9 = (bf16[96,384]{1,0:T(8,128)(2,1)S(1)}, bf16[96,384]{1,0:T(8,128)(2,1)S(1)}, u32[]{:S(2)}, u32[]{:S(2)}) collective-permute-start(bf16[96,384]{1,0:T(8,128)(2,1)S(1)} %get-tuple-element.23), channel_id=1, source_target_pairs={{0,6},{1,7},{2,4},{3,5},{4,2},{5,3},{6,0},{7,1},{8,14},{9,15},{10,... | collective-permute-start | bytes 221192 | tf_op jit(solution)/shard_map/ppermute | solution.py:558
  24.4 9.0 %collective-permute-start.10 = (bf16[96,384]{1,0:T(8,128)(2,1)S(1)}, bf16[96,384]{1,0:T(8,128)(2,1)S(1)}, u32[]{:S(2)}, u32[]{:S(2)}) collective-permute-start(bf16[96,384]{1,0:T(8,128)(2,1)S(1)} %get-tuple-element.23), channel_id=1, source_target_pairs={{0,4},{1,5},{2,6},{3,7},{4,0},{5,1},{6,2},{7,3},{8,12},{9,13},{10,... | collective-permute-start | bytes 221192 | tf_op jit(solution)/shard_map/ppermute | solution.py:558
  24.9 8.6 %collective-permute-start.8 = (f32[16,640]{1,0:T(8,128)S(1)}, f32[16,640]{1,0:T(8,128)S(1)}, u32[]{:S(2)}, u32[]{:S(2)}) collective-permute-start(f32[16,640]{1,0:T(8,128)S(1)} %get-tuple-element.19.pay_ref.refs_1_.refs_0_), channel_id=1, source_target_pairs={{0,2},{1,3},{2,0},{3,1},{4,6},{5,7},{6,4},{7,5},{8,10},{9,11},{10,... | collective-permute-start | bytes 122888 | tf_op jit(solution)/shard_map/ppermute | solution.py:558
  33.5 1.6 %collective-permute-start.12 = (bf16[192,384]{1,0:T(8,128)(2,1)S(1)}, bf16[192,384]{1,0:T(8,128)(2,1)S(1)}, u32[]{:S(2)}, u32[]{:S(2)}) collective-permute-start(bf16[192,384]{1,0:T(8,128)(2,1)S(1)} %get-tuple-element.25.refs_2_.refs_5_), channel_id=1, source_target_pairs={{0,1},{1,0},{2,3},{3,2},{4,5},{5,4},{6,7},{7,6},{8,9},{9,8},{10,11... | collective-permute-start | bytes 442376 | tf_op jit(solution)/shard_map/ppermute | solution.py:558
  33.5 1.5 %collective-permute-start.11 = (f32[32,640]{1,0:T(8,128)S(1)}, f32[32,640]{1,0:T(8,128)S(1)}, u32[]{:S(2)}, u32[]{:S(2)}) collective-permute-start(f32[32,640]{1,0:T(8,128)S(1)} %get-tuple-element.24.refs_0_.refs_3_), channel_id=1, source_target_pairs={{0,1},{1,0},{2,3},{3,2},{4,5},{5,4},{6,7},{7,6},{8,9},{9,8},{10,11... | collective-permute-start | bytes 245768 | tf_op jit(solution)/shard_map/ppermute | solution.py:558
  34.0 4.9 %collective-permute-start.7 = (bf16[512,384]{1,0:T(8,128)(2,1)S(1)}, bf16[512,384]{1,0:T(8,128)(2,1)S(1)}, u32[]{:S(2)}, u32[]{:S(2)}) collective-permute-start(bf16[512,384]{1,0:T(8,128)(2,1)S(1)} %shard_map.79.qg_ref.refs_0_), channel_id=1, source_target_pairs={{0,1},{1,0},{2,3},{3,2},{4,5},{5,4},{6,7},{7,6},{8,9},{9,8},{10,11... | collective-permute-start | bytes 1179656 | tf_op jit(solution)/shard_map/ppermute | solution.py:558
  35.1 3.9 %collective-permute-start.14 = (bf16[512,384]{1,0:T(8,128)(2,1)S(1)}, bf16[512,384]{1,0:T(8,128)(2,1)S(1)}, u32[]{:S(2)}, u32[]{:S(2)}) collective-permute-start(bf16[512,384]{1,0:T(8,128)(2,1)S(1)} %shard_map.85.refs_1_), channel_id=1, source_target_pairs={{0,1},{1,0},{2,3},{3,2},{4,5},{5,4},{6,7},{7,6},{8,9},{9,8},{10,11... | collective-permute-start | bytes 1179656 | tf_op jit(solution)/shard_map/ppermute | solution.py:558
  35.5 7.4 %collective-permute-start.15 = (bf16[80,384]{1,0:T(8,128)(2,1)S(1)}, bf16[80,384]{1,0:T(8,128)(2,1)S(1)}, u32[]{:S(2)}, u32[]{:S(2)}) collective-permute-start(bf16[80,384]{1,0:T(8,128)(2,1)S(1)} %shard_map.84._.refs_0_), channel_id=1, source_target_pairs={{0,24},{8,16},{16,8},{24,0},{1,25},{9,17},{17,9},{25,1},{2,26},{10... | collective-permute-start | bytes 184328 | tf_op jit(solution)/shard_map/ppermute | solution.py:558
  37.9 4.9 %collective-permute-start.16 = (bf16[80,384]{1,0:T(8,128)(2,1)S(1)}, bf16[80,384]{1,0:T(8,128)(2,1)S(1)}, u32[]{:S(2)}, u32[]{:S(2)}) collective-permute-start(bf16[80,384]{1,0:T(8,128)(2,1)S(1)} %shard_map.84._.refs_0_), channel_id=1, source_target_pairs={{0,16},{8,24},{16,0},{24,8},{1,17},{9,25},{17,1},{25,9},{2,18},{10... | collective-permute-start | bytes 184328 | tf_op jit(solution)/shard_map/ppermute | solution.py:558
  38.4 4.4 %collective-permute-start.17 = (bf16[80,384]{1,0:T(8,128)(2,1)S(1)}, bf16[80,384]{1,0:T(8,128)(2,1)S(1)}, u32[]{:S(2)}, u32[]{:S(2)}) collective-permute-start(bf16[80,384]{1,0:T(8,128)(2,1)S(1)} %shard_map.84._.refs_0_), channel_id=1, source_target_pairs={{0,8},{8,0},{16,24},{24,16},{1,9},{9,1},{17,25},{25,17},{2,10},{10... | collective-permute-start | bytes 184328 | tf_op jit(solution)/shard_map/ppermute | solution.py:558

commit v7 on v6

--- a/solution.py
+++ b/solution.py
@@ -596,7 +596,7 @@
         known, next_k, next_v, *near_came, us=0.2,
     )
     kv_parts = own_kv + [stacked, across(stacked, "ctxb", 1)]
-    (qg,) = call(merge_kernel, both, queries, grad_out, stacked, us=0.3)
+    (qg,) = call(merge_kernel, both, queries, grad_out, near_came[0], us=0.3)
     next_qg = across(qg, "ctxb", 2)
     core_qg = across(qg, "ctxb", 1)
     pay, far = call(

time: 45 us -> 45 us (level)
  no operation moved by 1% of the time
where the time goes in v7:
time: 45 us; the launch traced here: 44.9 us
  Pallas kernels  19.4 us (43%)
  starting transfers between devices  17.9 us (40%)
  waiting for transfers between devices  6.68 us (15%)
  between operations  0.86 us (2%)
    pallas_call x12, Pallas kernels, call(): pl.pallas_call(kernel, out_shape=tuple((jax.ShapeDtypeStruct(shape, dtype...  19.4 us
    ppermute x18, starting transfers between devices, across(): lax.ppermute(value, axis, [(source, source ^ mask) for source in range(si...  17.9 us
    ppermute x18, waiting for transfers between devices, across(): lax.ppermute(value, axis, [(source, source ^ mask) for source in range(si...  6.68 us
  transfers between devices with their start and end apart: 18, of which 4 were waited for; matrix products, arithmetic and copies ran while one was open for 0% of the time, Pallas kernels for 39%

profile of v7, /device:TPU:0, one launch (start us, length us, event | category | flops | bytes accessed | tf_op | source)
XLA Modules:
  0.0 44.9 jit_solution(210157856789775819)
XLA Ops:
  0.7 0.5 %collective-permute-start.1 = (bf16[256,384]{1,0:T(8,128)(2,1)}, bf16[256,384]{1,0:T(8,128)(2,1)S(1)}, u32[]{:S(2)}, u32[]{:S(2)}) collective-permute-start(bf16[256,384]{1,0:T(8,128)(2,1)} %k_ref.7), channel_id=1, source_target_pairs={{0,1},{1,0},{2,3},{3,2},{4,5},{5,4},{6,7},{7,6},{8,9},{9,8},{10,11... | collective-permute-start | bytes 589832 | tf_op jit(solution)/shard_map/ppermute | solution.py:558
  1.2 0.1 collective-permute-start.2
  1.3 3.0 %collective-permute-start.3 = (bf16[256,384]{1,0:T(8,128)(2,1)}, bf16[256,384]{1,0:T(8,128)(2,1)S(1)}, u32[]{:S(2)}, u32[]{:S(2)}) collective-permute-start(bf16[256,384]{1,0:T(8,128)(2,1)} %k_ref.7), channel_id=1, source_target_pairs={{0,2},{1,3},{2,0},{3,1},{4,6},{5,7},{6,4},{7,5},{8,10},{9,11},{10,... | collective-permute-start | bytes 589832 | tf_op jit(solution)/shard_map/ppermute | solution.py:558
  4.3 0.0 collective-permute-start.4
  4.3 2.3 %shard_map.76 = (bf16[64,384]{1,0:T(8,128)(2,1)}, bf16[64,384]{1,0:T(8,128)(2,1)}, bf16[64,384]{1,0:T(8,128)(2,1)}) custom-call(s32[6]{0:T(128)} %off_ref.11, bf16[256,384]{1,0:T(8,128)(2,1)} %q_ref.5, bf16[256,384]{1,0:T(8,128)(2,1)} %k_ref.7, bf16[256,384]{1,0:T(8,128)(2,1)} %v_ref.7, bf16[256,384]{1,0:T(8,128)(2,1)} %g_ref.5), custom_call_target="tpu_custom_call" | custom-call | flops 1495000064 | tf_op jit(solution)/shard_map/pallas_call | solution.py:543
  6.6 0.0 copy-start.4
  6.6 4.1 %collective-permute-start = (bf16[64,384]{1,0:T(8,128)(2,1)}, bf16[64,384]{1,0:T(8,128)(2,1)S(1)}, u32[]{:S(2)}, u32[]{:S(2)}) collective-permute-start(bf16[64,384]{1,0:T(8,128)(2,1)} %get-tuple-element.16), channel_id=1, source_target_pairs={{0,6},{1,7},{2,4},{3,5},{4,2},{5,3},{6,0},{7,1},{8,14},{9,15},{10,... | collective-permute-start | bytes 147464 | tf_op jit(solution)/shard_map/ppermute | solution.py:558
  10.7 0.0 collective-permute-done.1.refs_2_
  10.7 1.9 %shard_map.78.first_ref.known_ref = f32[24,256]{1,0:T(8,128)S(1)} custom-call(s32[6]{0:T(128)S(1)} %copy-done.4, bf16[256,384]{1,0:T(8,128)(2,1)S(1)} %copy-done, bf16[256,384]{1,0:T(8,128)(2,1)S(1)} %copy-done.1, bf16[256,384]{1,0:T(8,128)(2,1)S(1)} %copy-done.2, bf16[256,384]{1,0:T(8,128)(2,1)S(1)} %copy-done.3, ...), custom_call_target="tpu_custom_call" | custom-call | flops 2529999872 | tf_op jit(solution)/shard_map/pallas_call | solution.py:543
  12.6 5.0 %collective-permute-done._.refs_2_ = bf16[64,384]{1,0:T(8,128)(2,1)S(1)} collective-permute-done((bf16[64,384]{1,0:T(8,128)(2,1)}, bf16[64,384]{1,0:T(8,128)(2,1)S(1)}, u32[]{:S(2)}, u32[]{:S(2)}) %collective-permute-start) | collective-permute-done | bytes 49184 | tf_op jit(solution)/shard_map/ppermute | solution.py:558
  17.7 0.0 copy-start.5
  17.7 0.0 copy-start.6
  17.7 0.1 collective-permute-start.6
  17.8 1.1 %collective-permute-start.13 = (bf16[512,384]{1,0:T(8,128)(2,1)S(1)}, bf16[512,384]{1,0:T(8,128)(2,1)S(1)}, u32[]{:S(2)}, u32[]{:S(2)}) collective-permute-start(bf16[512,384]{1,0:T(8,128)(2,1)S(1)} %shard_map.77.qg_ref.refs_0_), channel_id=1, source_target_pairs={{0,2},{1,3},{2,0},{3,1},{4,6},{5,7},{6,4},{7,5},{8,10},{9,11},{10,... | collective-permute-start | bytes 1179656 | tf_op jit(solution)/shard_map/ppermute | solution.py:558
  19.0 0.7 %collective-permute-done.6.refs_1_.refs_5_ = bf16[640,384]{1,0:T(8,128)(2,1)S(1)} collective-permute-done((bf16[640,384]{1,0:T(8,128)(2,1)S(1)}, bf16[640,384]{1,0:T(8,128)(2,1)S(1)}, u32[]{:S(2)}, u32[]{:S(2)}) %collective-permute-start.6) | collective-permute-done | bytes 491552 | tf_op jit(solution)/shard_map/ppermute | solution.py:558
  19.6 2.6 %shard_map.80 = (f32[16,640]{1,0:T(8,128)S(1)}, bf16[96,384]{1,0:T(8,128)(2,1)S(1)}) custom-call(s32[6]{0:T(128)S(1)} %copy-done.4, bf16[256,384]{1,0:T(8,128)(2,1)S(1)} %copy-done, bf16[256,384]{1,0:T(8,128)(2,1)S(1)} %copy-done.1, f32[24,256]{1,0:T(8,128)S(1)} %shard_map.78.first_ref.known_ref, bf16[64,384]{1,0:T(8,128)(2,1)S(1)} %copy-done.5, ...), custom_call_target="tpu_custom_call" | custom-call | flops 2875000064 | tf_op jit(solution)/shard_map/pallas_call | solution.py:543
  22.2 2.1 %collective-permute-start.9 = (bf16[96,384]{1,0:T(8,128)(2,1)S(1)}, bf16[96,384]{1,0:T(8,128)(2,1)S(1)}, u32[]{:S(2)}, u32[]{:S(2)}) collective-permute-start(bf16[96,384]{1,0:T(8,128)(2,1)S(1)} %get-tuple-element.23), channel_id=1, source_target_pairs={{0,6},{1,7},{2,4},{3,5},{4,2},{5,3},{6,0},{7,1},{8,14},{9,15},{10,... | collective-permute-start | bytes 221192 | tf_op jit(solution)/shard_map/ppermute | solution.py:558
  24.4 0.5 %collective-permute-start.10 = (bf16[96,384]{1,0:T(8,128)(2,1)S(1)}, bf16[96,384]{1,0:T(8,128)(2,1)S(1)}, u32[]{:S(2)}, u32[]{:S(2)}) collective-permute-start(bf16[96,384]{1,0:T(8,128)(2,1)S(1)} %get-tuple-element.23), channel_id=1, source_target_pairs={{0,4},{1,5},{2,6},{3,7},{4,0},{5,1},{6,2},{7,3},{8,12},{9,13},{10,... | collective-permute-start | bytes 221192 | tf_op jit(solution)/shard_map/ppermute | solution.py:558
  24.9 1.8 %collective-permute-start.8 = (f32[16,640]{1,0:T(8,128)S(1)}, f32[16,640]{1,0:T(8,128)S(1)}, u32[]{:S(2)}, u32[]{:S(2)}) collective-permute-start(f32[16,640]{1,0:T(8,128)S(1)} %get-tuple-element.19.pay_ref.refs_1_.refs_0_), channel_id=1, source_target_pairs={{0,2},{1,3},{2,0},{3,1},{4,6},{5,7},{6,4},{7,5},{8,10},{9,11},{10,... | collective-permute-start | bytes 122888 | tf_op jit(solution)/shard_map/ppermute | solution.py:558
  26.7 4.6 %shard_map.81 = (f32[256,384]{1,0:T(8,128)S(1)}, f32[4,384]{1,0:T(4,128)S(1)}) custom-call(s32[6]{0:T(128)S(1)} %copy-done.4, bf16[512,384]{1,0:T(8,128)(2,1)S(1)} %shard_map.77.qg_ref.refs_0_, bf16[64,384]{1,0:T(8,128)(2,1)S(1)} %copy-done.5, f32[16,640]{1,0:T(8,128)S(1)} %get-tuple-element.19.pay_ref.refs_1_.refs_0_, bf16[256,384]{1,0:T(8,128)(2,1)S(1)} %copy-done.2, ...), custom_call_target="tpu_custom_call" | custom-call | flops 5750000128 | tf_op jit(solution)/shard_map/pallas_call | solution.py:543
  31.3 2.0 %shard_map.82 = (f32[256,384]{1,0:T(8,128)S(1)}, f32[256,384]{1,0:T(8,128)S(1)}) custom-call(s32[6]{0:T(128)S(1)} %copy-done.4, bf16[256,384]{1,0:T(8,128)(2,1)S(1)} %copy-done.2, bf16[256,384]{1,0:T(8,128)(2,1)S(1)} %copy-done.3, bf16[512,384]{1,0:T(8,128)(2,1)S(1)} %shard_map.77.qg_ref.refs_0_, f32[16,640]{1,0:T(8,128)S(1)} %get-tuple-element.19.pay_ref.refs_1_.refs_0_), custom_call_target="tpu_custom_call" | custom-call | flops 1495000064 | tf_op jit(solution)/shard_map/pallas_call | solution.py:543
  33.3 0.1 collective-permute-done.8.refs_1_
  33.5 0.1 collective-permute-start.12
  33.5 0.5 %collective-permute-start.11 = (f32[32,640]{1,0:T(8,128)S(1)}, f32[32,640]{1,0:T(8,128)S(1)}, u32[]{:S(2)}, u32[]{:S(2)}) collective-permute-start(f32[32,640]{1,0:T(8,128)S(1)} %get-tuple-element.24.refs_0_.refs_3_), channel_id=1, source_target_pairs={{0,1},{1,0},{2,3},{3,2},{4,5},{5,4},{6,7},{7,6},{8,9},{9,8},{10,11... | collective-permute-start | bytes 245768 | tf_op jit(solution)/shard_map/ppermute | solution.py:558
  34.0 0.1 collective-permute-start.7
  34.1 0.9 %collective-permute-done.11.refs_1_.refs_4_ = f32[32,640]{1,0:T(8,128)S(1)} collective-permute-done((f32[32,640]{1,0:T(8,128)S(1)}, f32[32,640]{1,0:T(8,128)S(1)}, u32[]{:S(2)}, u32[]{:S(2)}) %collective-permute-start.11) | collective-permute-done | bytes 81952 | tf_op jit(solution)/shard_map/ppermute | solution.py:558
  35.1 0.4 collective-permute-start.14
  35.5 2.4 %collective-permute-start.15 = (bf16[80,384]{1,0:T(8,128)(2,1)S(1)}, bf16[80,384]{1,0:T(8,128)(2,1)S(1)}, u32[]{:S(2)}, u32[]{:S(2)}) collective-permute-start(bf16[80,384]{1,0:T(8,128)(2,1)S(1)} %shard_map.84._.refs_0_), channel_id=1, source_target_pairs={{0,24},{8,16},{16,8},{24,0},{1,25},{9,17},{17,9},{25,1},{2,26},{10... | collective-permute-start | bytes 184328 | tf_op jit(solution)/shard_map/ppermute | solution.py:558
  37.9 0.5 %collective-permute-start.16 = (bf16[80,384]{1,0:T(8,128)(2,1)S(1)}, bf16[80,384]{1,0:T(8,128)(2,1)S(1)}, u32[]{:S(2)}, u32[]{:S(2)}) collective-permute-start(bf16[80,384]{1,0:T(8,128)(2,1)S(1)} %shard_map.84._.refs_0_), channel_id=1, source_target_pairs={{0,16},{8,24},{16,0},{24,8},{1,17},{9,25},{17,1},{25,9},{2,18},{10... | collective-permute-start | bytes 184328 | tf_op jit(solution)/shard_map/ppermute | solution.py:558
  38.4 0.5 %collective-permute-start.17 = (bf16[80,384]{1,0:T(8,128)(2,1)S(1)}, bf16[80,384]{1,0:T(8,128)(2,1)S(1)}, u32[]{:S(2)}, u32[]{:S(2)}) collective-permute-start(bf16[80,384]{1,0:T(8,128)(2,1)S(1)} %shard_map.84._.refs_0_), channel_id=1, source_target_pairs={{0,8},{8,0},{16,24},{24,16},{1,9},{9,1},{17,25},{25,17},{2,10},{10... | collective-permute-start | bytes 184328 | tf_op jit(solution)/shard_map/ppermute | solution.py:558
  39.0 3.9 %shard_map.86 = (f32[256,384]{1,0:T(8,128)S(1)}, f32[256,384]{1,0:T(8,128)S(1)}) custom-call(s32[6]{0:T(128)S(1)} %copy-done.4, bf16[256,384]{1,0:T(8,128)(2,1)S(1)} %copy-done.2, bf16[256,384]{1,0:T(8,128)(2,1)S(1)} %copy-done.3, bf16[512,384]{1,0:T(8,128)(2,1)S(1)} %collective-permute-done.7.refs_0_, bf16[512,384]{1,0:T(8,128)(2,1)S(1)} %shard_map.85.refs_1_, ...), custom_call_target="tpu_custom_call" | custom-call | flops 4600000000 | tf_op jit(solution)/shard_map/pallas_call | solution.py:543
  42.9 2.0 %shard_map.87 = (bf16[256,384]{1,0:T(8,128)(2,1)}, bf16[256,384]{1,0:T(8,128)(2,1)}, bf16[256,384]{1,0:T(8,128)(2,1)}) custom-call(s32[6]{0:T(128)S(1)} %copy-done.4, bf16[256,384]{1,0:T(8,128)(2,1)S(1)} %copy-done.2, bf16[256,384]{1,0:T(8,128)(2,1)S(1)} %copy-done.3, f32[256,384]{1,0:T(8,128)S(1)} %get-tuple-element.20.dq_in, ...), custom_call_target="tpu_custom_call" | custom-call | flops 3449999872 | tf_op jit(solution)/shard_map/pallas_call | solution.py:543
  (30 shorter events, 0.2 us)
Async XLA Ops:
  0.6 10.0 %copy-start.2 = (bf16[256,384]{1,0:T(8,128)(2,1)S(1)}, bf16[256,384]{1,0:T(8,128)(2,1)}, u32[]{:S(2)}) copy-start(bf16[256,384]{1,0:T(8,128)(2,1)} %k_ref.7) | copy-start | bytes 589828
  0.6 10.0 %copy-start.3 = (bf16[256,384]{1,0:T(8,128)(2,1)S(1)}, bf16[256,384]{1,0:T(8,128)(2,1)}, u32[]{:S(2)}) copy-start(bf16[256,384]{1,0:T(8,128)(2,1)} %v_ref.7) | copy-start | bytes 589828
  0.7 10.0 %copy-start = (bf16[256,384]{1,0:T(8,128)(2,1)S(1)}, bf16[256,384]{1,0:T(8,128)(2,1)}, u32[]{:S(2)}) copy-start(bf16[256,384]{1,0:T(8,128)(2,1)} %q_ref.5) | copy-start | bytes 589828
  0.7 10.0 %copy-start.1 = (bf16[256,384]{1,0:T(8,128)(2,1)S(1)}, bf16[256,384]{1,0:T(8,128)(2,1)}, u32[]{:S(2)}) copy-start(bf16[256,384]{1,0:T(8,128)(2,1)} %g_ref.5) | copy-start | bytes 589828
  0.7 10.0 %collective-permute-start.1 = (bf16[256,384]{1,0:T(8,128)(2,1)}, bf16[256,384]{1,0:T(8,128)(2,1)S(1)}, u32[]{:S(2)}, u32[]{:S(2)}) collective-permute-start(bf16[256,384]{1,0:T(8,128)(2,1)} %k_ref.7), channel_id=1, source_target_pairs={{0,1},{1,0},{2,3},{3,2},{4,5},{5,4},{6,7},{7,6},{8,9},{9,8},{10,11... | collective-permute-start | bytes 589832 | tf_op jit(solution)/shard_map/ppermute | solution.py:558
  1.2 9.5 %collective-permute-start.2 = (bf16[256,384]{1,0:T(8,128)(2,1)}, bf16[256,384]{1,0:T(8,128)(2,1)S(1)}, u32[]{:S(2)}, u32[]{:S(2)}) collective-permute-start(bf16[256,384]{1,0:T(8,128)(2,1)} %v_ref.7), channel_id=1, source_target_pairs={{0,1},{1,0},{2,3},{3,2},{4,5},{5,4},{6,7},{7,6},{8,9},{9,8},{10,11... | collective-permute-start | bytes 589832 | tf_op jit(solution)/shard_map/ppermute | solution.py:558
  1.3 16.3 %collective-permute-start.3 = (bf16[256,384]{1,0:T(8,128)(2,1)}, bf16[256,384]{1,0:T(8,128)(2,1)S(1)}, u32[]{:S(2)}, u32[]{:S(2)}) collective-permute-start(bf16[256,384]{1,0:T(8,128)(2,1)} %k_ref.7), channel_id=1, source_target_pairs={{0,2},{1,3},{2,0},{3,1},{4,6},{5,7},{6,4},{7,5},{8,10},{9,11},{10,... | collective-permute-start | bytes 589832 | tf_op jit(solution)/shard_map/ppermute | solution.py:558
  4.3 13.3 %collective-permute-start.4 = (bf16[256,384]{1,0:T(8,128)(2,1)}, bf16[256,384]{1,0:T(8,128)(2,1)S(1)}, u32[]{:S(2)}, u32[]{:S(2)}) collective-permute-start(bf16[256,384]{1,0:T(8,128)(2,1)} %v_ref.7), channel_id=1, source_target_pairs={{0,2},{1,3},{2,0},{3,1},{4,6},{5,7},{6,4},{7,5},{8,10},{9,11},{10,... | collective-permute-start | bytes 589832 | tf_op jit(solution)/shard_map/ppermute | solution.py:558
  6.6 4.2 %copy-start.4 = (s32[6]{0:T(128)S(1)}, s32[6]{0:T(128)}, u32[]{:S(2)}) copy-start(s32[6]{0:T(128)} %off_ref.11) | copy-start | bytes 76
  6.6 11.0 %collective-permute-start = (bf16[64,384]{1,0:T(8,128)(2,1)}, bf16[64,384]{1,0:T(8,128)(2,1)S(1)}, u32[]{:S(2)}, u32[]{:S(2)}) collective-permute-start(bf16[64,384]{1,0:T(8,128)(2,1)} %get-tuple-element.16), channel_id=1, source_target_pairs={{0,6},{1,7},{2,4},{3,5},{4,2},{5,3},{6,0},{7,1},{8,14},{9,15},{10,... | collective-permute-start | bytes 147464 | tf_op jit(solution)/shard_map/ppermute | solution.py:558
  10.7 6.9 %collective-permute-start.5 = (bf16[64,384]{1,0:T(8,128)(2,1)}, bf16[64,384]{1,0:T(8,128)(2,1)S(1)}, u32[]{:S(2)}, u32[]{:S(2)}) collective-permute-start(bf16[64,384]{1,0:T(8,128)(2,1)} %get-tuple-element.16), channel_id=1, source_target_pairs={{0,4},{1,5},{2,6},{3,7},{4,0},{5,1},{6,2},{7,3},{8,12},{9,13},{10,... | collective-permute-start | bytes 147464 | tf_op jit(solution)/shard_map/ppermute | solution.py:558
  17.7 2.0 %copy-start.5 = (bf16[64,384]{1,0:T(8,128)(2,1)S(1)}, bf16[64,384]{1,0:T(8,128)(2,1)}, u32[]{:S(2)}) copy-start(bf16[64,384]{1,0:T(8,128)(2,1)} %get-tuple-element.17.spec_ref.spec_in) | copy-start | bytes 147460
  17.7 1.9 %copy-start.6 = (bf16[64,384]{1,0:T(8,128)(2,1)S(1)}, bf16[64,384]{1,0:T(8,128)(2,1)}, u32[]{:S(2)}) copy-start(bf16[64,384]{1,0:T(8,128)(2,1)} %get-tuple-element.18.own_near_ref) | copy-start | bytes 147460
  17.7 1.9 %collective-permute-start.6 = (bf16[640,384]{1,0:T(8,128)(2,1)S(1)}, bf16[640,384]{1,0:T(8,128)(2,1)S(1)}, u32[]{:S(2)}, u32[]{:S(2)}) collective-permute-start(bf16[640,384]{1,0:T(8,128)(2,1)S(1)} %shard_map.79.refs_0_.refs_4_), channel_id=1, source_target_pairs={{0,1},{1,0},{2,3},{3,2},{4,5},{5,4},{6,7},{7,6},{8,9},{9,8},{10,11... | collective-permute-start | bytes 1474568 | tf_op jit(solution)/shard_map/ppermute | solution.py:558
  17.8 17.2 %collective-permute-start.13 = (bf16[512,384]{1,0:T(8,128)(2,1)S(1)}, bf16[512,384]{1,0:T(8,128)(2,1)S(1)}, u32[]{:S(2)}, u32[]{:S(2)}) collective-permute-start(bf16[512,384]{1,0:T(8,128)(2,1)S(1)} %shard_map.77.qg_ref.refs_0_), channel_id=1, source_target_pairs={{0,2},{1,3},{2,0},{3,1},{4,6},{5,7},{6,4},{7,5},{8,10},{9,11},{10,... | collective-permute-start | bytes 1179656 | tf_op jit(solution)/shard_map/ppermute | solution.py:558
  22.2 11.2 %collective-permute-start.9 = (bf16[96,384]{1,0:T(8,128)(2,1)S(1)}, bf16[96,384]{1,0:T(8,128)(2,1)S(1)}, u32[]{:S(2)}, u32[]{:S(2)}) collective-permute-start(bf16[96,384]{1,0:T(8,128)(2,1)S(1)} %get-tuple-element.23), channel_id=1, source_target_pairs={{0,6},{1,7},{2,4},{3,5},{4,2},{5,3},{6,0},{7,1},{8,14},{9,15},{10,... | collective-permute-start | bytes 221192 | tf_op jit(solution)/shard_map/ppermute | solution.py:558
  24.4 9.0 %collective-permute-start.10 = (bf16[96,384]{1,0:T(8,128)(2,1)S(1)}, bf16[96,384]{1,0:T(8,128)(2,1)S(1)}, u32[]{:S(2)}, u32[]{:S(2)}) collective-permute-start(bf16[96,384]{1,0:T(8,128)(2,1)S(1)} %get-tuple-element.23), channel_id=1, source_target_pairs={{0,4},{1,5},{2,6},{3,7},{4,0},{5,1},{6,2},{7,3},{8,12},{9,13},{10,... | collective-permute-start | bytes 221192 | tf_op jit(solution)/shard_map/ppermute | solution.py:558
  24.9 8.6 %collective-permute-start.8 = (f32[16,640]{1,0:T(8,128)S(1)}, f32[16,640]{1,0:T(8,128)S(1)}, u32[]{:S(2)}, u32[]{:S(2)}) collective-permute-start(f32[16,640]{1,0:T(8,128)S(1)} %get-tuple-element.19.pay_ref.refs_1_.refs_0_), channel_id=1, source_target_pairs={{0,2},{1,3},{2,0},{3,1},{4,6},{5,7},{6,4},{7,5},{8,10},{9,11},{10,... | collective-permute-start | bytes 122888 | tf_op jit(solution)/shard_map/ppermute | solution.py:558
  33.5 1.6 %collective-permute-start.12 = (bf16[192,384]{1,0:T(8,128)(2,1)S(1)}, bf16[192,384]{1,0:T(8,128)(2,1)S(1)}, u32[]{:S(2)}, u32[]{:S(2)}) collective-permute-start(bf16[192,384]{1,0:T(8,128)(2,1)S(1)} %get-tuple-element.25.refs_2_.refs_5_), channel_id=1, source_target_pairs={{0,1},{1,0},{2,3},{3,2},{4,5},{5,4},{6,7},{7,6},{8,9},{9,8},{10,11... | collective-permute-start | bytes 442376 | tf_op jit(solution)/shard_map/ppermute | solution.py:558
  33.5 1.5 %collective-permute-start.11 = (f32[32,640]{1,0:T(8,128)S(1)}, f32[32,640]{1,0:T(8,128)S(1)}, u32[]{:S(2)}, u32[]{:S(2)}) collective-permute-start(f32[32,640]{1,0:T(8,128)S(1)} %get-tuple-element.24.refs_0_.refs_3_), channel_id=1, source_target_pairs={{0,1},{1,0},{2,3},{3,2},{4,5},{5,4},{6,7},{7,6},{8,9},{9,8},{10,11... | collective-permute-start | bytes 245768 | tf_op jit(solution)/shard_map/ppermute | solution.py:558
  34.0 4.9 %collective-permute-start.7 = (bf16[512,384]{1,0:T(8,128)(2,1)S(1)}, bf16[512,384]{1,0:T(8,128)(2,1)S(1)}, u32[]{:S(2)}, u32[]{:S(2)}) collective-permute-start(bf16[512,384]{1,0:T(8,128)(2,1)S(1)} %shard_map.77.qg_ref.refs_0_), channel_id=1, source_target_pairs={{0,1},{1,0},{2,3},{3,2},{4,5},{5,4},{6,7},{7,6},{8,9},{9,8},{10,11... | collective-permute-start | bytes 1179656 | tf_op jit(solution)/shard_map/ppermute | solution.py:558
  35.1 3.9 %collective-permute-start.14 = (bf16[512,384]{1,0:T(8,128)(2,1)S(1)}, bf16[512,384]{1,0:T(8,128)(2,1)S(1)}, u32[]{:S(2)}, u32[]{:S(2)}) collective-permute-start(bf16[512,384]{1,0:T(8,128)(2,1)S(1)} %shard_map.85.refs_1_), channel_id=1, source_target_pairs={{0,1},{1,0},{2,3},{3,2},{4,5},{5,4},{6,7},{7,6},{8,9},{9,8},{10,11... | collective-permute-start | bytes 1179656 | tf_op jit(solution)/shard_map/ppermute | solution.py:558
  35.5 7.4 %collective-permute-start.15 = (bf16[80,384]{1,0:T(8,128)(2,1)S(1)}, bf16[80,384]{1,0:T(8,128)(2,1)S(1)}, u32[]{:S(2)}, u32[]{:S(2)}) collective-permute-start(bf16[80,384]{1,0:T(8,128)(2,1)S(1)} %shard_map.84._.refs_0_), channel_id=1, source_target_pairs={{0,24},{8,16},{16,8},{24,0},{1,25},{9,17},{17,9},{25,1},{2,26},{10... | collective-permute-start | bytes 184328 | tf_op jit(solution)/shard_map/ppermute | solution.py:558
  37.9 4.9 %collective-permute-start.16 = (bf16[80,384]{1,0:T(8,128)(2,1)S(1)}, bf16[80,384]{1,0:T(8,128)(2,1)S(1)}, u32[]{:S(2)}, u32[]{:S(2)}) collective-permute-start(bf16[80,384]{1,0:T(8,128)(2,1)S(1)} %shard_map.84._.refs_0_), channel_id=1, source_target_pairs={{0,16},{8,24},{16,0},{24,8},{1,17},{9,25},{17,1},{25,9},{2,18},{10... | collective-permute-start | bytes 184328 | tf_op jit(solution)/shard_map/ppermute | solution.py:558
  38.4 4.4 %collective-permute-start.17 = (bf16[80,384]{1,0:T(8,128)(2,1)S(1)}, bf16[80,384]{1,0:T(8,128)(2,1)S(1)}, u32[]{:S(2)}, u32[]{:S(2)}) collective-permute-start(bf16[80,384]{1,0:T(8,128)(2,1)S(1)} %shard_map.84._.refs_0_), channel_id=1, source_target_pairs={{0,8},{8,0},{16,24},{24,16},{1,9},{9,1},{17,25},{25,17},{2,10},{10... | collective-permute-start | bytes 184328 | tf_op jit(solution)/shard_map/ppermute | solution.py:558

commit v8 on v6

--- a/solution.py
+++ b/solution.py
@@ -76,47 +76,48 @@
     return (tiles * weight[None]).reshape(rows, columns)
 
 
-def pack_kernel(
-    off_in, q_ref, k_ref, v_ref, g_ref, near_kv_ref, near_qg_ref, spec_ref,
-    off_ref, buffer, sems, off_sem,
-):
-    rows, width = q_ref.shape
-    heads = width // HD
-    near_rows, spec_rows = rows // MIDDLE, rows // UPPER
-    places = (
-        (k_ref, 0, near_kv_ref, 0, 1),
-        (v_ref, 1, near_kv_ref, 1, 2),
-        (q_ref, 2, near_qg_ref, 0, 0),
-        (g_ref, 3, near_qg_ref, 1, 3),
-    )
-    off_copy = pltpu.make_async_copy(off_in, off_ref, off_sem)
-    off_copy.start()
-    copies = [
-        pltpu.make_async_copy(source, buffer.at[index], sems.at[index])
-        for source, index, _, _, _ in places
-    ]
-    for copy in copies:
-        copy.start()
-    off_copy.wait()
+def keep_rows(off_ref, read, near_ref, spec_ref):
+    near_rows, width = near_ref.shape[0] // 2, near_ref.shape[1]
+    rows, heads = near_rows * MIDDLE, width // HD
+    spec_rows, step = rows // UPPER, UPPER // MIDDLE
     offsets = lane_offsets(off_ref, heads, width)
     middle = iota((rows, width), 0) % MIDDLE == offsets % MIDDLE
     index = iota((near_rows, width), 0)
     gather = jnp.where(
         iota((near_rows, rows), 1) // MIDDLE == iota((near_rows, rows), 0), 1.0, 0.0
     ).astype(BF16)
-    spec_ref[...] = jnp.zeros(spec_ref.shape, BF16)
-    for (_, source, near_ref, slot, kind), copy in zip(places, copies):
-        copy.wait()
-        whole = buffer[source].astype(F32)
+    for slot in range(2):
+        whole = read(slot).astype(F32)
         kept = dot_nn(gather, jnp.where(middle, whole, 0.0).astype(BF16))
         near_ref[slot * near_rows : (slot + 1) * near_rows, :] = kept.astype(BF16)
-        step = UPPER // MIDDLE
         top = jnp.where(index % step == offsets // MIDDLE, kept, 0.0)
         top = top.reshape(spec_rows, step, width).sum(axis=1)
         pad = jnp.zeros((SPEC_PAD - spec_rows, width), F32)
-        spec_ref[kind * SPEC_PAD : (kind + 1) * SPEC_PAD, :] = jnp.concatenate(
+        spec_ref[slot * SPEC_PAD : (slot + 1) * SPEC_PAD, :] = jnp.concatenate(
             [top, pad], axis=0
         ).astype(BF16)
+
+
+def pack_kernel(off_in, k_ref, v_ref, near_ref, spec_ref, off_ref, buffer, sems, off_sem):
+    copies = [
+        pltpu.make_async_copy(source, buffer.at[index], sems.at[index])
+        for index, source in enumerate((k_ref, v_ref))
+    ]
+    off_copy = pltpu.make_async_copy(off_in, off_ref, off_sem)
+    off_copy.start()
+    for copy in copies:
+        copy.start()
+    off_copy.wait()
+
+    def read(slot):
+        copies[slot].wait()
+        return buffer[slot]
+
+    keep_rows(off_ref, read, near_ref, spec_ref)
+
+
+def choose_kernel(off_ref, q_ref, g_ref, near_ref, spec_ref):
+    keep_rows(off_ref, lambda slot: (q_ref, g_ref)[slot][...], near_ref, spec_ref)
 
 
 def split_terms(value):
@@ -200,7 +201,7 @@
             out_ref[row : row + 1, :] = term
 
 
-def forward_kernel(near_count, off_ref, q_ref, g_ref, known_ref, spec_ref, own_near_ref, *refs):
+def forward_kernel(near_count, off_ref, q_ref, g_ref, known_ref, kv_ref, qg_ref, own_near_ref, *refs):
     k_refs, v_refs, near_refs = next_refs(refs[:-2], q_ref.shape[0])
     out_ref, far_ref = refs[-2:]
     rows, width = q_ref.shape
@@ -239,7 +240,8 @@
     row = iota((STAT_ROWS, width), 0)
     place = iota((1, width), 1) % HD
     lines = [
-        spec_ref[kind * SPEC_PAD : kind * SPEC_PAD + spec_rows, :].astype(F32) for kind in range(4)
+        ref[slot * SPEC_PAD : slot * SPEC_PAD + spec_rows, :].astype(F32)
+        for ref, slot in ((qg_ref, 0), (kv_ref, 0), (kv_ref, 1), (qg_ref, 1))
     ]
     for index in range(spec_rows):
         value = jnp.sum(
@@ -297,7 +299,7 @@
     for pair in range(heads // 2):
         lanes = slice(pair * PAIR, (pair + 1) * PAIR)
         both_q = jnp.concatenate([qg_ref[:rows, lanes], spec_in[:SPEC_PAD, lanes]], axis=0)
-        both_g = jnp.concatenate([qg_ref[rows:, lanes], spec_in[3 * SPEC_PAD :, lanes]], axis=0)
+        both_g = jnp.concatenate([qg_ref[rows:, lanes], spec_in[SPEC_PAD:, lanes]], axis=0)
         keys = [r[:, lanes] for r in k_refs]
         if near_count:
             keys.append(near_part(near_refs, 0, lanes))
@@ -338,7 +340,7 @@
         spec_ref[spec_rows:, lanes] = result[full : full + spec_rows]
 
 
-def stack_kernel(first_ref, *refs):
+def stack_kernel(first_ref, second_ref, *refs):
     out, low = refs[-1], 0
     for ref in refs[:-1]:
         rows = ref.shape[0]
@@ -566,22 +568,17 @@
 
     next_k, next_v = across(key_matrix, "ctxb", 2), across(value_matrix, "ctxb", 2)
     core_k, core_v = across(key_matrix, "ctxb", 1), across(value_matrix, "ctxb", 1)
-    near_kv, near_qg, spec = call(
-        pack_kernel,
-        [
-            ((2 * near_rows, width), BF16),
-            ((2 * near_rows, width), BF16),
-            ((4 * SPEC_PAD, width), BF16),
-        ],
-        offsets, queries, key_matrix, value_matrix, grad_out,
-        us=1.3, raw=True, vmem_mib=60,
+    chosen = [((2 * near_rows, width), BF16), ((2 * SPEC_PAD, width), BF16)]
+    near_kv, spec_kv = call(
+        pack_kernel, chosen, offsets, key_matrix, value_matrix, us=1.3, raw=True, vmem_mib=60,
         scratch=[
             pltpu.SMEM(offsets.shape, jnp.int32),
-            pltpu.VMEM((4, rows, width), BF16),
-            pltpu.SemaphoreType.DMA((4,)),
+            pltpu.VMEM((2, rows, width), BF16),
+            pltpu.SemaphoreType.DMA((2,)),
             pltpu.SemaphoreType.DMA,
         ],
     )
+    near_qg, spec_qg = call(choose_kernel, chosen, offsets, queries, grad_out, us=1.0)
     near_came = [across(near_kv, "ctxb", mask) for mask in reversed(range(GROUP, slots, 2))]
     both = [((2 * rows, width), BF16)]
     own_kv = [key_matrix, value_matrix, core_k, core_v]
@@ -593,7 +590,7 @@
     (stacked,) = call(
         stack_kernel,
         [((2 * rows + 2 * near_rows * len(near_came), width), BF16)],
-        known, next_k, next_v, *near_came, us=0.2,
+        known, spec_qg, next_k, next_v, *near_came, us=0.2,
     )
     kv_parts = own_kv + [stacked, across(stacked, "ctxb", 1)]
     (qg,) = call(merge_kernel, both, queries, grad_out, stacked, us=0.3)
@@ -605,12 +602,12 @@
             ((STAT_ROWS, rows + width), F32),
             ((2 * near_rows + 2 * STAT_ROWS, width), BF16),
         ],
-        offsets, queries, grad_out, known, spec, near_qg, *kv_parts[4:], us=2.5,
+        offsets, queries, grad_out, known, spec_kv, spec_qg, near_qg, *kv_parts[4:], us=2.5,
     )
     dq, dq_spec = call(
         partial(query_kernel, near_count),
         [((rows, width), F32), ((2 * spec_rows, width), F32)],
-        offsets, qg, spec, pay, *kv_parts, us=5.0,
+        offsets, qg, spec_qg, pay, *kv_parts, us=5.0,
     )
     pays_far = [pay, across(pay, "ctxb", 2)]
     far_came = [across(far, "ctxb", mask) for mask in reversed(range(GROUP, slots, 2))]

time: 45 us -> 44.9 us (level)
  waiting for transfers between devices: 6.68 us -> 6.21 us
    ppermute x18, waiting for transfers between devices: 6.68 us -> 6.21 us  [across(): lax.ppermute(value, axis, [(source, source ^ mask) for source in range(si...]
    pallas_call x12 -> x13, Pallas kernels: 19.4 us -> 19.8 us  [call(): pl.pallas_call(kernel, out_shape=tuple((jax.ShapeDtypeStruct(shape, dtype...]
  transfers between devices with their start and end apart: 18 -> 18, of which waited for: 4 -> 4; matrix products, arithmetic and copies ran while one was open for 0% -> 0% of each run, Pallas kernels for 39% -> 40%
where the time goes in v8:
time: 44.9 us; the launch traced here: 44.7 us
  Pallas kernels  19.8 us (44%)
  starting transfers between devices  17.8 us (40%)
  waiting for transfers between devices  6.21 us (14%)
  between operations  0.87 us (2%)
    pallas_call x13, Pallas kernels, call(): pl.pallas_call(kernel, out_shape=tuple((jax.ShapeDtypeStruct(shape, dtype...  19.8 us
    ppermute x18, starting transfers between devices, across(): lax.ppermute(value, axis, [(source, source ^ mask) for source in range(si...  17.8 us
    ppermute x18, waiting for transfers between devices, across(): lax.ppermute(value, axis, [(source, source ^ mask) for source in range(si...  6.21 us
  transfers between devices with their start and end apart: 18, of which 4 were waited for; matrix products, arithmetic and copies ran while one was open for 0% of the time, Pallas kernels for 40%

profile of v8, /device:TPU:0, one launch (start us, length us, event | category | flops | bytes accessed | tf_op | source)
XLA Modules:
  0.0 44.7 jit_solution(5665523714786886594)
XLA Ops:
  0.6 0.5 %collective-permute-start = (bf16[256,384]{1,0:T(8,128)(2,1)}, bf16[256,384]{1,0:T(8,128)(2,1)S(1)}, u32[]{:S(2)}, u32[]{:S(2)}) collective-permute-start(bf16[256,384]{1,0:T(8,128)(2,1)} %k_ref.7), channel_id=1, source_target_pairs={{0,1},{1,0},{2,3},{3,2},{4,5},{5,4},{6,7},{7,6},{8,9},{9,8},{10,11... | collective-permute-start | bytes 589832 | tf_op jit(solution)/shard_map/ppermute | solution.py:560
  1.2 2.7 %collective-permute-start.2 = (bf16[256,384]{1,0:T(8,128)(2,1)}, bf16[256,384]{1,0:T(8,128)(2,1)S(1)}, u32[]{:S(2)}, u32[]{:S(2)}) collective-permute-start(bf16[256,384]{1,0:T(8,128)(2,1)} %k_ref.7), channel_id=1, source_target_pairs={{0,2},{1,3},{2,0},{3,1},{4,6},{5,7},{6,4},{7,5},{8,10},{9,11},{10,... | collective-permute-start | bytes 589832 | tf_op jit(solution)/shard_map/ppermute | solution.py:560
  3.8 0.2 collective-permute-start.1
  4.0 0.3 collective-permute-start.3
  4.3 1.9 %shard_map.78 = (bf16[64,384]{1,0:T(8,128)(2,1)}, bf16[32,384]{1,0:T(8,128)(2,1)}) custom-call(s32[6]{0:T(128)} %off_ref.13, bf16[256,384]{1,0:T(8,128)(2,1)} %k_ref.7, bf16[256,384]{1,0:T(8,128)(2,1)} %v_ref.7), custom_call_target="tpu_custom_call" | custom-call | flops 1495000064 | tf_op jit(solution)/shard_map/pallas_call | solution.py:545
  6.2 0.0 copy-start.4
  6.2 0.0 copy-start.6
  6.2 3.8 %collective-permute-start.4 = (bf16[64,384]{1,0:T(8,128)(2,1)}, bf16[64,384]{1,0:T(8,128)(2,1)S(1)}, u32[]{:S(2)}, u32[]{:S(2)}) collective-permute-start(bf16[64,384]{1,0:T(8,128)(2,1)} %get-tuple-element.18), channel_id=1, source_target_pairs={{0,6},{1,7},{2,4},{3,5},{4,2},{5,3},{6,0},{7,1},{8,14},{9,15},{10,... | collective-permute-start | bytes 147464 | tf_op jit(solution)/shard_map/ppermute | solution.py:560
  10.1 0.7 %shard_map.77 = (bf16[64,384]{1,0:T(8,128)(2,1)S(1)}, bf16[32,384]{1,0:T(8,128)(2,1)S(1)}) custom-call(s32[6]{0:T(128)S(1)} %copy-done.4, bf16[256,384]{1,0:T(8,128)(2,1)S(1)} %copy-done, bf16[256,384]{1,0:T(8,128)(2,1)S(1)} %copy-done.1), custom_call_target="tpu_custom_call" | custom-call | flops 1150000000 | tf_op jit(solution)/shard_map/pallas_call | solution.py:545
  10.8 0.1 collective-permute-start.5
  10.9 1.9 %shard_map.76.first_ref.known_ref = f32[24,256]{1,0:T(8,128)S(1)} custom-call(s32[6]{0:T(128)S(1)} %copy-done.4, bf16[256,384]{1,0:T(8,128)(2,1)S(1)} %copy-done, bf16[256,384]{1,0:T(8,128)(2,1)S(1)} %copy-done.1, bf16[256,384]{1,0:T(8,128)(2,1)S(1)} %copy-done.2, bf16[256,384]{1,0:T(8,128)(2,1)S(1)} %copy-done.3, ...), custom_call_target="tpu_custom_call" | custom-call | flops 2529999872 | tf_op jit(solution)/shard_map/pallas_call | solution.py:545
  12.8 4.6 %collective-permute-done.4.refs_2_ = bf16[64,384]{1,0:T(8,128)(2,1)S(1)} collective-permute-done((bf16[64,384]{1,0:T(8,128)(2,1)}, bf16[64,384]{1,0:T(8,128)(2,1)S(1)}, u32[]{:S(2)}, u32[]{:S(2)}) %collective-permute-start.4) | collective-permute-done | bytes 49184 | tf_op jit(solution)/shard_map/ppermute | solution.py:560
  17.5 0.1 collective-permute-start.6
  17.6 1.2 %collective-permute-start.13 = (bf16[512,384]{1,0:T(8,128)(2,1)S(1)}, bf16[512,384]{1,0:T(8,128)(2,1)S(1)}, u32[]{:S(2)}, u32[]{:S(2)}) collective-permute-start(bf16[512,384]{1,0:T(8,128)(2,1)S(1)} %shard_map.80.qg_ref.refs_0_), channel_id=1, source_target_pairs={{0,2},{1,3},{2,0},{3,1},{4,6},{5,7},{6,4},{7,5},{8,10},{9,11},{10,... | collective-permute-start | bytes 1179656 | tf_op jit(solution)/shard_map/ppermute | solution.py:560
  18.9 0.6 %collective-permute-done.6.refs_1_.refs_5_ = bf16[640,384]{1,0:T(8,128)(2,1)S(1)} collective-permute-done((bf16[640,384]{1,0:T(8,128)(2,1)S(1)}, bf16[640,384]{1,0:T(8,128)(2,1)S(1)}, u32[]{:S(2)}, u32[]{:S(2)}) %collective-permute-start.6) | collective-permute-done | bytes 491552 | tf_op jit(solution)/shard_map/ppermute | solution.py:560
  19.5 2.6 %shard_map.81 = (f32[16,640]{1,0:T(8,128)S(1)}, bf16[96,384]{1,0:T(8,128)(2,1)S(1)}) custom-call(s32[6]{0:T(128)S(1)} %copy-done.4, bf16[256,384]{1,0:T(8,128)(2,1)S(1)} %copy-done, bf16[256,384]{1,0:T(8,128)(2,1)S(1)} %copy-done.1, f32[24,256]{1,0:T(8,128)S(1)} %shard_map.76.first_ref.known_ref, bf16[32,384]{1,0:T(8,128)(2,1)S(1)} %copy-done.5, ...), custom_call_target="tpu_custom_call" | custom-call | flops 2875000064 | tf_op jit(solution)/shard_map/pallas_call | solution.py:545
  22.1 2.2 %collective-permute-start.9 = (bf16[96,384]{1,0:T(8,128)(2,1)S(1)}, bf16[96,384]{1,0:T(8,128)(2,1)S(1)}, u32[]{:S(2)}, u32[]{:S(2)}) collective-permute-start(bf16[96,384]{1,0:T(8,128)(2,1)S(1)} %get-tuple-element.25), channel_id=1, source_target_pairs={{0,6},{1,7},{2,4},{3,5},{4,2},{5,3},{6,0},{7,1},{8,14},{9,15},{10,... | collective-permute-start | bytes 221192 | tf_op jit(solution)/shard_map/ppermute | solution.py:560
  24.3 0.5 %collective-permute-start.10 = (bf16[96,384]{1,0:T(8,128)(2,1)S(1)}, bf16[96,384]{1,0:T(8,128)(2,1)S(1)}, u32[]{:S(2)}, u32[]{:S(2)}) collective-permute-start(bf16[96,384]{1,0:T(8,128)(2,1)S(1)} %get-tuple-element.25), channel_id=1, source_target_pairs={{0,4},{1,5},{2,6},{3,7},{4,0},{5,1},{6,2},{7,3},{8,12},{9,13},{10,... | collective-permute-start | bytes 221192 | tf_op jit(solution)/shard_map/ppermute | solution.py:560
  24.7 1.8 %collective-permute-start.8 = (f32[16,640]{1,0:T(8,128)S(1)}, f32[16,640]{1,0:T(8,128)S(1)}, u32[]{:S(2)}, u32[]{:S(2)}) collective-permute-start(f32[16,640]{1,0:T(8,128)S(1)} %get-tuple-element.21.pay_ref.refs_1_.refs_0_), channel_id=1, source_target_pairs={{0,2},{1,3},{2,0},{3,1},{4,6},{5,7},{6,4},{7,5},{8,10},{9,11},{10,... | collective-permute-start | bytes 122888 | tf_op jit(solution)/shard_map/ppermute | solution.py:560
  26.5 4.6 %shard_map.82 = (f32[256,384]{1,0:T(8,128)S(1)}, f32[4,384]{1,0:T(4,128)S(1)}) custom-call(s32[6]{0:T(128)S(1)} %copy-done.4, bf16[512,384]{1,0:T(8,128)(2,1)S(1)} %shard_map.80.qg_ref.refs_0_, bf16[32,384]{1,0:T(8,128)(2,1)S(1)} %get-tuple-element.17.second_ref.qg_ref.spec_in, f32[16,640]{1,0:T(8,128)S(1)} %get-tuple-element.21.pay_ref.refs_1_.refs_0_, ...), custom_call_target="tpu_custom_call" | custom-call | flops 5750000128 | tf_op jit(solution)/shard_map/pallas_call | solution.py:545
  31.1 2.0 %shard_map.83 = (f32[256,384]{1,0:T(8,128)S(1)}, f32[256,384]{1,0:T(8,128)S(1)}) custom-call(s32[6]{0:T(128)S(1)} %copy-done.4, bf16[256,384]{1,0:T(8,128)(2,1)S(1)} %copy-done.2, bf16[256,384]{1,0:T(8,128)(2,1)S(1)} %copy-done.3, bf16[512,384]{1,0:T(8,128)(2,1)S(1)} %shard_map.80.qg_ref.refs_0_, f32[16,640]{1,0:T(8,128)S(1)} %get-tuple-element.21.pay_ref.refs_1_.refs_0_), custom_call_target="tpu_custom_call" | custom-call | flops 1495000064 | tf_op jit(solution)/shard_map/pallas_call | solution.py:545
  33.2 0.1 collective-permute-done.8.refs_1_
  33.3 0.1 collective-permute-start.12
  33.4 0.5 %collective-permute-start.11 = (f32[32,640]{1,0:T(8,128)S(1)}, f32[32,640]{1,0:T(8,128)S(1)}, u32[]{:S(2)}, u32[]{:S(2)}) collective-permute-start(f32[32,640]{1,0:T(8,128)S(1)} %get-tuple-element.26.refs_0_.refs_3_), channel_id=1, source_target_pairs={{0,1},{1,0},{2,3},{3,2},{4,5},{5,4},{6,7},{7,6},{8,9},{9,8},{10,11... | collective-permute-start | bytes 245768 | tf_op jit(solution)/shard_map/ppermute | solution.py:560
  33.9 0.1 collective-permute-start.7
  33.9 0.9 %collective-permute-done.11.refs_1_.refs_4_ = f32[32,640]{1,0:T(8,128)S(1)} collective-permute-done((f32[32,640]{1,0:T(8,128)S(1)}, f32[32,640]{1,0:T(8,128)S(1)}, u32[]{:S(2)}, u32[]{:S(2)}) %collective-permute-start.11) | collective-permute-done | bytes 81952 | tf_op jit(solution)/shard_map/ppermute | solution.py:560
  34.9 0.4 collective-permute-start.14
  35.3 2.4 %collective-permute-start.15 = (bf16[80,384]{1,0:T(8,128)(2,1)S(1)}, bf16[80,384]{1,0:T(8,128)(2,1)S(1)}, u32[]{:S(2)}, u32[]{:S(2)}) collective-permute-start(bf16[80,384]{1,0:T(8,128)(2,1)S(1)} %shard_map.85._.refs_0_), channel_id=1, source_target_pairs={{0,24},{8,16},{16,8},{24,0},{1,25},{9,17},{17,9},{25,1},{2,26},{10... | collective-permute-start | bytes 184328 | tf_op jit(solution)/shard_map/ppermute | solution.py:560
  37.8 0.5 %collective-permute-start.16 = (bf16[80,384]{1,0:T(8,128)(2,1)S(1)}, bf16[80,384]{1,0:T(8,128)(2,1)S(1)}, u32[]{:S(2)}, u32[]{:S(2)}) collective-permute-start(bf16[80,384]{1,0:T(8,128)(2,1)S(1)} %shard_map.85._.refs_0_), channel_id=1, source_target_pairs={{0,16},{8,24},{16,0},{24,8},{1,17},{9,25},{17,1},{25,9},{2,18},{10... | collective-permute-start | bytes 184328 | tf_op jit(solution)/shard_map/ppermute | solution.py:560
  38.3 0.5 %collective-permute-start.17 = (bf16[80,384]{1,0:T(8,128)(2,1)S(1)}, bf16[80,384]{1,0:T(8,128)(2,1)S(1)}, u32[]{:S(2)}, u32[]{:S(2)}) collective-permute-start(bf16[80,384]{1,0:T(8,128)(2,1)S(1)} %shard_map.85._.refs_0_), channel_id=1, source_target_pairs={{0,8},{8,0},{16,24},{24,16},{1,9},{9,1},{17,25},{25,17},{2,10},{10... | collective-permute-start | bytes 184328 | tf_op jit(solution)/shard_map/ppermute | solution.py:560
  38.8 3.9 %shard_map.87 = (f32[256,384]{1,0:T(8,128)S(1)}, f32[256,384]{1,0:T(8,128)S(1)}) custom-call(s32[6]{0:T(128)S(1)} %copy-done.4, bf16[256,384]{1,0:T(8,128)(2,1)S(1)} %copy-done.2, bf16[256,384]{1,0:T(8,128)(2,1)S(1)} %copy-done.3, bf16[512,384]{1,0:T(8,128)(2,1)S(1)} %collective-permute-done.7.refs_0_, bf16[512,384]{1,0:T(8,128)(2,1)S(1)} %shard_map.86.refs_1_, ...), custom_call_target="tpu_custom_call" | custom-call | flops 4600000000 | tf_op jit(solution)/shard_map/pallas_call | solution.py:545
  42.7 2.0 %shard_map.88 = (bf16[256,384]{1,0:T(8,128)(2,1)}, bf16[256,384]{1,0:T(8,128)(2,1)}, bf16[256,384]{1,0:T(8,128)(2,1)}) custom-call(s32[6]{0:T(128)S(1)} %copy-done.4, bf16[256,384]{1,0:T(8,128)(2,1)S(1)} %copy-done.2, bf16[256,384]{1,0:T(8,128)(2,1)S(1)} %copy-done.3, f32[256,384]{1,0:T(8,128)S(1)} %get-tuple-element.22.dq_in, ...), custom_call_target="tpu_custom_call" | custom-call | flops 3449999872 | tf_op jit(solution)/shard_map/pallas_call | solution.py:545
  (31 shorter events, 0.2 us)
Async XLA Ops:
  0.6 9.4 %copy-start = (bf16[256,384]{1,0:T(8,128)(2,1)S(1)}, bf16[256,384]{1,0:T(8,128)(2,1)}, u32[]{:S(2)}) copy-start(bf16[256,384]{1,0:T(8,128)(2,1)} %q_ref.5) | copy-start | bytes 589828
  0.6 9.4 %copy-start.1 = (bf16[256,384]{1,0:T(8,128)(2,1)S(1)}, bf16[256,384]{1,0:T(8,128)(2,1)}, u32[]{:S(2)}) copy-start(bf16[256,384]{1,0:T(8,128)(2,1)} %g_ref.5) | copy-start | bytes 589828
  0.6 10.2 %collective-permute-start = (bf16[256,384]{1,0:T(8,128)(2,1)}, bf16[256,384]{1,0:T(8,128)(2,1)S(1)}, u32[]{:S(2)}, u32[]{:S(2)}) collective-permute-start(bf16[256,384]{1,0:T(8,128)(2,1)} %k_ref.7), channel_id=1, source_target_pairs={{0,1},{1,0},{2,3},{3,2},{4,5},{5,4},{6,7},{7,6},{8,9},{9,8},{10,11... | collective-permute-start | bytes 589832 | tf_op jit(solution)/shard_map/ppermute | solution.py:560
  1.2 16.3 %collective-permute-start.2 = (bf16[256,384]{1,0:T(8,128)(2,1)}, bf16[256,384]{1,0:T(8,128)(2,1)S(1)}, u32[]{:S(2)}, u32[]{:S(2)}) collective-permute-start(bf16[256,384]{1,0:T(8,128)(2,1)} %k_ref.7), channel_id=1, source_target_pairs={{0,2},{1,3},{2,0},{3,1},{4,6},{5,7},{6,4},{7,5},{8,10},{9,11},{10,... | collective-permute-start | bytes 589832 | tf_op jit(solution)/shard_map/ppermute | solution.py:560
  3.8 7.1 %collective-permute-start.1 = (bf16[256,384]{1,0:T(8,128)(2,1)}, bf16[256,384]{1,0:T(8,128)(2,1)S(1)}, u32[]{:S(2)}, u32[]{:S(2)}) collective-permute-start(bf16[256,384]{1,0:T(8,128)(2,1)} %v_ref.7), channel_id=1, source_target_pairs={{0,1},{1,0},{2,3},{3,2},{4,5},{5,4},{6,7},{7,6},{8,9},{9,8},{10,11... | collective-permute-start | bytes 589832 | tf_op jit(solution)/shard_map/ppermute | solution.py:560
  4.0 13.5 %collective-permute-start.3 = (bf16[256,384]{1,0:T(8,128)(2,1)}, bf16[256,384]{1,0:T(8,128)(2,1)S(1)}, u32[]{:S(2)}, u32[]{:S(2)}) collective-permute-start(bf16[256,384]{1,0:T(8,128)(2,1)} %v_ref.7), channel_id=1, source_target_pairs={{0,2},{1,3},{2,0},{3,1},{4,6},{5,7},{6,4},{7,5},{8,10},{9,11},{10,... | collective-permute-start | bytes 589832 | tf_op jit(solution)/shard_map/ppermute | solution.py:560
  6.2 3.9 %copy-start.4 = (s32[6]{0:T(128)S(1)}, s32[6]{0:T(128)}, u32[]{:S(2)}) copy-start(s32[6]{0:T(128)} %off_ref.13) | copy-start | bytes 76
  6.2 4.7 %copy-start.6 = (bf16[64,384]{1,0:T(8,128)(2,1)S(1)}, bf16[64,384]{1,0:T(8,128)(2,1)}, u32[]{:S(2)}) copy-start(bf16[64,384]{1,0:T(8,128)(2,1)} %get-tuple-element.18) | copy-start | bytes 147460
  6.2 4.7 %copy-start.2 = (bf16[256,384]{1,0:T(8,128)(2,1)S(1)}, bf16[256,384]{1,0:T(8,128)(2,1)}, u32[]{:S(2)}) copy-start(bf16[256,384]{1,0:T(8,128)(2,1)} %k_ref.7) | copy-start | bytes 589828
  6.2 4.7 %copy-start.3 = (bf16[256,384]{1,0:T(8,128)(2,1)S(1)}, bf16[256,384]{1,0:T(8,128)(2,1)}, u32[]{:S(2)}) copy-start(bf16[256,384]{1,0:T(8,128)(2,1)} %v_ref.7) | copy-start | bytes 589828
  6.2 11.2 %collective-permute-start.4 = (bf16[64,384]{1,0:T(8,128)(2,1)}, bf16[64,384]{1,0:T(8,128)(2,1)S(1)}, u32[]{:S(2)}, u32[]{:S(2)}) collective-permute-start(bf16[64,384]{1,0:T(8,128)(2,1)} %get-tuple-element.18), channel_id=1, source_target_pairs={{0,6},{1,7},{2,4},{3,5},{4,2},{5,3},{6,0},{7,1},{8,14},{9,15},{10,... | collective-permute-start | bytes 147464 | tf_op jit(solution)/shard_map/ppermute | solution.py:560
  10.8 6.6 %collective-permute-start.5 = (bf16[64,384]{1,0:T(8,128)(2,1)S(1)}, bf16[64,384]{1,0:T(8,128)(2,1)S(1)}, u32[]{:S(2)}, u32[]{:S(2)}) collective-permute-start(bf16[64,384]{1,0:T(8,128)(2,1)S(1)} %copy-done.6), channel_id=1, source_target_pairs={{0,4},{1,5},{2,6},{3,7},{4,0},{5,1},{6,2},{7,3},{8,12},{9,13},{10,... | collective-permute-start | bytes 147464 | tf_op jit(solution)/shard_map/ppermute | solution.py:560
  17.5 1.9 %copy-start.5 = (bf16[32,384]{1,0:T(8,128)(2,1)S(1)}, bf16[32,384]{1,0:T(8,128)(2,1)}, u32[]{:S(2)}) copy-start(bf16[32,384]{1,0:T(8,128)(2,1)} %get-tuple-element.19.kv_ref) | copy-start | bytes 73732
  17.5 1.9 %collective-permute-start.6 = (bf16[640,384]{1,0:T(8,128)(2,1)S(1)}, bf16[640,384]{1,0:T(8,128)(2,1)S(1)}, u32[]{:S(2)}, u32[]{:S(2)}) collective-permute-start(bf16[640,384]{1,0:T(8,128)(2,1)S(1)} %shard_map.79._.refs_0_.refs_4_), channel_id=1, source_target_pairs={{0,1},{1,0},{2,3},{3,2},{4,5},{5,4},{6,7},{7,6},{8,9},{9,8},{10,11... | collective-permute-start | bytes 1474568 | tf_op jit(solution)/shard_map/ppermute | solution.py:560
  17.6 17.2 %collective-permute-start.13 = (bf16[512,384]{1,0:T(8,128)(2,1)S(1)}, bf16[512,384]{1,0:T(8,128)(2,1)S(1)}, u32[]{:S(2)}, u32[]{:S(2)}) collective-permute-start(bf16[512,384]{1,0:T(8,128)(2,1)S(1)} %shard_map.80.qg_ref.refs_0_), channel_id=1, source_target_pairs={{0,2},{1,3},{2,0},{3,1},{4,6},{5,7},{6,4},{7,5},{8,10},{9,11},{10,... | collective-permute-start | bytes 1179656 | tf_op jit(solution)/shard_map/ppermute | solution.py:560
  22.1 11.2 %collective-permute-start.9 = (bf16[96,384]{1,0:T(8,128)(2,1)S(1)}, bf16[96,384]{1,0:T(8,128)(2,1)S(1)}, u32[]{:S(2)}, u32[]{:S(2)}) collective-permute-start(bf16[96,384]{1,0:T(8,128)(2,1)S(1)} %get-tuple-element.25), channel_id=1, source_target_pairs={{0,6},{1,7},{2,4},{3,5},{4,2},{5,3},{6,0},{7,1},{8,14},{9,15},{10,... | collective-permute-start | bytes 221192 | tf_op jit(solution)/shard_map/ppermute | solution.py:560
  24.3 9.0 %collective-permute-start.10 = (bf16[96,384]{1,0:T(8,128)(2,1)S(1)}, bf16[96,384]{1,0:T(8,128)(2,1)S(1)}, u32[]{:S(2)}, u32[]{:S(2)}) collective-permute-start(bf16[96,384]{1,0:T(8,128)(2,1)S(1)} %get-tuple-element.25), channel_id=1, source_target_pairs={{0,4},{1,5},{2,6},{3,7},{4,0},{5,1},{6,2},{7,3},{8,12},{9,13},{10,... | collective-permute-start | bytes 221192 | tf_op jit(solution)/shard_map/ppermute | solution.py:560
  24.7 8.5 %collective-permute-start.8 = (f32[16,640]{1,0:T(8,128)S(1)}, f32[16,640]{1,0:T(8,128)S(1)}, u32[]{:S(2)}, u32[]{:S(2)}) collective-permute-start(f32[16,640]{1,0:T(8,128)S(1)} %get-tuple-element.21.pay_ref.refs_1_.refs_0_), channel_id=1, source_target_pairs={{0,2},{1,3},{2,0},{3,1},{4,6},{5,7},{6,4},{7,5},{8,10},{9,11},{10,... | collective-permute-start | bytes 122888 | tf_op jit(solution)/shard_map/ppermute | solution.py:560
  33.3 1.6 %collective-permute-start.12 = (bf16[192,384]{1,0:T(8,128)(2,1)S(1)}, bf16[192,384]{1,0:T(8,128)(2,1)S(1)}, u32[]{:S(2)}, u32[]{:S(2)}) collective-permute-start(bf16[192,384]{1,0:T(8,128)(2,1)S(1)} %get-tuple-element.27.refs_2_.refs_5_), channel_id=1, source_target_pairs={{0,1},{1,0},{2,3},{3,2},{4,5},{5,4},{6,7},{7,6},{8,9},{9,8},{10,11... | collective-permute-start | bytes 442376 | tf_op jit(solution)/shard_map/ppermute | solution.py:560
  33.4 1.5 %collective-permute-start.11 = (f32[32,640]{1,0:T(8,128)S(1)}, f32[32,640]{1,0:T(8,128)S(1)}, u32[]{:S(2)}, u32[]{:S(2)}) collective-permute-start(f32[32,640]{1,0:T(8,128)S(1)} %get-tuple-element.26.refs_0_.refs_3_), channel_id=1, source_target_pairs={{0,1},{1,0},{2,3},{3,2},{4,5},{5,4},{6,7},{7,6},{8,9},{9,8},{10,11... | collective-permute-start | bytes 245768 | tf_op jit(solution)/shard_map/ppermute | solution.py:560
  33.9 4.9 %collective-permute-start.7 = (bf16[512,384]{1,0:T(8,128)(2,1)S(1)}, bf16[512,384]{1,0:T(8,128)(2,1)S(1)}, u32[]{:S(2)}, u32[]{:S(2)}) collective-permute-start(bf16[512,384]{1,0:T(8,128)(2,1)S(1)} %shard_map.80.qg_ref.refs_0_), channel_id=1, source_target_pairs={{0,1},{1,0},{2,3},{3,2},{4,5},{5,4},{6,7},{7,6},{8,9},{9,8},{10,11... | collective-permute-start | bytes 1179656 | tf_op jit(solution)/shard_map/ppermute | solution.py:560
  34.9 3.9 %collective-permute-start.14 = (bf16[512,384]{1,0:T(8,128)(2,1)S(1)}, bf16[512,384]{1,0:T(8,128)(2,1)S(1)}, u32[]{:S(2)}, u32[]{:S(2)}) collective-permute-start(bf16[512,384]{1,0:T(8,128)(2,1)S(1)} %shard_map.86.refs_1_), channel_id=1, source_target_pairs={{0,1},{1,0},{2,3},{3,2},{4,5},{5,4},{6,7},{7,6},{8,9},{9,8},{10,11... | collective-permute-start | bytes 1179656 | tf_op jit(solution)/shard_map/ppermute | solution.py:560
  35.3 7.4 %collective-permute-start.15 = (bf16[80,384]{1,0:T(8,128)(2,1)S(1)}, bf16[80,384]{1,0:T(8,128)(2,1)S(1)}, u32[]{:S(2)}, u32[]{:S(2)}) collective-permute-start(bf16[80,384]{1,0:T(8,128)(2,1)S(1)} %shard_map.85._.refs_0_), channel_id=1, source_target_pairs={{0,24},{8,16},{16,8},{24,0},{1,25},{9,17},{17,9},{25,1},{2,26},{10... | collective-permute-start | bytes 184328 | tf_op jit(solution)/shard_map/ppermute | solution.py:560
  37.8 4.9 %collective-permute-start.16 = (bf16[80,384]{1,0:T(8,128)(2,1)S(1)}, bf16[80,384]{1,0:T(8,128)(2,1)S(1)}, u32[]{:S(2)}, u32[]{:S(2)}) collective-permute-start(bf16[80,384]{1,0:T(8,128)(2,1)S(1)} %shard_map.85._.refs_0_), channel_id=1, source_target_pairs={{0,16},{8,24},{16,0},{24,8},{1,17},{9,25},{17,1},{25,9},{2,18},{10... | collective-permute-start | bytes 184328 | tf_op jit(solution)/shard_map/ppermute | solution.py:560
  38.3 4.4 %collective-permute-start.17 = (bf16[80,384]{1,0:T(8,128)(2,1)S(1)}, bf16[80,384]{1,0:T(8,128)(2,1)S(1)}, u32[]{:S(2)}, u32[]{:S(2)}) collective-permute-start(bf16[80,384]{1,0:T(8,128)(2,1)S(1)} %shard_map.85._.refs_0_), channel_id=1, source_target_pairs={{0,8},{8,0},{16,24},{24,16},{1,9},{9,1},{17,25},{25,17},{2,10},{10... | collective-permute-start | bytes 184328 | tf_op jit(solution)/shard_map/ppermute | solution.py:560
